TPU v7x, 32 devices: a whole 2x2x4 slice. The times are simulated.
32 devices in a mesh: section: 2 (over core), tensor: 4 (over y, x), dp: 4 (over z).
Axes of the slice: x: 2, y: 2, z: 4, core: 2. Of those that a mesh axis runs over, the one named last changes fastest.
Arguments:
- inputs: bfloat16 [8, 1024, 768], P('dp', 'tensor')
- norm_gains: float32 [2, 2, 768], P('section'), may hold values from 0.5 to 1.5
- attention_in: bfloat16 [2, 3, 768, 768], P('section', None, None, 'tensor'), may hold values from -0.21875 to 0.21875
- attention_out: bfloat16 [2, 768, 768], P('section', 'tensor'), may hold values from -1.25 to 1.25
- bias_table: float32 [2, 32, 12], P('section', None, 'tensor'), may hold values from -4 to 4
- router_weight: bfloat16 [2, 768, 4], P('section'), may hold values from -0.15625 to 0.15625
- up_weight: bfloat16 [2, 4, 768, 3072], P('section', None, None, 'tensor'), may hold values from -0.21875 to 0.21875
- down_weight: bfloat16 [2, 4, 3072, 768], P('section', None, 'tensor'), may hold values from -0.3125 to 0.3125
- routes: int32 [2, 8, 1024, 1], P('section', 'dp'), may hold values from 0 to 3; in each aligned block of 1024 rows (0 to 1023, 1024 to 2047, ..., all dimensions but the last counted through in order) at most 320 rows name the same one
- piece_starts: int32 [8, 2], P('dp'), may hold values from 0 to 768, as said below
- valid_mask: int32 [8, 1024], P('dp'), may hold values from 0 to 1, as said below
- cotangent: bfloat16 [8, 1024, 768], P('dp', 'tensor'), may hold values from -6 to 6
Outputs:
- layer_output: bfloat16 [2, 8, 1024, 768], P('section', 'dp', 'tensor')
- input_grad: float32 [2, 8, 1024, 768], P('section', 'dp', 'tensor')
- gain_grad: float32 [2, 2, 768], P('section')
- attention_in_grad: float32 [2, 3, 768, 768], P('section', None, 'dp', 'tensor')
- attention_out_grad: float32 [2, 768, 768], P('section', ('tensor', 'dp'))
- bias_grad: float32 [2, 32, 12], P('section', 'dp', 'tensor')
- router_grad: float32 [2, 768, 4], P('section')
- up_grad: float32 [2, 4, 768, 3072], P('section', None, 'dp', 'tensor')
- down_grad: float32 [2, 4, 3072, 768], P('section', None, ('tensor', 'dp'))
- root_means: float32 [2, 3], P('section')
Inputs may be any that keep to these rules, and one draw needn't show every extreme that they name: `routes`: in each sequence of each layer, no expert is named by more than 320 tokens. `piece_starts`: the 2 starts of a sequence rise; each piece of 256 tokens lies inside the sequence and pieces do not intersect. `valid_mask`: the valid tokens of a sequence form a prefix that holds its first token.
All inputs are finite; a program needn't handle non-finite values.
Results may differ from a plain program's by a relative error of at most 0.03.
Values may be sent and summed in bfloat16 or wider, within the bound.
No kernel may reach another device: no remote copies, remote signals or barrier semaphores. Data moves between devices by JAX's collectives and lax.ppermute only.
A program may use at most 320 MiB of HBM per device.

v0:
```python
import functools

import jax
import jax.numpy as jnp
import numpy as np
from jax import lax
from jax.experimental import pallas as pl
from jax.experimental.pallas import tpu as pltpu
from jax.sharding import PartitionSpec as P

D = 768
HEAD_DIM = 64
BUCKETS = 32
EXPERTS = 4
CAP = 320
SEQ = 1024
PIECE = 256
PIECES = 2
SLOTS = EXPERTS * CAP

QB = PIECE
BAND = 128
WIDE = 2 * QB + BAND
DIAGS = 6

epsilon = 1e-06
bucket_edges = (12, 16, 23, 32, 46, 64, 91)
masked_score = -1000000000.0
far_bucket_behind = 15

BF = jnp.bfloat16
F32 = jnp.float32
VMEM_LIMIT = 56 * 1024 * 1024


def dot(a, b, ca=1, cb=0):
    return lax.dot_general(a, b, (((ca,), (cb,)), ((), ())), preferred_element_type=F32)


def vm(count):
    return [pl.BlockSpec(memory_space=pltpu.VMEM)] * count


def smem():
    return pl.BlockSpec(memory_space=pltpu.SMEM)


def cost(flops, size):
    return pl.CostEstimate(flops=int(flops), bytes_accessed=int(size), transcendentals=0)


def shape(dims, kind):
    return jax.ShapeDtypeStruct(dims, kind)


def exchange(value, axis, mask):
    count = lax.axis_size(axis)
    return lax.ppermute(value, axis, [(i, i ^ mask) for i in range(count)])


def gather_parts(value):
    return [value] + [exchange(value, "tensor", k) for k in range(1, lax.axis_size("tensor"))]


def swap_parts(parts):
    return [parts[0]] + [exchange(p, "tensor", k) for k, p in enumerate(parts) if k]


def natural(t, k, size):
    return pl.ds(pl.multiple_of(jnp.bitwise_xor(t, k) * size, size), size)


def offset_buckets(offsets):
    distance = np.abs(offsets)
    far = np.full(offsets.shape, 8, np.int32)
    for edge_value in bucket_edges:
        far = far + (distance >= edge_value)
    return np.where(distance < 8, distance, far) + np.where(offsets > 0, 16, 0)


def diagonal_one_hot():
    lane = np.arange(2 * BAND)
    y = np.where(lane < BAND, lane, lane - 2 * BAND)
    offsets = BAND * (np.arange(DIAGS)[:, None] - 2) - y[None, :]
    hot = offset_buckets(offsets)[:, :, None] == np.arange(BUCKETS)
    hot = hot & (lane != BAND)[None, :, None]
    return hot.astype(np.float32)


def bias_body(rows_ref, out_ref):
    heads = out_ref.shape[1]
    for layer in range(out_ref.shape[0]):
        for h in range(heads):
            for d in range(DIAGS):
                row = rows_ref[layer, pl.ds(h * DIAGS + d, 1), :]
                tile = pltpu.roll(
                    jnp.broadcast_to(row, (BAND, 2 * BAND)), 0, 1, stride=1, stride_axis=0
                )[:, :BAND]
                for i in range(WIDE // BAND):
                    for j in range(QB // BAND):
                        if i - j == d - 1:
                            out_ref[
                                layer, h, i * BAND : (i + 1) * BAND, j * BAND : (j + 1) * BAND
                            ] = tile


def bias_tiles(rows):
    heads = rows.shape[1] // DIAGS
    return pl.pallas_call(
        bias_body,
        out_shape=shape((rows.shape[0], heads, WIDE, QB), F32),
        in_specs=vm(1),
        out_specs=vm(1)[0],
        compiler_params=pltpu.CompilerParams(vmem_limit_bytes=VMEM_LIMIT),
        cost_estimate=cost(1e6, 4e6),
        name="bias_tiles",
    )(rows)


def block_range(j):
    last = min(SEQ, QB * (j + 2))
    left = max(0, QB * j - BAND)
    return left, last, left - (QB * j - BAND)


def fill_mask(mask_ref, valid_ref, s0, s1, j):
    left, last, _ = block_range(j)
    width = last - left
    key = left + lax.broadcasted_iota(jnp.int32, (width, 1), 0)
    query = QB * j + lax.broadcasted_iota(jnp.int32, (1, QB), 1)

    def label(position, outside):
        second = jnp.where((position >= s1) & (position < s1 + PIECE), 1, outside)
        return jnp.where((position >= s0) & (position < s0 + PIECE), 0, second)

    allowed = (key <= query) | (label(key, -1) == label(query, -2))
    mask_ref[:width, :] = jnp.where(allowed, valid_ref[left:last, :], masked_score)


def fwd_attention_body(parts, norm_inside, *refs):
    info, valid_col, gain, w_ref, bias_ref = refs[:5]
    x_refs = refs[5 : 5 + parts]
    xn_ref, qkv_ref, turned_ref, lse_ref = refs[5 + parts : 9 + parts]
    out_refs = refs[9 + parts : 9 + 2 * parts]
    vt_ref, att_ref, mask_ref, valid_ref = refs[9 + 2 * parts :]
    t, s0, s1 = info[0], info[1], info[2]
    rows = SEQ // parts
    heads = qkv_ref.shape[1]

    valid_ref[...] = jnp.broadcast_to(valid_col[...], (SEQ, QB))
    for k in range(parts):
        where = natural(t, k, rows)
        x = x_refs[k][...]
        if norm_inside:
            xf = x.astype(F32)
            scale = lax.rsqrt(jnp.mean(xf * xf, axis=-1, keepdims=True) + epsilon)
            x = (xf * scale * gain[...]).astype(BF)
        xn_ref[where, :] = x
        for i in range(3):
            product = dot(x, w_ref[i])
            if i == 0:
                product = product * HEAD_DIM**-0.5
            turned = product.T.astype(BF)
            if i < 2:
                turned_ref[i, :, where] = turned
            else:
                vt_ref[:, where] = turned
            product = product.astype(BF)
            for h in range(heads):
                qkv_ref[i, h, where, :] = product[:, h * HEAD_DIM : (h + 1) * HEAD_DIM]

    for j in range(SEQ // QB):
        left, last, skip = block_range(j)
        width = last - left
        columns = slice(j * QB, (j + 1) * QB)
        fill_mask(mask_ref, valid_ref, s0, s1, j)

        def one_head(h, carry):
            lanes = pl.ds(pl.multiple_of(h * HEAD_DIM, HEAD_DIM), HEAD_DIM)
            scores = dot(qkv_ref[1, h, :last, :], turned_ref[0, lanes, columns])
            near = scores[left:] + bias_ref[h, skip : skip + width, :] + mask_ref[:width, :]
            highest = jnp.max(near, axis=0, keepdims=True)
            if left:
                far = scores[:left] + valid_ref[:left, :]
                highest = jnp.maximum(highest, jnp.max(far, axis=0, keepdims=True))
            near = jnp.exp(near - highest)
            total = jnp.sum(near, axis=0, keepdims=True)
            out = dot(vt_ref[lanes, left:last], near.astype(BF))
            if left:
                far = jnp.exp(far - highest)
                total = total + jnp.sum(far, axis=0, keepdims=True)
                out = out + dot(vt_ref[lanes, :left], far.astype(BF))
            lse_ref[h, :, columns] = highest + jnp.log(total)
            att_ref[lanes, columns] = (out * (1.0 / total)).astype(BF)
            return carry

        lax.fori_loop(0, heads, one_head, 0)

    for k in range(parts):
        out_refs[k][...] = att_ref[:, natural(t, k, rows)]


def fwd_attention(info, valid_col, gain, w, bias, x_parts, norm_inside):
    parts = len(x_parts)
    rows = SEQ // parts
    wide = w.shape[2]
    heads = wide // HEAD_DIM
    outs = pl.pallas_call(
        functools.partial(fwd_attention_body, parts, norm_inside),
        out_shape=[
            shape((SEQ, D), BF),
            shape((3, heads, SEQ, HEAD_DIM), BF),
            shape((2, wide, SEQ), BF),
            shape((heads, 1, SEQ), F32),
        ]
        + [shape((wide, rows), BF)] * parts,
        in_specs=[smem()] + vm(4 + parts),
        out_specs=vm(4 + parts),
        scratch_shapes=[
            pltpu.VMEM((wide, SEQ), BF),
            pltpu.VMEM((wide, SEQ), BF),
            pltpu.VMEM((WIDE, QB), F32),
            pltpu.VMEM((SEQ, QB), F32),
        ],
        compiler_params=pltpu.CompilerParams(vmem_limit_bytes=VMEM_LIMIT),
        cost_estimate=cost(9e9, 1e7),
        name="fwd_attention",
    )(info, valid_col, gain, w, bias, *x_parts)
    return outs[:4], list(outs[4:])


def bwd_attention_body(parts, *refs):
    info, valid_col, w_ref, bias_ref, qkv_ref, turned_ref, lse_ref = refs[:7]
    d_refs = refs[7 : 7 + parts]
    proj_ref, diag_ref, far_ref = refs[7 + parts : 10 + parts]
    out_refs = refs[10 + parts : 10 + 2 * parts]
    (
        d_ref,
        dt_ref,
        dq_ref,
        dk_ref,
        dv_ref,
        sum_ref,
        mask_ref,
        valid_ref,
    ) = refs[10 + 2 * parts :]
    t, s0, s1 = info[0], info[1], info[2]
    rows = SEQ // parts
    heads = qkv_ref.shape[1]

    valid_ref[...] = jnp.broadcast_to(valid_col[...], (SEQ, QB))
    for k in range(parts):
        where = natural(t, k, rows)
        block = d_refs[k][...]
        dt_ref[:, where] = block.astype(F32).T.astype(BF)
        for h in range(heads):
            d_ref[h, where, :] = block[:, h * HEAD_DIM : (h + 1) * HEAD_DIM]
    dk_ref[...] = jnp.zeros_like(dk_ref)
    dv_ref[...] = jnp.zeros_like(dv_ref)
    sum_ref[...] = jnp.zeros_like(sum_ref)
    far_ref[...] = jnp.zeros_like(far_ref)

    for j in range(SEQ // QB):
        left, last, skip = block_range(j)
        width = last - left
        columns = slice(j * QB, (j + 1) * QB)
        fill_mask(mask_ref, valid_ref, s0, s1, j)

        def one_head(h, carry):
            lanes = pl.ds(pl.multiple_of(h * HEAD_DIM, HEAD_DIM), HEAD_DIM)
            q_block = qkv_ref[0, h, columns, :]
            d_block = d_ref[h, columns, :]
            lse = lse_ref[h, :, columns]
            scores = dot(qkv_ref[1, h, :last, :], turned_ref[0, lanes, columns])
            slopes = dot(qkv_ref[2, h, :last, :], dt_ref[lanes, columns])
            near = scores[left:] + bias_ref[h, skip : skip + width, :] + mask_ref[:width, :]
            near = jnp.exp(near - lse)
            near_slope = near * slopes[left:]
            row_dot = jnp.sum(near_slope, axis=0, keepdims=True)
            if left:
                far = jnp.exp(scores[:left] + valid_ref[:left, :] - lse)
                far_slope = far * slopes[:left]
                row_dot = row_dot + jnp.sum(far_slope, axis=0, keepdims=True)
            near_slope = near_slope - near * row_dot
            sum_ref[h, skip : skip + width, :] += near_slope
            near_slope = near_slope.astype(BF)
            dk_ref[h, left:last, :] += dot(near_slope, q_block)
            dv_ref[h, left:last, :] += dot(near.astype(BF), d_block)
            dq = dot(turned_ref[1, lanes, left:last], near_slope)
            if left:
                far_slope = far_slope - far * row_dot
                far_ref[h] += jnp.sum(far_slope.reshape(left // 8, 8, QB), axis=0)
                far_slope = far_slope.astype(BF)
                dk_ref[h, :left, :] += dot(far_slope, q_block)
                dv_ref[h, :left, :] += dot(far.astype(BF), d_block)
                dq = dq + dot(turned_ref[1, lanes, :left], far_slope)
            dq_ref[lanes, columns] = dq * HEAD_DIM**-0.5
            return carry

        lax.fori_loop(0, heads, one_head, 0)

    for first in range(0, SEQ, rows):
        where = slice(first, first + rows)
        proj_ref[0, where, :] = dq_ref[:, where].T.astype(BF)
        for i, source in ((1, dk_ref), (2, dv_ref)):
            proj_ref[i, where, :] = jnp.concatenate(
                [source[h, where, :].astype(BF) for h in range(heads)], axis=1
            )
    for k in range(parts):
        where = natural(t, k, rows)
        total = dot(proj_ref[0, where, :], w_ref[0], 1, 1)
        for i in (1, 2):
            total = total + dot(proj_ref[i, where, :], w_ref[i], 1, 1)
        out_refs[k][...] = total.astype(BF)

    for h in range(heads):
        for d in range(DIAGS):
            tile = None
            for i in range(WIDE // BAND):
                for j in range(QB // BAND):
                    if i - j == d - 1:
                        more = sum_ref[
                            h, i * BAND : (i + 1) * BAND, j * BAND : (j + 1) * BAND
                        ]
                        tile = more if tile is None else tile + more
            diag_ref[h * DIAGS + d] = tile


def diagonal_body(tiles_ref, out_ref):
    row = lax.broadcasted_iota(jnp.int32, (BAND, BAND), 0)
    column = lax.broadcasted_iota(jnp.int32, (BAND, BAND), 1)
    flip = (row + column == BAND - 1).astype(F32)
    for i in range(tiles_ref.shape[0]):
        tile = lax.dot_general(
            flip,
            tiles_ref[i],
            (((1,), (0,)), ((), ())),
            precision=lax.Precision.HIGHEST,
            preferred_element_type=F32,
        )
        tile = jnp.concatenate([tile, jnp.zeros_like(tile)], axis=1)
        tile = pltpu.roll(tile, BAND + 1, 1, stride=1, stride_axis=0)
        out_ref[i : i + 1, :] = jnp.sum(tile, axis=0, keepdims=True)


def diagonal_sums(tiles):
    return pl.pallas_call(
        diagonal_body,
        out_shape=shape((tiles.shape[0], 2 * BAND), F32),
        in_specs=vm(1),
        out_specs=vm(1)[0],
        compiler_params=pltpu.CompilerParams(vmem_limit_bytes=VMEM_LIMIT),
        cost_estimate=cost(1e8, 1e6),
        name="diagonal_sums",
    )(tiles)


def bwd_attention(info, valid_col, w, bias, saved, d_parts):
    parts = len(d_parts)
    rows = SEQ // parts
    wide = w.shape[2]
    heads = wide // HEAD_DIM
    qkv, turned, lse = saved
    outs = pl.pallas_call(
        functools.partial(bwd_attention_body, parts),
        out_shape=[
            shape((3, SEQ, wide), BF),
            shape((heads * DIAGS, BAND, BAND), F32),
            shape((heads, 8, QB), F32),
        ]
        + [shape((rows, D), BF)] * parts,
        in_specs=[smem()] + vm(6 + parts),
        out_specs=vm(3 + parts),
        scratch_shapes=[
            pltpu.VMEM((heads, SEQ, HEAD_DIM), BF),
            pltpu.VMEM((wide, SEQ), BF),
            pltpu.VMEM((wide, SEQ), F32),
            pltpu.VMEM((heads, SEQ, HEAD_DIM), F32),
            pltpu.VMEM((heads, SEQ, HEAD_DIM), F32),
            pltpu.VMEM((heads, WIDE, QB), F32),
            pltpu.VMEM((WIDE, QB), F32),
            pltpu.VMEM((SEQ, QB), F32),
        ],
        compiler_params=pltpu.CompilerParams(vmem_limit_bytes=VMEM_LIMIT),
        cost_estimate=cost(1.8e10, 1e7),
        name="bwd_attention",
    )(info, valid_col, w, bias, qkv, turned, lse, *d_parts)
    return outs[:3], list(outs[3:])


def choose(select, own_ref, other_ref, to_ref):
    @pl.when(select == 0)
    def _():
        to_ref[...] = own_ref[0]

    @pl.when(select != 0)
    def _():
        to_ref[...] = other_ref[0]


def combine(parts, rows, target_col, slots_ref, out_refs):
    slot = lax.broadcasted_iota(jnp.int32, (rows, SLOTS), 1)
    for k in list(range(1, parts)) + [0]:
        hot = (target_col[k * rows : (k + 1) * rows, :] == slot).astype(BF)
        out_refs[k][...] = dot(hot, slots_ref[...]).astype(BF)


def dispatch(e, target_row, tokens_ref):
    slot = e * CAP + lax.broadcasted_iota(jnp.int32, (CAP, SEQ), 0)
    return dot((target_row[...] == slot).astype(BF), tokens_ref[...]).astype(BF)


def fwd_experts_body(parts, *refs):
    sel, target_row, target_col, router, up_own, up_other, down_own, down_other = refs[:8]
    x_refs = refs[8 : 8 + parts]
    in_ref, act_ref, slope_ref, gate_ref, probs_ref = refs[8 + parts : 13 + parts]
    out_refs = refs[13 + parts : 13 + 2 * parts]
    x_ref, slots_ref, up_ref, down_ref = refs[13 + 2 * parts :]
    rows = SEQ // parts
    e = pl.program_id(0)

    @pl.when(e == 0)
    def _():
        lane = lax.broadcasted_iota(jnp.int32, (rows, 128), 1)
        for k in range(parts):
            where = slice(k * rows, (k + 1) * rows)
            x = x_refs[k][...]
            x_ref[where, :] = x
            logits = jnp.where(lane < EXPERTS, dot(x, router[...], 1, 1), -1e30)
            probs = jnp.exp(logits - jnp.max(logits, axis=-1, keepdims=True))
            probs = probs / jnp.sum(probs, axis=-1, keepdims=True)
            target = target_col[where, :]
            hit = (target >= lane * CAP) & (target < lane * CAP + CAP)
            gate_ref[where, :] = jnp.sum(jnp.where(hit, probs, 0.0), axis=-1, keepdims=True)
            if k == 0:
                probs_ref[...] = probs

    choose(sel[0], up_own, up_other, up_ref)
    choose(sel[0], down_own, down_other, down_ref)
    expert_in = dispatch(e, target_row, x_ref)
    in_ref[0] = expert_in
    up = dot(expert_in, up_ref[...])
    inner = np.sqrt(2 / np.pi).astype(np.float32)
    square = up * up
    bend = jnp.tanh(inner * (up * (1.0 + 0.044715 * square)))
    half = 0.5 * (1.0 + bend)
    act = (up * half).astype(BF)
    act_ref[0] = act
    slope_ref[0] = half + 0.5 * up * (1.0 - bend * bend) * (
        inner * (1.0 + 3 * 0.044715 * square)
    )
    slots_ref[pl.ds(pl.multiple_of(e * CAP, CAP), CAP), :] = dot(act, down_ref[...]).astype(BF)

    @pl.when(e == EXPERTS - 1)
    def _():
        combine(parts, rows, target_col, slots_ref, out_refs)


def expert_specs(block):
    own = pl.BlockSpec(block, lambda e, sel: (e * (1 - sel[0]), 0, 0))
    other = pl.BlockSpec(block, lambda e, sel: (e * sel[0], 0, 0))
    return [own, other]


def whole(dims):
    return pl.BlockSpec(dims, lambda e, sel: (0,) * len(dims))


def fwd_experts(select, target_row, target_col, router, up_pair, down_pair, x_parts):
    parts = len(x_parts)
    rows = SEQ // parts
    hidden = up_pair[0].shape[2]
    each = pl.BlockSpec((1, CAP, D), lambda e, sel: (e, 0, 0))
    each_hidden = pl.BlockSpec((1, CAP, hidden), lambda e, sel: (e, 0, 0))
    outs = pl.pallas_call(
        functools.partial(fwd_experts_body, parts),
        grid_spec=pltpu.PrefetchScalarGridSpec(
            num_scalar_prefetch=1,
            grid=(EXPERTS,),
            in_specs=[whole((1, SEQ)), whole((SEQ, 1)), whole((128, D))]
            + expert_specs((1, D, hidden))
            + expert_specs((1, hidden, D))
            + [whole((rows, D))] * parts,
            out_specs=[each, each_hidden, each_hidden, whole((SEQ, 1)), whole((rows, 128))]
            + [whole((rows, D))] * parts,
            scratch_shapes=[
                pltpu.VMEM((SEQ, D), BF),
                pltpu.VMEM((SLOTS, D), BF),
                pltpu.VMEM((D, hidden), BF),
                pltpu.VMEM((hidden, D), BF),
            ],
        ),
        out_shape=[
            shape((EXPERTS, CAP, D), BF),
            shape((EXPERTS, CAP, hidden), BF),
            shape((EXPERTS, CAP, hidden), F32),
            shape((SEQ, 1), F32),
            shape((rows, 128), F32),
        ]
        + [shape((rows, D), BF)] * parts,
        compiler_params=pltpu.CompilerParams(vmem_limit_bytes=VMEM_LIMIT),
        cost_estimate=cost(1.2e10, 3e7),
        name="fwd_experts",
    )(select, target_row, target_col, router, *up_pair, *down_pair, *x_parts)
    return outs[:5], list(outs[5:])


def bwd_experts_body(parts, *refs):
    sel, target_row, target_col, gate, slope_ref, up_own, up_other, down_own, down_other = refs[:9]
    g_refs = refs[9 : 9 + parts]
    dout_ref, dup_ref = refs[9 + parts : 11 + parts]
    out_refs = refs[11 + parts : 11 + 2 * parts]
    g_ref, slots_ref, up_ref, down_ref = refs[11 + 2 * parts :]
    rows = SEQ // parts
    e = pl.program_id(0)

    @pl.when(e == 0)
    def _():
        for k in range(parts):
            where = slice(k * rows, (k + 1) * rows)
            g_ref[where, :] = (gate[where, :] * g_refs[k][...].astype(F32)).astype(BF)

    choose(sel[0], up_own, up_other, up_ref)
    choose(sel[0], down_own, down_other, down_ref)
    d_out = dispatch(e, target_row, g_ref)
    dout_ref[0] = d_out
    d_up = (slope_ref[0] * dot(d_out, down_ref[...], 1, 1)).astype(BF)
    dup_ref[0] = d_up
    slots_ref[pl.ds(pl.multiple_of(e * CAP, CAP), CAP), :] = dot(d_up, up_ref[...], 1, 1).astype(
        BF
    )

    @pl.when(e == EXPERTS - 1)
    def _():
        combine(parts, rows, target_col, slots_ref, out_refs)


def bwd_experts(select, target_row, target_col, gate, slope, up_pair, down_pair, g_parts):
    parts = len(g_parts)
    rows = SEQ // parts
    hidden = up_pair[0].shape[2]
    each = pl.BlockSpec((1, CAP, D), lambda e, sel: (e, 0, 0))
    each_hidden = pl.BlockSpec((1, CAP, hidden), lambda e, sel: (e, 0, 0))
    outs = pl.pallas_call(
        functools.partial(bwd_experts_body, parts),
        grid_spec=pltpu.PrefetchScalarGridSpec(
            num_scalar_prefetch=1,
            grid=(EXPERTS,),
            in_specs=[whole((1, SEQ)), whole((SEQ, 1)), whole((SEQ, 1)), each_hidden]
            + expert_specs((1, D, hidden))
            + expert_specs((1, hidden, D))
            + [whole((rows, D))] * parts,
            out_specs=[each, each_hidden] + [whole((rows, D))] * parts,
            scratch_shapes=[
                pltpu.VMEM((SEQ, D), BF),
                pltpu.VMEM((SLOTS, D), BF),
                pltpu.VMEM((D, hidden), BF),
                pltpu.VMEM((hidden, D), BF),
            ],
        ),
        out_shape=[shape((EXPERTS, CAP, D), BF), shape((EXPERTS, CAP, hidden), BF)]
        + [shape((rows, D), BF)] * parts,
        compiler_params=pltpu.CompilerParams(vmem_limit_bytes=VMEM_LIMIT),
        cost_estimate=cost(1.2e10, 3e7),
        name="bwd_experts",
    )(select, target_row, target_col, gate, slope, *up_pair, *down_pair, *g_parts)
    return outs[:2], list(outs[2:])


def norm(vector, gain):
    return vector * lax.rsqrt(jnp.mean(vector * vector, axis=-1, keepdims=True) + epsilon) * gain


def norm_back(vector, gain, grad):
    scale = lax.rsqrt(jnp.mean(vector * vector, axis=-1, keepdims=True) + epsilon)
    unit = vector * scale
    scaled = grad * gain
    inner = jnp.mean(unit * scaled, axis=-1, keepdims=True)
    return scale * (scaled - unit * inner), grad * unit


def total_of(value):
    return jnp.sum(jnp.sum(value, axis=0, keepdims=True), axis=1, keepdims=True)


def after_attention_body(parts, *refs):
    h_ref, gain, valid = refs[:3]
    p_refs, w_refs = refs[3 : 3 + parts], refs[3 + parts : 3 + 2 * parts]
    mid_ref, xn_ref, stat_ref = refs[3 + 2 * parts :]
    branch = dot(p_refs[0][...], w_refs[0][...], 0, 0)
    for k in range(1, parts):
        branch = branch + dot(p_refs[k][...], w_refs[k][...], 0, 0)
    h = h_ref[...].astype(F32)
    mid = h + branch
    mid_ref[...] = mid
    xn_ref[...] = norm(mid, gain[...]).astype(BF)
    weight = valid[...]
    lane = lax.broadcasted_iota(jnp.int32, (1, 128), 1)
    sums = jnp.where(lane == 0, total_of(weight * h * h), 0.0)
    sums = jnp.where(lane == 1, total_of(weight * branch * branch), sums)
    stat_ref[...] = jnp.where(lane == 3, total_of(weight), sums)


def after_attention(h, gain, valid, pieces, w_parts):
    parts = len(pieces)
    rows = h.shape[0]
    return pl.pallas_call(
        functools.partial(after_attention_body, parts),
        out_shape=[shape((rows, D), F32), shape((rows, D), BF), shape((1, 128), F32)],
        in_specs=vm(3 + 2 * parts),
        out_specs=vm(3),
        compiler_params=pltpu.CompilerParams(vmem_limit_bytes=VMEM_LIMIT),
        cost_estimate=cost(2e9, 4e6),
        name="after_attention",
    )(h, gain, valid, *pieces, *w_parts)


def after_experts_body(parts, *refs):
    mid_ref, gate, gain, valid = refs[:4]
    y_refs = refs[4 : 4 + parts]
    comb_ref, out_ref, xn_ref, stat_ref = refs[4 + parts :]
    total = y_refs[0][...].astype(F32)
    for k in range(1, parts):
        total = total + y_refs[k][...].astype(F32)
    combined = total.astype(BF)
    comb_ref[...] = combined
    branch = gate[...] * combined.astype(F32)
    out = (mid_ref[...] + branch).astype(BF)
    out_ref[...] = out
    xn_ref[...] = norm(out.astype(F32), gain[...]).astype(BF)
    lane = lax.broadcasted_iota(jnp.int32, (1, 128), 1)
    stat_ref[...] = jnp.where(lane == 2, total_of(valid[...] * branch * branch), 0.0)


def after_experts(mid, gate, gain, valid, y_parts):
    parts = len(y_parts)
    rows = mid.shape[0]
    return pl.pallas_call(
        functools.partial(after_experts_body, parts),
        out_shape=[shape((rows, D), BF)] * 3 + [shape((1, 128), F32)],
        in_specs=vm(4 + parts),
        out_specs=vm(4),
        compiler_params=pltpu.CompilerParams(vmem_limit_bytes=VMEM_LIMIT),
        cost_estimate=cost(1e8, 4e6),
        name="after_experts",
    )(mid, gate, gain, valid, *y_parts)


def middle_back_body(parts, *refs):
    g_ref, comb_ref, probs_ref, target_col, router, mid_ref, gain, xn_ref = refs[:8]
    y_refs, w_refs = refs[8 : 8 + parts], refs[8 + parts : 8 + 2 * parts]
    dmid_ref, da_ref, gain_ref, router_ref = refs[8 + 2 * parts : 12 + 2 * parts]
    out_refs = refs[12 + 2 * parts :]
    rows = g_ref.shape[0]
    g = g_ref[...].astype(F32)
    total = y_refs[0][...].astype(F32)
    for k in range(1, parts):
        total = total + y_refs[k][...].astype(F32)
    d_in = total.astype(BF).astype(F32)
    d_gate = jnp.sum(g * comb_ref[...].astype(F32), axis=-1, keepdims=True)
    lane = lax.broadcasted_iota(jnp.int32, (rows, 128), 1)
    target = target_col[...]
    hit = (target >= lane * CAP) & (target < lane * CAP + CAP)
    probs = probs_ref[...]
    chosen = jnp.where(hit, d_gate, 0.0)
    inner = jnp.sum(probs * chosen, axis=-1, keepdims=True)
    d_logits = (probs * (chosen - inner)).astype(BF)
    router_ref[...] = dot(d_logits, xn_ref[...], 0, 0)[:8]
    d_xn = d_in + dot(d_logits, router[...])
    d_norm, d_gain = norm_back(mid_ref[...], gain[...], d_xn)
    gain_ref[...] = jnp.sum(d_gain, axis=0, keepdims=True)
    d_mid = g + d_norm
    dmid_ref[...] = d_mid
    d_a = d_mid.astype(BF)
    da_ref[...] = d_a
    for k in list(range(1, parts)) + [0]:
        out_refs[k][...] = dot(d_a, w_refs[k][...], 1, 1).astype(BF)


def middle_back(g, combined, probs, target_col, router, mid, gain, xn, y_parts, w_parts):
    parts = len(y_parts)
    rows = g.shape[0]
    wide = w_parts[0].shape[0]
    outs = pl.pallas_call(
        functools.partial(middle_back_body, parts),
        out_shape=[shape((rows, D), F32), shape((rows, D), BF), shape((1, D), F32)]
        + [shape((8, D), F32)]
        + [shape((rows, wide), BF)] * parts,
        in_specs=vm(8 + 2 * parts),
        out_specs=vm(4 + parts),
        compiler_params=pltpu.CompilerParams(vmem_limit_bytes=VMEM_LIMIT),
        cost_estimate=cost(2e9, 6e6),
        name="middle_back",
    )(g, combined, probs, target_col, router, mid, gain, xn, *y_parts, *w_parts)
    return outs[:4], list(outs[4:])


def input_back_body(parts, *refs):
    dmid_ref, h_ref, gain = refs[:3]
    y_refs = refs[3 : 3 + parts]
    wide_ref, low_ref, gain_ref = refs[3 + parts :]
    total = y_refs[0][...].astype(F32)
    for k in range(1, parts):
        total = total + y_refs[k][...].astype(F32)
    d_norm, d_gain = norm_back(h_ref[...].astype(F32), gain[...], total)
    gain_ref[...] = jnp.sum(d_gain, axis=0, keepdims=True)
    d_h = dmid_ref[...] + d_norm
    wide_ref[...] = d_h
    low_ref[...] = d_h.astype(BF)


def input_back(d_mid, h, gain, y_parts):
    parts = len(y_parts)
    rows = h.shape[0]
    return pl.pallas_call(
        functools.partial(input_back_body, parts),
        out_shape=[shape((rows, D), F32), shape((rows, D), BF), shape((1, D), F32)],
        in_specs=vm(3 + parts),
        out_specs=vm(3),
        compiler_params=pltpu.CompilerParams(vmem_limit_bytes=VMEM_LIMIT),
        cost_estimate=cost(1e8, 4e6),
        name="input_back",
    )(d_mid, h, gain, *y_parts)


def scatter_sum(value, dim):
    count = lax.axis_size("dp")
    if count != 4:
        return lax.psum_scatter(value, "dp", scatter_dimension=dim, tiled=True).astype(F32)
    z = lax.axis_index("dp")
    size = value.shape[dim] // count
    half = size // 2

    def chunk(i, start, length):
        return lax.dynamic_slice_in_dim(value, ((z + i) % count) * size + start, length, dim)

    def send(x, step):
        return lax.ppermute(x, "dp", [(i, (i + step) % count) for i in range(count)])

    ahead = send(chunk(2, 0, half), 1)
    behind = send(chunk(2, half, half), -1)
    low = jnp.concatenate(
        [
            (chunk(1, 0, half).astype(F32) + ahead.astype(F32)).astype(BF),
            chunk(1, half, half),
        ],
        axis=dim,
    )
    high = jnp.concatenate(
        [
            chunk(3, 0, half),
            (chunk(3, half, half).astype(F32) + behind.astype(F32)).astype(BF),
        ],
        axis=dim,
    )
    return (
        chunk(0, 0, size).astype(F32) + send(low, 1).astype(F32) + send(high, -1).astype(F32)
    )


def sum_small(value, axis):
    count = lax.axis_size(axis)
    if count != 4:
        return lax.psum(value, axis)
    return (value + exchange(value, axis, 1)) + (
        exchange(value, axis, 2) + exchange(value, axis, 3)
    )


def local(
    inputs,
    norm_gains,
    attention_in,
    attention_out,
    bias_table,
    router_weight,
    up_weight,
    down_weight,
    routes,
    piece_starts,
    valid_mask,
    cotangent,
):
    s = lax.axis_index("section")
    t = lax.axis_index("tensor")
    z = lax.axis_index("dp")
    tensor = lax.axis_size("tensor")
    rows = inputs.shape[1]
    wide = attention_in.shape[3]
    heads = wide // HEAD_DIM
    first = s == 0

    def mine(array):
        return lax.dynamic_index_in_dim(array, s, 0, keepdims=False)

    def by_layer(own, other):
        return jnp.where(first, own, other), jnp.where(first, other, own)

    def swap(value):
        return exchange(value, "section", 1)

    h0 = mine(inputs)
    g1 = mine(cotangent)
    h0_parts = gather_parts(h0)

    def pack(route_row):
        table = jnp.pad(bias_table[0].reshape(1, -1), ((0, 0), (0, D - BUCKETS * heads)))
        route_rows = jnp.pad(route_row.astype(F32), (0, 2 * D - SEQ)).reshape(2, D)
        return jnp.concatenate(
            [norm_gains[0], router_weight[0].T.astype(F32), table, route_rows], axis=0
        )

    route_own = lax.dynamic_index_in_dim(routes[0], s, 0, keepdims=False)[:, 0]
    route_sent = lax.dynamic_index_in_dim(routes[0], 1 - s, 0, keepdims=False)[:, 0]
    smalls = by_layer(pack(route_own), swap(pack(route_sent)))
    w_in = by_layer(attention_in[0], swap(attention_in[0]))
    w_out = by_layer(attention_out[0], swap(attention_out[0]))
    up_pair = (up_weight[0], swap(up_weight[0]))
    down_pair = (down_weight[0], swap(down_weight[0]))
    w_out_parts = [gather_parts(w_out[0]), gather_parts(w_out[1])]

    valid = mine(valid_mask)
    valid_col = jnp.where(valid > 0, 0.0, masked_score).astype(F32)[:, None]
    valid_own = lax.dynamic_slice_in_dim(valid, t * rows, rows, 0).astype(F32)[:, None]
    starts = mine(piece_starts)
    info = jnp.concatenate([t[None], starts]).astype(jnp.int32)

    hot = diagonal_one_hot()
    tables = jnp.stack([sm[6, : BUCKETS * heads].reshape(BUCKETS, heads) for sm in smalls])
    tables = tables - tables[:, far_bucket_behind : far_bucket_behind + 1]
    bias_rows = jnp.einsum("dyb,lbh->lhdy", hot, tables, precision=lax.Precision.HIGHEST)
    bias = bias_tiles(bias_rows.reshape(2, heads * DIAGS, 2 * BAND))

    gains = [(sm[0:1], sm[1:2]) for sm in smalls]
    routers = [jnp.pad(sm[2:6], ((0, 124), (0, 0))).astype(BF) for sm in smalls]
    order = jnp.bitwise_xor(t, jnp.arange(tensor, dtype=jnp.int32))
    targets = []
    for sm in smalls:
        route = sm[7:9].reshape(-1)[:SEQ].astype(jnp.int32)
        hits = (route[:, None] == jnp.arange(EXPERTS, dtype=jnp.int32)[None, :]).astype(jnp.int32)
        slot = jnp.sum(hits * (jnp.cumsum(hits, axis=0) - 1), axis=1)
        target = (route * CAP + slot).reshape(tensor, rows)
        target = jnp.take(target, order, axis=0).reshape(SEQ)
        targets.append((target[None, :], target[:, None]))
    selects = [jnp.where(s == layer, 0, 1).astype(jnp.int32)[None] for layer in range(2)]

    hidden = [h0, None]
    x_parts = h0_parts
    saved = []
    outputs = []
    stats = []
    for layer in range(2):
        row, col = targets[layer]
        gain_in, gain_mid = gains[layer]
        kept, att_parts = fwd_attention(
            info, valid_col, gain_in, w_in[layer], bias[layer], x_parts, layer == 0
        )
        pieces = swap_parts(att_parts)
        mid, xn_mid, stat = after_attention(
            hidden[layer], gain_mid, valid_own, pieces, w_out_parts[layer]
        )
        ex, y_parts = fwd_experts(
            selects[layer],
            row,
            col,
            routers[layer],
            up_pair,
            down_pair,
            gather_parts(xn_mid),
        )
        gate = ex[3]
        combined, out, xn_next, stat_more = after_experts(
            mid, gate[:rows], gains[1][0], valid_own, swap_parts(y_parts)
        )
        outputs.append(out)
        stats.append(stat + stat_more)
        saved.append((kept, pieces, mid, xn_mid, ex, combined))
        if layer == 0:
            hidden[1] = out
            x_parts = gather_parts(xn_next)

    g = g1
    half = EXPERTS // 2
    grads = [None, None]
    for layer in (1, 0):
        row, col = targets[layer]
        gain_in, gain_mid = gains[layer]
        kept, pieces, mid, xn_mid, ex, combined = saved[layer]
        expert_in, act, slope, gate, probs = ex
        (d_out, d_up), y_parts = bwd_experts(
            selects[layer], row, col, gate, slope, up_pair, down_pair, gather_parts(g)
        )

        def weight_grad(left, right):
            def one(which):
                return jnp.einsum(
                    "eca,ecb->eab",
                    lax.dynamic_slice_in_dim(left, which * half, half, 0),
                    lax.dynamic_slice_in_dim(right, which * half, half, 0),
                    preferred_element_type=F32,
                )

            received = swap(one(1 - s).astype(BF))
            return scatter_sum((one(s) + received.astype(F32)).astype(BF), 1)

        grad_down = weight_grad(act, d_out)
        grad_up = weight_grad(expert_in, d_up)
        (d_mid, d_a, grad_gain_mid, grad_router), d_pieces = middle_back(
            g,
            combined,
            probs,
            col[:rows],
            routers[layer],
            mid,
            gain_mid,
            xn_mid,
            swap_parts(y_parts),
            w_out_parts[layer],
        )
        out_terms = swap_parts([dot(piece, d_a).astype(BF) for piece in pieces])
        grad_w_out = functools.reduce(jnp.add, [term.astype(F32) for term in out_terms])
        xn, qkv, turned, lse = kept
        (d_proj, diag, far), x_terms = bwd_attention(
            info, valid_col, w_in[layer], bias[layer], (qkv, turned, lse), swap_parts(d_pieces)
        )
        grad_w_in = jnp.einsum("sd,jsf->jdf", xn, d_proj, preferred_element_type=F32)
        grad_table = jnp.einsum(
            "dyb,hdy->bh",
            hot,
            diagonal_sums(diag).reshape(heads, DIAGS, 2 * BAND),
            precision=lax.Precision.HIGHEST,
        )
        grad_table = grad_table.at[far_bucket_behind].add(jnp.sum(far, axis=(1, 2)))
        d_h, d_h_low, grad_gain_in = input_back(
            d_mid, hidden[layer], gain_in, swap_parts(x_terms)
        )
        g = d_h_low
        small = jnp.concatenate(
            [
                grad_gain_in,
                grad_gain_mid,
                grad_router[:EXPERTS],
                jnp.pad(stats[layer], ((0, 0), (0, D - 128))),
                jnp.pad(grad_table.reshape(1, -1), ((0, 0), (0, D - BUCKETS * heads))),
            ],
            axis=0,
        )
        grads[layer] = (
            d_h,
            grad_down,
            grad_up,
            grad_w_in.astype(BF),
            grad_w_out.astype(BF),
            small,
        )

    def kept_sent(pair):
        return jnp.where(first, pair[0], pair[1]), jnp.where(first, pair[1], pair[0])

    def placed(own, received):
        return jnp.where(
            first,
            jnp.concatenate([own, received], axis=0),
            jnp.concatenate([received, own], axis=0),
        )

    keep, sent = kept_sent(outputs)
    layer_out = placed(keep[None], swap(sent)[None])
    keep, sent = kept_sent((grads[0][0], grads[1][0].astype(BF).astype(F32)))
    input_grad = placed(keep[None], swap(sent.astype(BF)).astype(F32)[None])
    expert_grads = []
    for which in (1, 2):
        keep, sent = kept_sent((grads[0][which], grads[1][which]))
        expert_grads.append(placed(keep, swap(sent.astype(BF)).astype(F32)))
    keep, sent = kept_sent((grads[0][3], grads[1][3]))
    grad_w_in = scatter_sum((keep.astype(F32) + swap(sent).astype(F32)).astype(BF), 1)
    keep, sent = kept_sent((grads[0][4], grads[1][4]))
    grad_w_out = scatter_sum((keep.astype(F32) + swap(sent).astype(F32)).astype(BF), 0)
    keep, sent = kept_sent((grads[0][5], grads[1][5]))
    small = keep + swap(sent)
    shared = sum_small(small[:7], "tensor")
    small = sum_small(jnp.concatenate([shared, small[7:]], axis=0), "dp")
    table = small[7, : BUCKETS * heads].reshape(BUCKETS, heads)
    share = BUCKETS // lax.axis_size("dp")
    stat = small[6]
    root_means = jnp.sqrt(stat[:3] / (stat[3] * D))
    return (
        layer_out[None],
        input_grad[None],
        small[None, 0:2],
        grad_w_in[None],
        grad_w_out[None],
        lax.dynamic_slice_in_dim(table, z * share, share, 0)[None],
        small[2:6].T[None],
        expert_grads[1][None],
        expert_grads[0][None],
        root_means[None],
    )


def solution(mesh):
    placed = (
        P("dp", "tensor", None),
        P("section", None, None),
        P("section", None, None, "tensor"),
        P("section", "tensor", None),
        P("section", None, "tensor"),
        P("section", None, None),
        P("section", None, None, "tensor"),
        P("section", None, "tensor", None),
        P("section", "dp", None, None),
        P("dp", None),
        P("dp", None),
        P("dp", "tensor", None),
    )
    return jax.shard_map(
        local,
        mesh=mesh,
        in_specs=placed,
        out_specs=(
            P("section", "dp", "tensor", None),
            P("section", "dp", "tensor", None),
            P("section", None, None),
            P("section", None, "dp", "tensor"),
            P("section", ("tensor", "dp"), None),
            P("section", "dp", "tensor"),
            P("section", None, None),
            P("section", None, "dp", "tensor"),
            P("section", None, ("tensor", "dp"), None),
            P("section", None),
        ),
        check_vma=False,
    )
```

profile of v0, /device:TPU:0, one launch (start us, length us, event | category | flops | bytes accessed | tf_op | source)
XLA Modules:
  0.0 680.8 jit_solution(3462497948688684841)
XLA Ops:
  38.2 12.5 %collective-permute-done.3.refs_7_ = bf16[256,768]{1,0:T(8,128)(2,1)} collective-permute-done((bf16[256,768]{1,0:T(8,128)(2,1)S(1)}, bf16[256,768]{1,0:T(8,128)(2,1)}, u32[]{:S(2)}, u32[]{:S(2)}) %collective-permute-start.3) | collective-permute-done | bytes 393248 | tf_op jit(solution)/shard_map/ppermute | solution.py:58
  52.5 15.6 %fwd_attention.2 = (bf16[1024,768]{1,0:T(8,128)(2,1)}, bf16[3,3,1024,64]{3,2,1,0:T(8,128)(2,1)}, bf16[2,192,1024]{2,1,0:T(8,128)(2,1)}, f32[3,1,1024]{2,1,0:T(1,...) custom-call(s32[3]{0:T(128)} %pad_add_fusion.refs_0_, ...), custom_call_target="tpu_custom_call" | custom-call | flops 8999999488 | bytes 10000000 | tf_op jit(solution)/shard_map/fwd_attention/pallas_call | solution.py:208
  87.0 6.4 collective-permute-done.14.refs_9_
  93.3 5.9 collective-permute-done.15.refs_10_
  100.1 17.5 %fwd_experts.2 = (bf16[4,320,768]{2,1,0:T(8,128)(2,1)}, bf16[4,320,768]{2,1,0:T(8,128)(2,1)}, f32[4,320,768]{2,1,0:T(8,128)}, f32[1024,1]{1,0:T(8,128)}, f32[256...) custom-call(s32[1]{0:T(128)} %bitcast.19.refs_0_, ...), custom_call_target="tpu_custom_call" | custom-call | flops 12000000000 | bytes 30000000 | tf_op jit(solution)/shard_map/fwd_experts/pallas_call | solution.py:475
  124.2 5.3 collective-permute-done.17.refs_5_
  129.5 5.9 collective-permute-done.18.refs_6_
  144.9 6.7 collective-permute-done.20.refs_6_
  153.1 8.5 %collective-permute-done.21.refs_7_ = bf16[256,768]{1,0:T(8,128)(2,1)S(1)} collective-permute-done((bf16[256,768]{1,0:T(8,128)(2,1)}, bf16[256,768]{1,0:T(8,128)(2,1)S(1)}, u32[]{:S(2)}, u32[]{:S(2)}) %collective-permute-start.21) | collective-permute-done | bytes 393248 | tf_op jit(solution)/shard_map/ppermute | solution.py:58
  162.6 15.0 %fwd_attention.3 = (bf16[1024,768]{1,0:T(8,128)(2,1)}, bf16[3,3,1024,64]{3,2,1,0:T(8,128)(2,1)}, bf16[2,192,1024]{2,1,0:T(8,128)(2,1)}, f32[3,1,1024]{2,1,0:T(1,...) custom-call(s32[3]{0:T(128)} %pad_add_fusion.refs_0_, ...), custom_call_target="tpu_custom_call" | custom-call | flops 8999999488 | bytes 10000000 | tf_op jit(solution)/shard_map/fwd_attention/pallas_call | solution.py:208
  195.1 8.8 %collective-permute-done.29.refs_9_ = bf16[256,768]{1,0:T(8,128)(2,1)S(1)} collective-permute-done((bf16[256,768]{1,0:T(8,128)(2,1)}, bf16[256,768]{1,0:T(8,128)(2,1)S(1)}, u32[]{:S(2)}, u32[]{:S(2)}) %collective-permute-start.29) | collective-permute-done | bytes 393248 | tf_op jit(solution)/shard_map/ppermute | solution.py:58
  204.3 8.6 %collective-permute-done.30.refs_10_ = bf16[256,768]{1,0:T(8,128)(2,1)S(1)} collective-permute-done((bf16[256,768]{1,0:T(8,128)(2,1)}, bf16[256,768]{1,0:T(8,128)(2,1)S(1)}, u32[]{:S(2)}, u32[]{:S(2)}) %collective-permute-start.30) | collective-permute-done | bytes 393248 | tf_op jit(solution)/shard_map/ppermute | solution.py:58
  213.8 17.7 %fwd_experts.3 = (bf16[4,320,768]{2,1,0:T(8,128)(2,1)}, bf16[4,320,768]{2,1,0:T(8,128)(2,1)}, f32[4,320,768]{2,1,0:T(8,128)}, f32[1024,1]{1,0:T(8,128)}, f32[256...) custom-call(s32[1]{0:T(128)} %bitcast.24.refs_0_, ...), custom_call_target="tpu_custom_call" | custom-call | flops 12000000000 | bytes 30000000 | tf_op jit(solution)/shard_map/fwd_experts/pallas_call | solution.py:475
  236.0 16.1 %bwd_experts.2 = (bf16[4,320,768]{2,1,0:T(8,128)(2,1)}, bf16[4,320,768]{2,1,0:T(8,128)(2,1)}, bf16[256,768]{1,0:T(8,128)(2,1)}, bf16[256,768]{1,0:T(8,128)(2,1)}...) custom-call(s32[1]{0:T(128)} %bitcast.24.refs_0_, s32[1,1024]{1,0:T(1,128)} %bitcast.195, s32[1024,1]{1,0:T(8,128)} %bitcast.175, ...), custom_call_target="tpu_custom_call" | custom-call | flops 12000000000 | bytes 30000000 | tf_op jit(solution)/shard_map/bwd_experts/pallas_call | solution.py:544
  286.0 20.2 %bwd_attention.2 = (bf16[3,1024,192]{2,1,0:T(8,128)(2,1)}, f32[18,128,128]{2,1,0:T(8,128)}, f32[3,8,256]{2,1,0:T(8,128)}, bf16[256,768]{1,0:T(8,128)(2,1)}, bf16...) custom-call(s32[3]{0:T(128)} %pad_add_fusion.refs_0_, f32[1024,1]{1,0:T(8,128)} %copy.85.refs_1_, ...), custom_call_target="tpu_custom_call" | custom-call | flops 17999998976 | bytes 10000000 | tf_op jit(solution)/shard_map/bwd_attention/pallas_call | solution.py:364
  318.5 6.9 %collective-permute-done.47.refs_6_ = bf16[256,768]{1,0:T(8,128)(2,1)S(1)} collective-permute-done((bf16[256,768]{1,0:T(8,128)(2,1)}, bf16[256,768]{1,0:T(8,128)(2,1)S(1)}, u32[]{:S(2)}, u32[]{:S(2)}) %collective-permute-start.47) | collective-permute-done | bytes 393248 | tf_op jit(solution)/shard_map/ppermute | solution.py:58
  336.4 5.3 collective-permute-done.48.refs_10_
  341.8 7.3 %collective-permute-done.49.refs_11_ = bf16[256,768]{1,0:T(8,128)(2,1)S(1)} collective-permute-done((bf16[256,768]{1,0:T(8,128)(2,1)}, bf16[256,768]{1,0:T(8,128)(2,1)S(1)}, u32[]{:S(2)}, u32[]{:S(2)}) %collective-permute-start.49) | collective-permute-done | bytes 393248 | tf_op jit(solution)/shard_map/ppermute | solution.py:58
  349.8 16.9 %bwd_experts.3 = (bf16[4,320,768]{2,1,0:T(8,128)(2,1)}, bf16[4,320,768]{2,1,0:T(8,128)(2,1)}, bf16[256,768]{1,0:T(8,128)(2,1)}, bf16[256,768]{1,0:T(8,128)(2,1)}...) custom-call(s32[1]{0:T(128)} %bitcast.19.refs_0_, s32[1,1024]{1,0:T(1,128)} %bitcast.192, s32[1024,1]{1,0:T(8,128)} %bitcast.173, ...), custom_call_target="tpu_custom_call" | custom-call | flops 12000000000 | bytes 30000000 | tf_op jit(solution)/shard_map/bwd_experts/pallas_call | solution.py:544
  403.2 20.4 %bwd_attention.3 = (bf16[3,1024,192]{2,1,0:T(8,128)(2,1)}, f32[18,128,128]{2,1,0:T(8,128)}, f32[3,8,256]{2,1,0:T(8,128)}, bf16[256,768]{1,0:T(8,128)(2,1)}, bf16...) custom-call(s32[3]{0:T(128)} %pad_add_fusion.refs_0_, f32[1024,1]{1,0:T(8,128)} %copy.85.refs_1_, ...), custom_call_target="tpu_custom_call" | custom-call | flops 17999998976 | bytes 10000000 | tf_op jit(solution)/shard_map/bwd_attention/pallas_call | solution.py:364
  501.2 6.0 collective-permute-done.90
  515.7 4.9 collective-permute-done.101
  520.6 14.7 %collective-permute-start.91 = (bf16[2,192,768]{2,1,0:T(8,128)(2,1)S(1)}, bf16[2,192,768]{2,1,0:T(8,128)(2,1)S(1)}, u32[]{:S(2)}, u32[]{:S(2)}) collective-permute-start(bf16[2,192,768]{2,1,0:T(8,128)(2,1)S(1)} %pad_maximum_fusion.2), channel_id=1, source_target_pairs={{0,1},{1,2},{2,3},{3,0},{4,5},{5,6},{6,7},{7,4},{8,9},{9,10},{10,1... | collective-permute-start | bytes 1769480 | tf_op jit(solution)/shard_map/ppermute | solution.py:738
  546.4 14.1 %collective-permute-done.85 = bf16[2,96,768]{2,1,0:T(8,128)(2,1)S(1)} collective-permute-done((bf16[2,96,768]{2,1,0:T(8,128)(2,1)S(1)}, bf16[2,96,768]{2,1,0:T(8,128)(2,1)S(1)}, u32[]{:S(2)}, u32[]{:S(2)}) %collective-permute-start.85) | collective-permute-done | bytes 294944 | tf_op jit(solution)/shard_map/ppermute | solution.py:738
  560.5 11.4 %collective-permute-start.98 = (bf16[2,96,768]{2,1,0:T(8,128)(2,1)S(1)}, bf16[2,96,768]{2,1,0:T(8,128)(2,1)S(1)}, u32[]{:S(2)}, u32[]{:S(2)}) collective-permute-start(bf16[2,96,768]{2,1,0:T(8,128)(2,1)S(1)} %get-tuple-element.268), channel_id=1, source_target_pairs={{0,3},{1,0},{2,1},{3,2},{4,7},{5,4},{6,5},{7,6},{8,11},{9,8},{10,9... | collective-permute-start | bytes 884744 | tf_op jit(solution)/shard_map/ppermute | solution.py:738
  573.1 8.6 %collective-permute-start.69 = (bf16[3,96,192]{1,2,0:T(8,128)(2,1)S(1)}, bf16[3,96,192]{1,2,0:T(8,128)(2,1)S(1)}, u32[]{:S(2)}, u32[]{:S(2)}) collective-permute-start(bf16[3,96,192]{1,2,0:T(8,128)(2,1)S(1)} %get-tuple-element.287), channel_id=1, source_target_pairs={{0,1},{1,2},{2,3},{3,0},{4,5},{5,6},{6,7},{7,4},{8,9},{9,10},{10,1... | collective-permute-start | bytes 331784 | tf_op jit(solution)/shard_map/ppermute | solution.py:738
  581.7 7.4 %collective-permute-start.86 = (bf16[2,192,768]{2,1,0:T(8,128)(2,1)S(1)}, bf16[2,192,768]{2,1,0:T(8,128)(2,1)S(1)}, u32[]{:S(2)}, u32[]{:S(2)}) collective-permute-start(bf16[2,192,768]{2,1,0:T(8,128)(2,1)S(1)} %pad_maximum_fusion), channel_id=1, source_target_pairs={{0,1},{1,2},{2,3},{3,0},{4,5},{5,6},{6,7},{7,4},{8,9},{9,10},{10,1... | collective-permute-start | bytes 1769480 | tf_op jit(solution)/shard_map/ppermute | solution.py:738
  589.3 6.5 collective-permute-done.69
  600.3 7.8 %collective-permute-done.71 = bf16[3,96,192]{1,2,0:T(8,128)(2,1)S(1)} collective-permute-done((bf16[3,96,192]{1,2,0:T(8,128)(2,1)S(1)}, bf16[3,96,192]{1,2,0:T(8,128)(2,1)S(1)}, u32[]{:S(2)}, u32[]{:S(2)}) %collective-permute-start.71) | collective-permute-done | bytes 110624 | tf_op jit(solution)/shard_map/ppermute | solution.py:738
  614.0 22.1 %collective-permute-done.104 = bf16[2,192,768]{2,1,0:T(8,128)(2,1)S(1)} collective-permute-done((bf16[2,192,768]{2,1,0:T(8,128)(2,1)S(1)}, bf16[2,192,768]{2,1,0:T(8,128)(2,1)S(1)}, u32[]{:S(2)}, u32[]{:S(2)}) %collective-permute-start.104) | collective-permute-done | bytes 589856 | tf_op jit(solution)/shard_map/ppermute | solution.py:738
  638.2 25.4 %collective-permute-done.99 = bf16[2,192,768]{2,1,0:T(8,128)(2,1)S(1)} collective-permute-done((bf16[2,192,768]{2,1,0:T(8,128)(2,1)S(1)}, bf16[2,192,768]{2,1,0:T(8,128)(2,1)S(1)}, u32[]{:S(2)}, u32[]{:S(2)}) %collective-permute-start.99) | collective-permute-done | bytes 589856 | tf_op jit(solution)/shard_map/ppermute | solution.py:738
  664.9 8.9 %collective-permute-done.72 = bf16[3,192,192]{1,2,0:T(8,128)(2,1)S(1)} collective-permute-done((bf16[3,192,192]{1,2,0:T(8,128)(2,1)S(1)}, bf16[3,192,192]{1,2,0:T(8,128)(2,1)S(1)}, u32[]{:S(2)}, u32[]{:S(2)}) %collective-permute-start.72) | collective-permute-done | bytes 221216 | tf_op jit(solution)/shard_map/ppermute | solution.py:738
  (579 shorter events, 312.7 us)
Async XLA Ops:
  5.0 32.1 %collective-permute-start.2 = (bf16[256,768]{1,0:T(8,128)(2,1)S(1)}, bf16[256,768]{1,0:T(8,128)(2,1)}, u32[]{:S(2)}, u32[]{:S(2)}) collective-permute-start(bf16[256,768]{1,0:T(8,128)(2,1)S(1)} %dynamic-slice_bitcast_fusion.1.refs_5_.refs_0_.refs_1_), channel_id=1, source_target_pairs={{0,4},{4,0},{8,12},{12,8},{1,5},{5,1},{9,13},{13,9},{2,6},{6,2},{1... | collective-permute-start | bytes 1179656 | tf_op jit(solution)/shard_map/ppermute | solution.py:58
  8.0 91.3 %collective-permute-start.12 = (bf16[4,768,768]{2,1,0:T(8,128)(2,1)}, bf16[4,768,768]{2,1,0:T(8,128)(2,1)}, u32[]{:S(2)}, u32[]{:S(2)}) collective-permute-start(bf16[4,768,768]{2,1,0:T(8,128)(2,1)} %bitcast.203), channel_id=1, source_target_pairs={{0,16},{16,0},{1,17},{17,1},{2,18},{18,2},{3,19},{19,3},{4,20},{20... | collective-permute-start | bytes 14155784 | tf_op jit(solution)/shard_map/ppermute | solution.py:58
  14.7 84.6 %collective-permute-start.13 = (bf16[4,768,768]{2,1,0:T(8,128)(2,1)}, bf16[4,768,768]{2,1,0:T(8,128)(2,1)}, u32[]{:S(2)}, u32[]{:S(2)}) collective-permute-start(bf16[4,768,768]{2,1,0:T(8,128)(2,1)} %bitcast.208), channel_id=1, source_target_pairs={{0,16},{16,0},{1,17},{17,1},{2,18},{18,2},{3,19},{19,3},{4,20},{20... | collective-permute-start | bytes 14155784 | tf_op jit(solution)/shard_map/ppermute | solution.py:58
  37.1 31.0 %collective-permute-start.9 = (bf16[192,768]{1,0:T(8,128)(2,1)S(1)}, bf16[192,768]{1,0:T(8,128)(2,1)S(1)}, u32[]{:S(2)}, u32[]{:S(2)}) collective-permute-start(bf16[192,768]{1,0:T(8,128)(2,1)S(1)} %get-tuple-element.294.refs_7_.refs_12_), channel_id=1, source_target_pairs={{0,4},{4,0},{8,12},{12,8},{1,5},{5,1},{9,13},{13,9},{2,6},{6,2},{1... | collective-permute-start | bytes 884744 | tf_op jit(solution)/shard_map/ppermute | solution.py:58
  142.9 35.6 %collective-permute-start.26 = (bf16[192,768]{1,0:T(8,128)(2,1)S(1)}, bf16[192,768]{1,0:T(8,128)(2,1)S(1)}, u32[]{:S(2)}, u32[]{:S(2)}) collective-permute-start(bf16[192,768]{1,0:T(8,128)(2,1)S(1)} %copy-done.26), channel_id=1, source_target_pairs={{0,4},{4,0},{8,12},{12,8},{1,5},{5,1},{9,13},{13,9},{2,6},{6,2},{1... | collective-permute-start | bytes 884744 | tf_op jit(solution)/shard_map/ppermute | solution.py:58
  143.5 40.1 %collective-permute-start.27 = (bf16[192,768]{1,0:T(8,128)(2,1)S(1)}, bf16[192,768]{1,0:T(8,128)(2,1)S(1)}, u32[]{:S(2)}, u32[]{:S(2)}) collective-permute-start(bf16[192,768]{1,0:T(8,128)(2,1)S(1)} %copy-done.26), channel_id=1, source_target_pairs={{0,8},{4,12},{8,0},{12,4},{1,9},{5,13},{9,1},{13,5},{2,10},{6,14},... | collective-permute-start | bytes 884744 | tf_op jit(solution)/shard_map/ppermute | solution.py:58
  151.6 32.9 %collective-permute-start.28 = (bf16[192,768]{1,0:T(8,128)(2,1)S(1)}, bf16[192,768]{1,0:T(8,128)(2,1)}, u32[]{:S(2)}, u32[]{:S(2)}) collective-permute-start(bf16[192,768]{1,0:T(8,128)(2,1)S(1)} %copy-done.26), channel_id=1, source_target_pairs={{0,12},{4,8},{8,4},{12,0},{1,13},{5,9},{9,5},{13,1},{2,14},{6,10},... | collective-permute-start | bytes 884744 | tf_op jit(solution)/shard_map/ppermute | solution.py:58
  183.6 49.7 %collective-permute-start.36 = (bf16[256,768]{1,0:T(8,128)(2,1)S(1)}, bf16[256,768]{1,0:T(8,128)(2,1)S(1)}, u32[]{:S(2)}, u32[]{:S(2)}) collective-permute-start(bf16[256,768]{1,0:T(8,128)(2,1)S(1)} %dynamic-slice_bitcast_fusion.refs_9_.refs_0_), channel_id=1, source_target_pairs={{0,4},{4,0},{8,12},{12,8},{1,5},{5,1},{9,13},{13,9},{2,6},{6,2},{1... | collective-permute-start | bytes 1179656 | tf_op jit(solution)/shard_map/ppermute | solution.py:58
  184.6 50.6 %collective-permute-start.37 = (bf16[256,768]{1,0:T(8,128)(2,1)S(1)}, bf16[256,768]{1,0:T(8,128)(2,1)S(1)}, u32[]{:S(2)}, u32[]{:S(2)}) collective-permute-start(bf16[256,768]{1,0:T(8,128)(2,1)S(1)} %dynamic-slice_bitcast_fusion.refs_9_.refs_0_), channel_id=1, source_target_pairs={{0,8},{4,12},{8,0},{12,4},{1,9},{5,13},{9,1},{13,5},{2,10},{6,14},... | collective-permute-start | bytes 1179656 | tf_op jit(solution)/shard_map/ppermute | solution.py:58
  204.0 31.1 %collective-permute-start.38 = (bf16[256,768]{1,0:T(8,128)(2,1)S(1)}, bf16[256,768]{1,0:T(8,128)(2,1)S(1)}, u32[]{:S(2)}, u32[]{:S(2)}) collective-permute-start(bf16[256,768]{1,0:T(8,128)(2,1)S(1)} %dynamic-slice_bitcast_fusion.refs_9_.refs_0_), channel_id=1, source_target_pairs={{0,12},{4,8},{8,4},{12,0},{1,13},{5,9},{9,5},{13,1},{2,14},{6,10},... | collective-permute-start | bytes 1179656 | tf_op jit(solution)/shard_map/ppermute | solution.py:58
  232.9 31.4 %collective-permute-start.33 = (bf16[256,768]{1,0:T(8,128)(2,1)}, bf16[256,768]{1,0:T(8,128)(2,1)S(1)}, u32[]{:S(2)}, u32[]{:S(2)}) collective-permute-start(bf16[256,768]{1,0:T(8,128)(2,1)} %get-tuple-element.151), channel_id=1, source_target_pairs={{0,8},{4,12},{8,0},{12,4},{1,9},{5,13},{9,1},{13,5},{2,10},{6,14},... | collective-permute-start | bytes 1179656 | tf_op jit(solution)/shard_map/ppermute | solution.py:58
  233.3 31.0 %collective-permute-start.34 = (bf16[256,768]{1,0:T(8,128)(2,1)}, bf16[256,768]{1,0:T(8,128)(2,1)S(1)}, u32[]{:S(2)}, u32[]{:S(2)}) collective-permute-start(bf16[256,768]{1,0:T(8,128)(2,1)} %get-tuple-element.152), channel_id=1, source_target_pairs={{0,12},{4,8},{8,4},{12,0},{1,13},{5,9},{9,5},{13,1},{2,14},{6,10},... | collective-permute-start | bytes 1179656 | tf_op jit(solution)/shard_map/ppermute | solution.py:58
  269.4 100.9 %collective-permute-start.35 = (bf16[256,768]{1,0:T(8,128)(2,1)S(1)}, bf16[256,768]{1,0:T(8,128)(2,1)S(1)}, u32[]{:S(2)}, u32[]{:S(2)}) collective-permute-start(bf16[256,768]{1,0:T(8,128)(2,1)S(1)} %get-tuple-element.292), channel_id=1, source_target_pairs={{0,16},{16,0},{1,17},{17,1},{2,18},{18,2},{3,19},{19,3},{4,20},{20... | collective-permute-start | bytes 1179656 | tf_op jit(solution)/shard_map/ppermute | solution.py:58
  395.1 40.3 %collective-permute-start.75 = (bf16[192,768]{1,0:T(8,128)(2,1)}, bf16[192,768]{1,0:T(8,128)(2,1)}, u32[]{:S(2)}, u32[]{:S(2)}) collective-permute-start(bf16[192,768]{1,0:T(8,128)(2,1)} %convolution_convert_fusion.8), channel_id=1, source_target_pairs={{0,12},{4,8},{8,4},{12,0},{1,13},{5,9},{9,5},{13,1},{2,14},{6,10},... | collective-permute-start | bytes 884744 | tf_op jit(solution)/shard_map/ppermute | solution.py:58
  398.1 40.1 %collective-permute-start.74 = (bf16[192,768]{1,0:T(8,128)(2,1)}, bf16[192,768]{1,0:T(8,128)(2,1)}, u32[]{:S(2)}, u32[]{:S(2)}) collective-permute-start(bf16[192,768]{1,0:T(8,128)(2,1)} %convolution_convert_fusion.9), channel_id=1, source_target_pairs={{0,8},{4,12},{8,0},{12,4},{1,9},{5,13},{9,1},{13,5},{2,10},{6,14},... | collective-permute-start | bytes 884744 | tf_op jit(solution)/shard_map/ppermute | solution.py:58
  401.6 37.7 %collective-permute-start.73 = (bf16[192,768]{1,0:T(8,128)(2,1)}, bf16[192,768]{1,0:T(8,128)(2,1)}, u32[]{:S(2)}, u32[]{:S(2)}) collective-permute-start(bf16[192,768]{1,0:T(8,128)(2,1)} %convolution_convert_fusion.10), channel_id=1, source_target_pairs={{0,4},{4,0},{8,12},{12,8},{1,5},{5,1},{9,13},{13,9},{2,6},{6,2},{1... | collective-permute-start | bytes 884744 | tf_op jit(solution)/shard_map/ppermute | solution.py:58
  443.9 38.2 %collective-permute-start.89 = (bf16[2,768,768]{2,1,0:T(8,128)(2,1)}, bf16[2,768,768]{2,1,0:T(8,128)(2,1)}, u32[]{:S(2)}, u32[]{:S(2)}) collective-permute-start(bf16[2,768,768]{2,1,0:T(8,128)(2,1)} %convolution_convert_fusion.2), channel_id=1, source_target_pairs={{0,16},{16,0},{1,17},{17,1},{2,18},{18,2},{3,19},{19,3},{4,20},{20... | collective-permute-start | bytes 7077896 | tf_op jit(solution)/shard_map/ppermute | solution.py:58
  446.8 42.1 %collective-permute-start.100 = (bf16[2,768,768]{2,1,0:T(8,128)(2,1)}, bf16[2,768,768]{2,1,0:T(8,128)(2,1)}, u32[]{:S(2)}, u32[]{:S(2)}) collective-permute-start(bf16[2,768,768]{2,1,0:T(8,128)(2,1)} %convolution_convert_fusion), channel_id=1, source_target_pairs={{0,16},{16,0},{1,17},{17,1},{2,18},{18,2},{3,19},{19,3},{4,20},{20... | collective-permute-start | bytes 7077896 | tf_op jit(solution)/shard_map/ppermute | solution.py:58
  467.8 67.8 %collective-permute-start.84 = (bf16[2,768,768]{2,1,0:T(8,128)(2,1)}, bf16[2,768,768]{2,1,0:T(8,128)(2,1)}, u32[]{:S(2)}, u32[]{:S(2)}) collective-permute-start(bf16[2,768,768]{2,1,0:T(8,128)(2,1)} %convolution_convert_fusion.3), channel_id=1, source_target_pairs={{0,16},{16,0},{1,17},{17,1},{2,18},{18,2},{3,19},{19,3},{4,20},{20... | collective-permute-start | bytes 7077896 | tf_op jit(solution)/shard_map/ppermute | solution.py:58
  481.5 62.2 %collective-permute-start.95 = (bf16[2,768,768]{2,1,0:T(8,128)(2,1)}, bf16[2,768,768]{2,1,0:T(8,128)(2,1)S(1)}, u32[]{:S(2)}, u32[]{:S(2)}) collective-permute-start(bf16[2,768,768]{2,1,0:T(8,128)(2,1)} %convolution_convert_fusion.1), channel_id=1, source_target_pairs={{0,16},{16,0},{1,17},{17,1},{2,18},{18,2},{3,19},{19,3},{4,20},{20... | collective-permute-start | bytes 7077896 | tf_op jit(solution)/shard_map/ppermute | solution.py:58
  513.6 94.7 %collective-permute-start.93 = (bf16[2,192,768]{2,1,0:T(8,128)(2,1)S(1)}, bf16[2,192,768]{2,1,0:T(8,128)(2,1)S(1)}, u32[]{:S(2)}, u32[]{:S(2)}) collective-permute-start(bf16[2,192,768]{2,1,0:T(8,128)(2,1)S(1)} %pad_maximum_fusion.3), channel_id=1, source_target_pairs={{0,3},{1,0},{2,1},{3,2},{4,7},{5,4},{6,5},{7,6},{8,11},{9,8},{10,9... | collective-permute-start | bytes 1769480 | tf_op jit(solution)/shard_map/ppermute | solution.py:738
  520.6 89.5 %collective-permute-start.91 = (bf16[2,192,768]{2,1,0:T(8,128)(2,1)S(1)}, bf16[2,192,768]{2,1,0:T(8,128)(2,1)S(1)}, u32[]{:S(2)}, u32[]{:S(2)}) collective-permute-start(bf16[2,192,768]{2,1,0:T(8,128)(2,1)S(1)} %pad_maximum_fusion.2), channel_id=1, source_target_pairs={{0,1},{1,2},{2,3},{3,0},{4,5},{5,6},{6,7},{7,4},{8,9},{9,10},{10,1... | collective-permute-start | bytes 1769480 | tf_op jit(solution)/shard_map/ppermute | solution.py:738
  542.2 29.7 %collective-permute-start.87 = (bf16[2,96,768]{2,1,0:T(8,128)(2,1)S(1)}, bf16[2,96,768]{2,1,0:T(8,128)(2,1)S(1)}, u32[]{:S(2)}, u32[]{:S(2)}) collective-permute-start(bf16[2,96,768]{2,1,0:T(8,128)(2,1)S(1)} %get-tuple-element.280), channel_id=1, source_target_pairs={{0,3},{1,0},{2,1},{3,2},{4,7},{5,4},{6,5},{7,6},{8,11},{9,8},{10,9... | collective-permute-start | bytes 884744 | tf_op jit(solution)/shard_map/ppermute | solution.py:738
  572.1 40.1 %collective-permute-start.88 = (bf16[2,192,768]{2,1,0:T(8,128)(2,1)S(1)}, bf16[2,192,768]{2,1,0:T(8,128)(2,1)S(1)}, u32[]{:S(2)}, u32[]{:S(2)}) collective-permute-start(bf16[2,192,768]{2,1,0:T(8,128)(2,1)S(1)} %pad_maximum_fusion.1), channel_id=1, source_target_pairs={{0,3},{1,0},{2,1},{3,2},{4,7},{5,4},{6,5},{7,6},{8,11},{9,8},{10,9... | collective-permute-start | bytes 1769480 | tf_op jit(solution)/shard_map/ppermute | solution.py:738
  581.7 30.8 %collective-permute-start.86 = (bf16[2,192,768]{2,1,0:T(8,128)(2,1)S(1)}, bf16[2,192,768]{2,1,0:T(8,128)(2,1)S(1)}, u32[]{:S(2)}, u32[]{:S(2)}) collective-permute-start(bf16[2,192,768]{2,1,0:T(8,128)(2,1)S(1)} %pad_maximum_fusion), channel_id=1, source_target_pairs={{0,1},{1,2},{2,3},{3,0},{4,5},{5,6},{6,7},{7,4},{8,9},{9,10},{10,1... | collective-permute-start | bytes 1769480 | tf_op jit(solution)/shard_map/ppermute | solution.py:738
  608.1 28.0 %collective-permute-start.104 = (bf16[2,192,768]{2,1,0:T(8,128)(2,1)S(1)}, bf16[2,192,768]{2,1,0:T(8,128)(2,1)S(1)}, u32[]{:S(2)}, u32[]{:S(2)}) collective-permute-start(bf16[2,192,768]{2,1,0:T(8,128)(2,1)S(1)} %pad_maximum_fusion.7), channel_id=1, source_target_pairs={{0,3},{1,0},{2,1},{3,2},{4,7},{5,4},{6,5},{7,6},{8,11},{9,8},{10,9... | collective-permute-start | bytes 1769480 | tf_op jit(solution)/shard_map/ppermute | solution.py:738
  608.4 29.4 %collective-permute-start.102 = (bf16[2,192,768]{2,1,0:T(8,128)(2,1)S(1)}, bf16[2,192,768]{2,1,0:T(8,128)(2,1)S(1)}, u32[]{:S(2)}, u32[]{:S(2)}) collective-permute-start(bf16[2,192,768]{2,1,0:T(8,128)(2,1)S(1)} %pad_maximum_fusion.6), channel_id=1, source_target_pairs={{0,1},{1,2},{2,3},{3,0},{4,5},{5,6},{6,7},{7,4},{8,9},{9,10},{10,1... | collective-permute-start | bytes 1769480 | tf_op jit(solution)/shard_map/ppermute | solution.py:738
  610.1 53.4 %collective-permute-start.99 = (bf16[2,192,768]{2,1,0:T(8,128)(2,1)S(1)}, bf16[2,192,768]{2,1,0:T(8,128)(2,1)S(1)}, u32[]{:S(2)}, u32[]{:S(2)}) collective-permute-start(bf16[2,192,768]{2,1,0:T(8,128)(2,1)S(1)} %pad_maximum_fusion.5), channel_id=1, source_target_pairs={{0,3},{1,0},{2,1},{3,2},{4,7},{5,4},{6,5},{7,6},{8,11},{9,8},{10,9... | collective-permute-start | bytes 1769480 | tf_op jit(solution)/shard_map/ppermute | solution.py:738
  612.2 51.4 %collective-permute-start.97 = (bf16[2,192,768]{2,1,0:T(8,128)(2,1)S(1)}, bf16[2,192,768]{2,1,0:T(8,128)(2,1)S(1)}, u32[]{:S(2)}, u32[]{:S(2)}) collective-permute-start(bf16[2,192,768]{2,1,0:T(8,128)(2,1)S(1)} %pad_maximum_fusion.4), channel_id=1, source_target_pairs={{0,1},{1,2},{2,3},{3,0},{4,5},{5,6},{6,7},{7,4},{8,9},{9,10},{10,1... | collective-permute-start | bytes 1769480 | tf_op jit(solution)/shard_map/ppermute | solution.py:738
  613.8 61.2 %collective-permute-start.94 = (bf16[2,192,768]{2,1,0:T(8,128)(2,1)}, bf16[2,192,768]{2,1,0:T(8,128)(2,1)}, u32[]{:S(2)}, u32[]{:S(2)}) collective-permute-start(bf16[2,192,768]{2,1,0:T(8,128)(2,1)} %get-tuple-element.256), channel_id=1, source_target_pairs={{0,16},{16,0},{1,17},{17,1},{2,18},{18,2},{3,19},{19,3},{4,20},{20... | collective-permute-start | bytes 1769480 | tf_op jit(solution)/shard_map/ppermute | solution.py:58
  636.1 37.6 %collective-permute-start.72 = (bf16[3,192,192]{1,2,0:T(8,128)(2,1)S(1)}, bf16[3,192,192]{1,2,0:T(8,128)(2,1)S(1)}, u32[]{:S(2)}, u32[]{:S(2)}) collective-permute-start(bf16[3,192,192]{1,2,0:T(8,128)(2,1)S(1)} %pad_maximum_fusion.9), channel_id=1, source_target_pairs={{0,3},{1,0},{2,1},{3,2},{4,7},{5,4},{6,5},{7,6},{8,11},{9,8},{10,9... | collective-permute-start | bytes 663560 | tf_op jit(solution)/shard_map/ppermute | solution.py:738
  637.8 36.0 %collective-permute-start.70 = (bf16[3,192,192]{1,2,0:T(8,128)(2,1)S(1)}, bf16[3,192,192]{1,2,0:T(8,128)(2,1)S(1)}, u32[]{:S(2)}, u32[]{:S(2)}) collective-permute-start(bf16[3,192,192]{1,2,0:T(8,128)(2,1)S(1)} %pad_maximum_fusion.8), channel_id=1, source_target_pairs={{0,1},{1,2},{2,3},{3,0},{4,5},{5,6},{6,7},{7,4},{8,9},{9,10},{10,1... | collective-permute-start | bytes 663560 | tf_op jit(solution)/shard_map/ppermute | solution.py:738
  (173 other events, 1742.0 us)
where the time goes:
time: 690 us; the launch traced here: 681 us
  waiting for transfers between devices  219 us (32%)
  Pallas kernels  179 us (26%)
  starting transfers between devices  151 us (22%)
  local copies, waits for them, and re-layouts  49.4 us (7%)
  matrix products  49.4 us (7%)
  other arithmetic  30.8 us (4%)
    ppermute x82, waiting for transfers between devices, exchange(): return lax.ppermute(value, axis, [(i, i ^ mask) for i in range(count)])  114 us
    ppermute x24, waiting for transfers between devices, send(): lax.ppermute(x, 'dp', [(i, (i + step) % count) for i in range(count)])  105 us
    ppermute x82, starting transfers between devices, exchange(): return lax.ppermute(value, axis, [(i, i ^ mask) for i in range(count)])  78.7 us
    ppermute x24, starting transfers between devices, send(): lax.ppermute(x, 'dp', [(i, (i + step) % count) for i in range(count)])  71.9 us
    pallas_call x2, Pallas kernels, bwd_attention(): pl.pallas_call(functools.partial(bwd_attention_body, parts), out_shape=[s...  40.6 us
    pallas_call x2, Pallas kernels, fwd_experts(): pl.pallas_call(functools.partial(fwd_experts_body, parts), grid_spec=pltp...  35.3 us
    pallas_call x2, Pallas kernels, bwd_experts(): pl.pallas_call(functools.partial(bwd_experts_body, parts), grid_spec=pltp...  33 us
    pallas_call x2, Pallas kernels, fwd_attention(): pl.pallas_call(functools.partial(fwd_attention_body, parts, norm_inside),...  30.5 us
  transfers between devices with their start and end apart: 106, of which 38 were waited for; matrix products, arithmetic and copies ran while one was open for 16% of the time, Pallas kernels for 23%

commit v1 on v0

v1 whole, which is shorter than its diff:
```python
import functools

import jax
import jax.numpy as jnp
import numpy as np
from jax import lax
from jax.experimental import pallas as pl
from jax.experimental.pallas import tpu as pltpu
from jax.sharding import PartitionSpec as P

D = 768
HEAD_DIM = 64
BUCKETS = 32
EXPERTS = 4
CAP = 320
SEQ = 1024
PIECE = 256
PIECES = 2
SLOTS = EXPERTS * CAP

QB = PIECE
BAND = 128
WIDE = 2 * QB + BAND
DIAGS = 6

epsilon = 1e-06
bucket_edges = (12, 16, 23, 32, 46, 64, 91)
masked_score = -1000000000.0
far_bucket_behind = 15

BF = jnp.bfloat16
F32 = jnp.float32
MIB = 1024 * 1024


def dot(a, b, ca=1, cb=0):
    return lax.dot_general(a, b, (((ca,), (cb,)), ((), ())), preferred_element_type=F32)


def vm(count):
    return [pl.BlockSpec(memory_space=pltpu.VMEM)] * count


def smem():
    return pl.BlockSpec(memory_space=pltpu.SMEM)


def any_space(count):
    return [pl.BlockSpec(memory_space=pl.ANY)] * count


def limit(mib):
    return pltpu.CompilerParams(vmem_limit_bytes=mib * MIB)


def cost(flops, size):
    return pl.CostEstimate(flops=int(flops), bytes_accessed=int(size), transcendentals=0)


def shape(dims, kind):
    return jax.ShapeDtypeStruct(dims, kind)


def in_hbm(dims, kind):
    return pltpu.HBM(dims, kind)


def from_hbm(value):
    return pltpu.with_memory_space_constraint(value, pltpu.HBM)


def choose(select, own_ref, other_ref, to_ref):
    @pl.when(select == 0)
    def _():
        to_ref[...] = own_ref[...]

    @pl.when(select != 0)
    def _():
        to_ref[...] = other_ref[...]


def exchange(value, axis, mask):
    count = lax.axis_size(axis)
    return lax.ppermute(value, axis, [(i, i ^ mask) for i in range(count)])


def gather_parts(value):
    return [value] + [exchange(value, "tensor", k) for k in range(1, lax.axis_size("tensor"))]


def swap_parts(parts):
    return [parts[0]] + [exchange(p, "tensor", k) for k, p in enumerate(parts) if k]


def natural(t, k, size):
    return pl.ds(pl.multiple_of(jnp.bitwise_xor(t, k) * size, size), size)


def norm(vector, gain):
    return vector * lax.rsqrt(jnp.mean(vector * vector, axis=-1, keepdims=True) + epsilon) * gain


def total_of(value):
    return jnp.sum(jnp.sum(value, axis=0, keepdims=True), axis=1, keepdims=True)


def offset_buckets(offsets):
    distance = np.abs(offsets)
    far = np.full(offsets.shape, 8, np.int32)
    for edge_value in bucket_edges:
        far = far + (distance >= edge_value)
    return np.where(distance < 8, distance, far) + np.where(offsets > 0, 16, 0)


def diagonal_one_hot():
    lane = np.arange(2 * BAND)
    y = np.where(lane < BAND, lane, lane - 2 * BAND)
    offsets = BAND * (np.arange(DIAGS)[:, None] - 2) - y[None, :]
    hot = offset_buckets(offsets)[:, :, None] == np.arange(BUCKETS)
    hot = hot & (lane != BAND)[None, :, None]
    return hot.astype(np.float32)


def prepare_body(layer, place, own_gain, other_gain, own_table, other_table, hot, valid_ref, *refs):
    s = place[1]
    refs = refs[-5:] if layer == 0 else refs[-3:]
    gain_ref, tile_ref = refs[:2]
    heads = own_table.shape[0]
    own = s == layer
    gain_ref[...] = jnp.where(own, own_gain[...], other_gain[...])
    table = jnp.where(own, own_table[...], other_table[...])
    table = table - table[:, far_bucket_behind : far_bucket_behind + 1]
    by_offset = lax.dot_general(
        table,
        hot[...],
        (((1,), (0,)), ((), ())),
        precision=lax.Precision.HIGHEST,
        preferred_element_type=F32,
    )
    for h in range(heads):
        for d in range(DIAGS):
            row = by_offset[h : h + 1, d * 2 * BAND : (d + 1) * 2 * BAND]
            tile_ref[h * DIAGS + d] = pltpu.roll(
                jnp.broadcast_to(row, (BAND, 2 * BAND)), 0, 1, stride=1, stride_axis=0
            )[:, :BAND]
    if layer == 0:
        key_ref, own_ref, scratch = refs[2], refs[3], refs[4]
        rows = own_ref.shape[0]
        valid = jnp.where(s == 0, valid_ref[0:1, :], valid_ref[1:2, :]).astype(F32)
        column = jnp.broadcast_to(valid, (128, SEQ)).T[:, :1]
        scratch[...] = column
        key_ref[...] = jnp.where(column > 0, 0.0, masked_score)
        own_ref[...] = scratch[pl.ds(pl.multiple_of(place[0] * rows, rows), rows), :]


def prepare(layer, place, gains, tables, hot, valid, rows):
    outs = [shape((2, D), F32), shape((tables[0].shape[0] * DIAGS, BAND, BAND), F32)]
    if layer == 0:
        outs += [shape((SEQ, 1), F32), shape((rows, 1), F32)]
    return pl.pallas_call(
        functools.partial(prepare_body, layer),
        out_shape=outs,
        in_specs=[smem()] + vm(6),
        out_specs=vm(len(outs)),
        scratch_shapes=[pltpu.VMEM((SEQ, 1), F32)],
        compiler_params=limit(16),
        cost_estimate=cost(1e6, 1e5),
        name="prepare",
    )(place, *gains, *tables, hot, valid)


def targets_body(parts, place, own_route, other_route, own_router, other_router, *outs):
    row_refs, col_refs, router_refs, scratch = outs[:2], outs[2:4], outs[4:6], outs[6]
    t, s = place[0], place[1]
    rows = SEQ // parts
    before = lax.broadcasted_iota(jnp.int32, (SEQ, SEQ), 0)
    upto = (before <= lax.broadcasted_iota(jnp.int32, (SEQ, SEQ), 1)).astype(BF)
    expert = lax.broadcasted_iota(jnp.int32, (8, SEQ), 0)
    for layer in range(2):
        own = s == layer
        route = jnp.where(own, own_route[...], other_route[...])
        route = jnp.where(s == 0, route[0:1, :], route[1:2, :])
        hit = route == expert
        count = dot(hit.astype(BF), upto)
        slot = jnp.where(hit, count - 1.0 + (expert * CAP).astype(F32), 0.0)
        scratch[...] = jnp.sum(slot, axis=0, keepdims=True)
        for k in range(parts):
            row_refs[layer][:, k * rows : (k + 1) * rows] = scratch[:, natural(t, k, rows)].astype(
                jnp.int32
            )
        scratch[...] = row_refs[layer][...].astype(F32)
        turned = jnp.broadcast_to(scratch[...], (128, SEQ)).T
        col_refs[layer][...] = turned[:, :1].astype(jnp.int32)
        router_refs[layer][...] = jnp.zeros_like(router_refs[layer])
        router_refs[layer][:EXPERTS, :] = jnp.where(
            own, own_router[...].astype(F32), other_router[...].astype(F32)
        ).astype(BF)


def make_targets(place, routes, routers, parts):
    row, col = shape((1, SEQ), jnp.int32), shape((SEQ, 1), jnp.int32)
    router = shape((128, D), BF)
    return pl.pallas_call(
        functools.partial(targets_body, parts),
        out_shape=[row, row, col, col, router, router],
        in_specs=[smem()] + vm(4),
        out_specs=vm(6),
        scratch_shapes=[pltpu.VMEM((1, SEQ), F32)],
        compiler_params=limit(16),
        cost_estimate=cost(1e6, 1e5),
        name="make_targets",
    )(place, *routes, *routers)


def near_bias(tiles_ref, h, skip, width):
    first, last = skip // BAND, (skip + width) // BAND
    columns = [
        jnp.concatenate([tiles_ref[h * DIAGS + i - j + 1] for i in range(first, last)], axis=0)
        for j in range(QB // BAND)
    ]
    return jnp.concatenate(columns, axis=1)


def block_range(j):
    last = min(SEQ, QB * (j + 2))
    left = max(0, QB * j - BAND)
    return left, last, left - (QB * j - BAND)


def fill_mask(mask_ref, valid_ref, s0, s1, j):
    left, last, _ = block_range(j)
    width = last - left
    key = left + lax.broadcasted_iota(jnp.int32, (width, 1), 0)
    query = QB * j + lax.broadcasted_iota(jnp.int32, (1, QB), 1)

    def label(position, outside):
        second = jnp.where((position >= s1) & (position < s1 + PIECE), 1, outside)
        return jnp.where((position >= s0) & (position < s0 + PIECE), 0, second)

    allowed = (key <= query) | (label(key, -1) == label(query, -2))
    mask_ref[:width, :] = jnp.where(allowed, valid_ref[left:last, :], masked_score)


def fwd_attention_body(parts, norm_inside, *refs):
    place, starts, valid_col, gain, w_own, w_other, tiles_ref = refs[:7]
    x_refs = refs[7 : 7 + parts]
    xn_out, qkv_out, turned_out, lse_ref = refs[7 + parts : 11 + parts]
    out_refs = refs[11 + parts : 11 + 2 * parts]
    w_ref, xn_ref, qkv_ref, turned_ref, vt_ref, att_ref, mask_ref, valid_ref, sems = refs[
        11 + 2 * parts :
    ]
    t, s = place[0], place[1]
    s0, s1 = starts[s, 0], starts[s, 1]
    rows = SEQ // parts
    heads = qkv_ref.shape[1]
    wide = heads * HEAD_DIM

    choose(place[2], w_own, w_other, w_ref)
    valid_ref[...] = jnp.broadcast_to(valid_col[...], (SEQ, QB))
    for k in range(parts):
        where = natural(t, k, rows)
        x = x_refs[k][...]
        if norm_inside:
            x = norm(x.astype(F32), gain[0:1, :]).astype(BF)
        xn_ref[where, :] = x
        projected = dot(x, w_ref[...], 1, 1)
        for i in range(3):
            product = projected[:, i * wide : (i + 1) * wide]
            if i == 0:
                product = product * HEAD_DIM**-0.5
            turned = product.T.astype(BF)
            if i < 2:
                turned_ref[i, :, where] = turned
            else:
                vt_ref[:, where] = turned
            product = product.astype(BF)
            for h in range(heads):
                qkv_ref[i, h, where, :] = product[:, h * HEAD_DIM : (h + 1) * HEAD_DIM]

    copies = [
        pltpu.make_async_copy(a, b, sems.at[i])
        for i, (a, b) in enumerate(
            ((xn_ref, xn_out), (qkv_ref, qkv_out), (turned_ref, turned_out))
        )
    ]
    for copy in copies:
        copy.start()

    for j in range(SEQ // QB):
        left, last, skip = block_range(j)
        width = last - left
        columns = slice(j * QB, (j + 1) * QB)
        fill_mask(mask_ref, valid_ref, s0, s1, j)

        def one_head(h, carry):
            lanes = pl.ds(pl.multiple_of(h * HEAD_DIM, HEAD_DIM), HEAD_DIM)
            scores = dot(qkv_ref[1, h, :last, :], turned_ref[0, lanes, columns])
            near = scores[left:] + near_bias(tiles_ref, h, skip, width) + mask_ref[:width, :]
            highest = jnp.max(near, axis=0, keepdims=True)
            if left:
                far = scores[:left] + valid_ref[:left, :]
                highest = jnp.maximum(highest, jnp.max(far, axis=0, keepdims=True))
            near = jnp.exp(near - highest)
            total = jnp.sum(near, axis=0, keepdims=True)
            out = dot(vt_ref[lanes, left:last], near.astype(BF))
            if left:
                far = jnp.exp(far - highest)
                total = total + jnp.sum(far, axis=0, keepdims=True)
                out = out + dot(vt_ref[lanes, :left], far.astype(BF))
            lse_ref[h, :, columns] = highest + jnp.log(total)
            att_ref[lanes, columns] = (out * (1.0 / total)).astype(BF)
            return carry

        lax.fori_loop(0, heads, one_head, 0)

    for k in range(parts):
        out_refs[k][...] = att_ref[:, natural(t, k, rows)]
    for copy in copies:
        copy.wait()


def fwd_attention(place, starts, valid_col, gain, w_pair, tiles, x_parts, norm_inside):
    parts = len(x_parts)
    rows = SEQ // parts
    wide = w_pair[0].shape[0] // 3
    heads = wide // HEAD_DIM
    kept = [
        shape((SEQ, D), BF),
        shape((3, heads, SEQ, HEAD_DIM), BF),
        shape((2, wide, SEQ), BF),
    ]
    outs = pl.pallas_call(
        functools.partial(fwd_attention_body, parts, norm_inside),
        out_shape=[in_hbm(a.shape, a.dtype) for a in kept]
        + [shape((heads, 1, SEQ), F32)] + [shape((wide, rows), BF)] * parts,
        in_specs=[smem()] * 2 + vm(5 + parts),
        out_specs=any_space(3) + vm(1 + parts),
        scratch_shapes=[pltpu.VMEM((3 * wide, D), BF)]
        + [pltpu.VMEM(a.shape, a.dtype) for a in kept]
        + [
            pltpu.VMEM((wide, SEQ), BF),
            pltpu.VMEM((wide, SEQ), BF),
            pltpu.VMEM((WIDE, QB), F32),
            pltpu.VMEM((SEQ, QB), F32),
            pltpu.SemaphoreType.DMA((3,)),
        ],
        compiler_params=limit(32),
        cost_estimate=cost(9e9, 1e7),
        name="fwd_attention",
    )(place, starts, valid_col, gain, *w_pair, tiles, *x_parts)
    return outs[:4], list(outs[4:])


def bwd_attention_body(parts, *refs):
    place, starts, valid_col, gain, w_own, w_other, tiles_ref, xn_ref = refs[:8]
    qkv_ref, turned_ref, lse_ref = refs[8:11]
    d_refs = refs[11 : 11 + parts]
    refs = refs[11 + parts :]
    proj_ref, sum_ref, far_ref, gain_ref = refs[:4]
    out_refs = refs[4 : 4 + parts]
    w_ref, d_ref, dt_ref, dq_ref, dk_ref, dv_ref, mask_ref, valid_ref = refs[4 + parts :]
    t, s = place[0], place[1]
    s0, s1 = starts[s, 0], starts[s, 1]
    rows = SEQ // parts
    heads = qkv_ref.shape[1]

    choose(place[2], w_own, w_other, w_ref)
    valid_ref[...] = jnp.broadcast_to(valid_col[...], (SEQ, QB))
    for k in range(parts):
        where = natural(t, k, rows)
        block = d_refs[k][...]
        dt_ref[:, where] = block.astype(F32).T.astype(BF)
        for h in range(heads):
            d_ref[h, where, :] = block[:, h * HEAD_DIM : (h + 1) * HEAD_DIM]
    dk_ref[...] = jnp.zeros_like(dk_ref)
    dv_ref[...] = jnp.zeros_like(dv_ref)
    sum_ref[...] = jnp.zeros_like(sum_ref)
    far_ref[...] = jnp.zeros_like(far_ref)

    for j in range(SEQ // QB):
        left, last, skip = block_range(j)
        width = last - left
        columns = slice(j * QB, (j + 1) * QB)
        fill_mask(mask_ref, valid_ref, s0, s1, j)

        def one_head(h, carry):
            lanes = pl.ds(pl.multiple_of(h * HEAD_DIM, HEAD_DIM), HEAD_DIM)
            q_block = qkv_ref[0, h, columns, :]
            d_block = d_ref[h, columns, :]
            lse = lse_ref[h, :, columns]
            scores = dot(qkv_ref[1, h, :last, :], turned_ref[0, lanes, columns])
            slopes = dot(qkv_ref[2, h, :last, :], dt_ref[lanes, columns])
            near = scores[left:] + near_bias(tiles_ref, h, skip, width) + mask_ref[:width, :]
            near = jnp.exp(near - lse)
            near_slope = near * slopes[left:]
            row_dot = jnp.sum(near_slope, axis=0, keepdims=True)
            if left:
                far = jnp.exp(scores[:left] + valid_ref[:left, :] - lse)
                far_slope = far * slopes[:left]
                row_dot = row_dot + jnp.sum(far_slope, axis=0, keepdims=True)
            near_slope = near_slope - near * row_dot
            for i in range(width // BAND):
                for c in range(QB // BAND):
                    sum_ref[h * DIAGS + skip // BAND + i - c + 1] += near_slope[
                        i * BAND : (i + 1) * BAND, c * BAND : (c + 1) * BAND
                    ]
            near_slope = near_slope.astype(BF)
            dk_ref[h, left:last, :] += dot(near_slope, q_block)
            dv_ref[h, left:last, :] += dot(near.astype(BF), d_block)
            dq = dot(turned_ref[1, lanes, left:last], near_slope)
            if left:
                far_slope = far_slope - far * row_dot
                far_ref[h] += jnp.sum(far_slope.reshape(left // 8, 8, QB), axis=0)
                far_slope = far_slope.astype(BF)
                dk_ref[h, :left, :] += dot(far_slope, q_block)
                dv_ref[h, :left, :] += dot(far.astype(BF), d_block)
                dq = dq + dot(turned_ref[1, lanes, :left], far_slope)
            dq_ref[lanes, columns] = dq * HEAD_DIM**-0.5
            return carry

        lax.fori_loop(0, heads, one_head, 0)

    for first in range(0, SEQ, rows):
        where = slice(first, first + rows)
        blocks = [dq_ref[:, where].T.astype(BF)]
        for source in (dk_ref, dv_ref):
            blocks += [source[h, where, :].astype(BF) for h in range(heads)]
        proj_ref[where, :] = jnp.concatenate(blocks, axis=1)
    gain_sum = jnp.zeros((1, D), F32)
    for k in range(parts):
        where = natural(t, k, rows)
        total = dot(proj_ref[where, :], w_ref[...])
        out_refs[k][...] = total.astype(BF)
        gain_sum = gain_sum + jnp.sum(total * xn_ref[where, :].astype(F32), axis=0, keepdims=True)
    gain_ref[...] = gain_sum / gain[0:1, :]


def bwd_attention(place, starts, valid_col, gain, w_pair, tiles, saved, d_parts):
    parts = len(d_parts)
    rows = SEQ // parts
    wide = w_pair[0].shape[0] // 3
    heads = wide // HEAD_DIM
    outs = pl.pallas_call(
        functools.partial(bwd_attention_body, parts),
        out_shape=[
            shape((SEQ, 3 * wide), BF),
            shape((heads * DIAGS, BAND, BAND), F32),
            shape((heads, 8, QB), F32),
            shape((1, D), F32),
        ]
        + [shape((rows, D), BF)] * parts,
        in_specs=[smem()] * 2 + vm(9 + parts),
        out_specs=vm(4 + parts),
        scratch_shapes=[
            pltpu.VMEM((3 * wide, D), BF),
            pltpu.VMEM((heads, SEQ, HEAD_DIM), BF),
            pltpu.VMEM((wide, SEQ), BF),
            pltpu.VMEM((wide, SEQ), F32),
            pltpu.VMEM((heads, SEQ, HEAD_DIM), F32),
            pltpu.VMEM((heads, SEQ, HEAD_DIM), F32),
            pltpu.VMEM((WIDE, QB), F32),
            pltpu.VMEM((SEQ, QB), F32),
        ],
        compiler_params=limit(36),
        cost_estimate=cost(1.8e10, 1e7),
        name="bwd_attention",
    )(place, starts, valid_col, gain, *w_pair, tiles, *saved, *d_parts)
    return outs[:4], list(outs[4:])


def small_sums_body(paired, place, tiles_ref, far_ref, hot, gain_in, gain_mid, router, *refs):
    stats, refs = refs[:2], refs[2:]
    heads = far_ref.shape[0]
    row = lax.broadcasted_iota(jnp.int32, (BAND, BAND), 0)
    column = lax.broadcasted_iota(jnp.int32, (BAND, BAND), 1)
    flip = (row + column == BAND - 1).astype(F32)
    out = refs[-1]
    out[...] = jnp.zeros_like(out)
    out[0:1, :] = gain_in[...]
    out[1:2, :] = gain_mid[...]
    out[2 : 2 + EXPERTS, :] = router[:EXPERTS, :]
    out[6:7, :128] = stats[0][...] + stats[1][...]
    by_offset = []
    for h in range(heads):
        sums = []
        for d in range(DIAGS):
            tile = lax.dot_general(
                flip,
                tiles_ref[h * DIAGS + d],
                (((1,), (0,)), ((), ())),
                precision=lax.Precision.HIGHEST,
                preferred_element_type=F32,
            )
            tile = jnp.concatenate([tile, jnp.zeros_like(tile)], axis=1)
            tile = pltpu.roll(tile, BAND + 1, 1, stride=1, stride_axis=0)
            sums.append(jnp.sum(tile, axis=0, keepdims=True))
        by_offset.append(jnp.concatenate(sums, axis=1))
    table = lax.dot_general(
        jnp.concatenate(by_offset, axis=0),
        hot[...],
        (((1,), (1,)), ((), ())),
        precision=lax.Precision.HIGHEST,
        preferred_element_type=F32,
    )
    bucket = lax.broadcasted_iota(jnp.int32, (1, BUCKETS), 1)
    for h in range(heads):
        behind = jnp.where(bucket == far_bucket_behind, total_of(far_ref[h]), 0.0)
        out[8 + h : 9 + h, :BUCKETS] = table[h : h + 1, :] + behind
    if paired:
        other, keep, sent = refs[:3]
        first = place[1] == 0
        keep[...] = jnp.where(first, out[...], other[...])
        sent[...] = jnp.where(first, other[...], out[...])


def small_sums(place, tiles, far, hot, gain_in, gain_mid, router, stats, other):
    paired = other is not None
    array = shape((16, D), F32)
    outs = pl.pallas_call(
        functools.partial(small_sums_body, paired),
        out_shape=[array] * (2 if paired else 1),
        in_specs=[smem()] + vm(8 + paired),
        out_specs=vm(2 if paired else 1),
        scratch_shapes=[pltpu.VMEM((16, D), F32)] if paired else [],
        compiler_params=limit(16),
        cost_estimate=cost(1e6, 1e5),
        name="small_sums",
    )(place, tiles, far, hot, gain_in, gain_mid, router, *stats, *([other] if paired else []))
    return outs if paired else outs[0]


def combine(parts, rows, target_col, slots_ref, out_refs):
    slot = lax.broadcasted_iota(jnp.int32, (rows, SLOTS), 1)
    for k in list(range(1, parts)) + [0]:
        hot = (target_col[k * rows : (k + 1) * rows, :] == slot).astype(BF)
        out_refs[k][...] = dot(hot, slots_ref[...]).astype(BF)


def dispatch(e, target_row, tokens_ref):
    slot = e * CAP + lax.broadcasted_iota(jnp.int32, (CAP, SEQ), 0)
    return dot((target_row[...] == slot).astype(BF), tokens_ref[...]).astype(BF)


def fwd_experts_body(parts, *refs):
    sel, target_row, target_col, router, up_own, up_other, down_own, down_other = refs[:8]
    x_refs = refs[8 : 8 + parts]
    in_ref, act_ref, slope_ref, gate_ref, probs_ref = refs[8 + parts : 13 + parts]
    out_refs = refs[13 + parts : 13 + 2 * parts]
    x_ref, slots_ref, up_ref, down_ref = refs[13 + 2 * parts :]
    rows = SEQ // parts
    e = pl.program_id(0)

    @pl.when(e == 0)
    def _():
        lane = lax.broadcasted_iota(jnp.int32, (rows, 128), 1)
        for k in range(parts):
            where = slice(k * rows, (k + 1) * rows)
            x = x_refs[k][...]
            x_ref[where, :] = x
            logits = jnp.where(lane < EXPERTS, dot(x, router[...], 1, 1), -1e30)
            probs = jnp.exp(logits - jnp.max(logits, axis=-1, keepdims=True))
            probs = probs / jnp.sum(probs, axis=-1, keepdims=True)
            target = target_col[where, :]
            hit = (target >= lane * CAP) & (target < lane * CAP + CAP)
            gate_ref[where, :] = jnp.sum(jnp.where(hit, probs, 0.0), axis=-1, keepdims=True)
            if k == 0:
                probs_ref[...] = probs

    choose(sel[0], up_own.at[0], up_other.at[0], up_ref)
    choose(sel[0], down_own.at[0], down_other.at[0], down_ref)
    expert_in = dispatch(e, target_row, x_ref)
    in_ref[0] = expert_in
    up = dot(expert_in, up_ref[...])
    inner = np.sqrt(2 / np.pi).astype(np.float32)
    square = up * up
    bend = jnp.tanh(inner * (up * (1.0 + 0.044715 * square)))
    half = 0.5 * (1.0 + bend)
    act = (up * half).astype(BF)
    act_ref[0] = act
    slope_ref[0] = half + 0.5 * up * (1.0 - bend * bend) * (
        inner * (1.0 + 3 * 0.044715 * square)
    )
    slots_ref[pl.ds(pl.multiple_of(e * CAP, CAP), CAP), :] = dot(act, down_ref[...]).astype(BF)

    @pl.when(e == EXPERTS - 1)
    def _():
        combine(parts, rows, target_col, slots_ref, out_refs)


def expert_specs(block):
    own = pl.BlockSpec(block, lambda e, sel: (e * (1 - sel[0]), 0, 0))
    other = pl.BlockSpec(block, lambda e, sel: (e * sel[0], 0, 0))
    return [own, other]


def whole(dims):
    return pl.BlockSpec(dims, lambda e, sel: (0,) * len(dims))


def fwd_experts(select, target_row, target_col, router, up_pair, down_pair, x_parts):
    parts = len(x_parts)
    rows = SEQ // parts
    hidden = up_pair[0].shape[2]
    each = pl.BlockSpec((1, CAP, D), lambda e, sel: (e, 0, 0))
    each_hidden = pl.BlockSpec((1, CAP, hidden), lambda e, sel: (e, 0, 0))
    outs = pl.pallas_call(
        functools.partial(fwd_experts_body, parts),
        grid_spec=pltpu.PrefetchScalarGridSpec(
            num_scalar_prefetch=1,
            grid=(EXPERTS,),
            in_specs=[whole((1, SEQ)), whole((SEQ, 1)), whole((128, D))]
            + expert_specs((1, D, hidden))
            + expert_specs((1, hidden, D))
            + [whole((rows, D))] * parts,
            out_specs=[each, each_hidden, each_hidden, whole((SEQ, 1)), whole((rows, 128))]
            + [whole((rows, D))] * parts,
            scratch_shapes=[
                pltpu.VMEM((SEQ, D), BF),
                pltpu.VMEM((SLOTS, D), BF),
                pltpu.VMEM((D, hidden), BF),
                pltpu.VMEM((hidden, D), BF),
            ],
        ),
        out_shape=[
            in_hbm((EXPERTS, CAP, D), BF),
            in_hbm((EXPERTS, CAP, hidden), BF),
            in_hbm((EXPERTS, CAP, hidden), F32),
            shape((SEQ, 1), F32),
            shape((rows, 128), F32),
        ]
        + [shape((rows, D), BF)] * parts,
        compiler_params=limit(44),
        cost_estimate=cost(1.2e10, 3e7),
        name="fwd_experts",
    )(
        select,
        target_row,
        target_col,
        router,
        *[from_hbm(a) for a in (*up_pair, *down_pair)],
        *x_parts,
    )
    return outs[:5], list(outs[5:])


def bwd_experts_body(parts, *refs):
    sel, target_row, target_col, gate, slope_ref, up_own, up_other, down_own, down_other = refs[:9]
    g_refs = refs[9 : 9 + parts]
    refs = refs[9 + parts :]
    dout_ref, dup_ref = refs[:2]
    out_refs = refs[2 : 2 + parts]
    g_ref, slots_ref, up_ref, down_ref = refs[2 + parts :]
    rows = SEQ // parts
    e = pl.program_id(0)

    @pl.when(e == 0)
    def _():
        for k in range(parts):
            where = slice(k * rows, (k + 1) * rows)
            g_ref[where, :] = (gate[where, :] * g_refs[k][...].astype(F32)).astype(BF)

    choose(sel[0], up_own.at[0], up_other.at[0], up_ref)
    choose(sel[0], down_own.at[0], down_other.at[0], down_ref)
    d_out = dispatch(e, target_row, g_ref)
    dout_ref[0] = d_out
    d_up = (slope_ref[0] * dot(d_out, down_ref[...], 1, 1)).astype(BF)
    dup_ref[0] = d_up
    slots_ref[pl.ds(pl.multiple_of(e * CAP, CAP), CAP), :] = dot(d_up, up_ref[...], 1, 1).astype(
        BF
    )

    @pl.when(e == EXPERTS - 1)
    def _():
        combine(parts, rows, target_col, slots_ref, out_refs)


def bwd_experts(select, target_row, target_col, gate, slope, up_pair, down_pair, g_parts):
    parts = len(g_parts)
    rows = SEQ // parts
    hidden = up_pair[0].shape[2]
    each = pl.BlockSpec((1, CAP, D), lambda e, sel: (e, 0, 0))
    each_hidden = pl.BlockSpec((1, CAP, hidden), lambda e, sel: (e, 0, 0))
    outs = pl.pallas_call(
        functools.partial(bwd_experts_body, parts),
        grid_spec=pltpu.PrefetchScalarGridSpec(
            num_scalar_prefetch=1,
            grid=(EXPERTS,),
            in_specs=[whole((1, SEQ)), whole((SEQ, 1)), whole((SEQ, 1)), each_hidden]
            + expert_specs((1, D, hidden))
            + expert_specs((1, hidden, D))
            + [whole((rows, D))] * parts,
            out_specs=[each, each_hidden] + [whole((rows, D))] * parts,
            scratch_shapes=[
                pltpu.VMEM((SEQ, D), BF),
                pltpu.VMEM((SLOTS, D), BF),
                pltpu.VMEM((D, hidden), BF),
                pltpu.VMEM((hidden, D), BF),
            ],
        ),
        out_shape=[in_hbm((EXPERTS, CAP, D), BF), in_hbm((EXPERTS, CAP, hidden), BF)]
        + [shape((rows, D), BF)] * parts,
        compiler_params=limit(44),
        cost_estimate=cost(1.2e10, 3e7),
        name="bwd_experts",
    )(
        select,
        target_row,
        target_col,
        gate,
        *[from_hbm(a) for a in (slope, *up_pair, *down_pair)],
        *g_parts,
    )
    return outs[:2], list(outs[2:])


def norm_back(vector, gain, grad):
    scale = lax.rsqrt(jnp.mean(vector * vector, axis=-1, keepdims=True) + epsilon)
    unit = vector * scale
    scaled = grad * gain
    inner = jnp.mean(unit * scaled, axis=-1, keepdims=True)
    return scale * (scaled - unit * inner), grad * unit


def after_attention_body(parts, *refs):
    h_ref, gain, valid = refs[:3]
    p_refs, w_refs = refs[3 : 3 + parts], refs[3 + parts : 3 + 2 * parts]
    mid_ref, xn_ref, stat_ref = refs[3 + 2 * parts :]
    branch = dot(p_refs[0][...], w_refs[0][...], 0, 0)
    for k in range(1, parts):
        branch = branch + dot(p_refs[k][...], w_refs[k][...], 0, 0)
    h = h_ref[...].astype(F32)
    mid = h + branch
    mid_ref[...] = mid
    xn_ref[...] = norm(mid, gain[1:2, :]).astype(BF)
    weight = valid[...]
    lane = lax.broadcasted_iota(jnp.int32, (1, 128), 1)
    sums = jnp.where(lane == 0, total_of(weight * h * h), 0.0)
    sums = jnp.where(lane == 1, total_of(weight * branch * branch), sums)
    stat_ref[...] = jnp.where(lane == 3, total_of(weight), sums)


def after_attention(h, gain, valid, pieces, w_parts):
    parts = len(pieces)
    rows = h.shape[0]
    return pl.pallas_call(
        functools.partial(after_attention_body, parts),
        out_shape=[shape((rows, D), F32), shape((rows, D), BF), shape((1, 128), F32)],
        in_specs=vm(3 + 2 * parts),
        out_specs=vm(3),
        compiler_params=limit(24),
        cost_estimate=cost(2e9, 4e6),
        name="after_attention",
    )(h, gain, valid, *pieces, *w_parts)


def after_experts_body(parts, *refs):
    mid_ref, gate, gain, valid = refs[:4]
    y_refs = refs[4 : 4 + parts]
    comb_ref, out_ref, xn_ref, stat_ref = refs[4 + parts :]
    total = y_refs[0][...].astype(F32)
    for k in range(1, parts):
        total = total + y_refs[k][...].astype(F32)
    combined = total.astype(BF)
    comb_ref[...] = combined
    branch = gate[: mid_ref.shape[0], :] * combined.astype(F32)
    out = (mid_ref[...] + branch).astype(BF)
    out_ref[...] = out
    xn_ref[...] = norm(out.astype(F32), gain[0:1, :]).astype(BF)
    lane = lax.broadcasted_iota(jnp.int32, (1, 128), 1)
    stat_ref[...] = jnp.where(lane == 2, total_of(valid[...] * branch * branch), 0.0)


def after_experts(mid, gate, gain, valid, y_parts):
    parts = len(y_parts)
    rows = mid.shape[0]
    return pl.pallas_call(
        functools.partial(after_experts_body, parts),
        out_shape=[shape((rows, D), BF)] * 3 + [shape((1, 128), F32)],
        in_specs=vm(4 + parts),
        out_specs=vm(4),
        compiler_params=limit(24),
        cost_estimate=cost(1e8, 4e6),
        name="after_experts",
    )(mid, gate, gain, valid, *y_parts)


def middle_back_body(parts, *refs):
    g_ref, comb_ref, probs_ref, target_col, router, mid_ref, gain, xn_ref = refs[:8]
    y_refs, w_refs = refs[8 : 8 + parts], refs[8 + parts : 8 + 2 * parts]
    refs = refs[8 + 2 * parts :]
    dmid_ref, da_ref, gain_ref, router_ref = refs[:4]
    out_refs = refs[4:]
    rows = g_ref.shape[0]
    g = g_ref[...].astype(F32)
    total = y_refs[0][...].astype(F32)
    for k in range(1, parts):
        total = total + y_refs[k][...].astype(F32)
    d_in = total.astype(BF).astype(F32)
    d_gate = jnp.sum(g * comb_ref[...].astype(F32), axis=-1, keepdims=True)
    lane = lax.broadcasted_iota(jnp.int32, (rows, 128), 1)
    target = target_col[:rows, :]
    hit = (target >= lane * CAP) & (target < lane * CAP + CAP)
    probs = probs_ref[...]
    chosen = jnp.where(hit, d_gate, 0.0)
    inner = jnp.sum(probs * chosen, axis=-1, keepdims=True)
    d_logits = (probs * (chosen - inner)).astype(BF)
    router_ref[...] = dot(d_logits, xn_ref[...], 0, 0)[:8]
    d_xn = d_in + dot(d_logits, router[...])
    d_norm, d_gain = norm_back(mid_ref[...], gain[1:2, :], d_xn)
    gain_ref[...] = jnp.sum(d_gain, axis=0, keepdims=True)
    d_mid = g + d_norm
    dmid_ref[...] = d_mid
    d_a = d_mid.astype(BF)
    da_ref[...] = d_a
    for k in list(range(1, parts)) + [0]:
        out_refs[k][...] = dot(d_a, w_refs[k][...], 1, 1).astype(BF)


def middle_back(g, combined, probs, target_col, router, mid, gain, xn, y_parts, w_parts):
    parts = len(y_parts)
    rows = g.shape[0]
    wide = w_parts[0].shape[0]
    outs = pl.pallas_call(
        functools.partial(middle_back_body, parts),
        out_shape=[shape((rows, D), F32), shape((rows, D), BF), shape((1, D), F32)]
        + [shape((8, D), F32)]
        + [shape((rows, wide), BF)] * parts,
        in_specs=vm(8 + 2 * parts),
        out_specs=vm(4 + parts),
        compiler_params=limit(24),
        cost_estimate=cost(2e9, 6e6),
        name="middle_back",
    )(g, combined, probs, target_col, router, mid, gain, xn, *y_parts, *w_parts)
    return outs[:4], list(outs[4:])


def input_back_body(parts, *refs):
    dmid_ref, h_ref, gain = refs[:3]
    y_refs = refs[3 : 3 + parts]
    wide_ref, low_ref = refs[3 + parts :]
    total = y_refs[0][...].astype(F32)
    for k in range(1, parts):
        total = total + y_refs[k][...].astype(F32)
    d_h = dmid_ref[...] + norm_back(h_ref[...].astype(F32), gain[0:1, :], total)[0]
    wide_ref[...] = d_h
    low_ref[...] = d_h.astype(BF)


def input_back(d_mid, h, gain, y_parts):
    parts = len(y_parts)
    rows = h.shape[0]
    return pl.pallas_call(
        functools.partial(input_back_body, parts),
        out_shape=[shape((rows, D), F32), shape((rows, D), BF)],
        in_specs=vm(3 + parts),
        out_specs=vm(2),
        compiler_params=limit(24),
        cost_estimate=cost(1e8, 4e6),
        name="input_back",
    )(d_mid, h, gain, *y_parts)


def expert_grads_body(order, act, d_out, expert_in, d_up, send_ref, keep_ref):
    del order
    for place, out in enumerate((send_ref, keep_ref)):

        @pl.when(pl.program_id(0) // (EXPERTS // 2) == place)
        def _():
            out[0, 0] = dot(act[0], d_out[0], 0, 0).astype(BF)
            out[1, 0] = dot(expert_in[0], d_up[0], 0, 0).astype(BF)


def expert_grads(order, act, d_out, expert_in, d_up):
    half = EXPERTS // 2
    hidden = act.shape[2]
    values = (act, d_out, expert_in, d_up)
    block = (2, 1, hidden, D)
    outs = pl.pallas_call(
        expert_grads_body,
        grid_spec=pltpu.PrefetchScalarGridSpec(
            num_scalar_prefetch=1,
            grid=(EXPERTS,),
            in_specs=[
                pl.BlockSpec((1,) + a.shape[1:], lambda e, order: (order[e], 0, 0)) for a in values
            ],
            out_specs=[
                pl.BlockSpec(block, lambda e, order: (0, jnp.minimum(e, half - 1), 0, 0)),
                pl.BlockSpec(block, lambda e, order: (0, jnp.maximum(e - half, 0), 0, 0)),
            ],
        ),
        out_shape=[in_hbm((2, half, hidden, D), BF)] * 2,
        compiler_params=limit(28),
        cost_estimate=cost(1e6, 1e5),
        name="expert_grads",
    )(order, *[from_hbm(a) for a in values])
    return [a.reshape(2 * half, hidden, D) for a in outs]


def out_grads_body(parts, *refs):
    pieces, d_a, outs = refs[:parts], refs[parts], refs[parts + 1 :]
    for k in list(range(1, parts)) + [0]:
        outs[k][...] = dot(pieces[k][...], d_a[...]).astype(BF)


def out_grads(pieces, d_a):
    parts = len(pieces)
    wide = pieces[0].shape[0]
    return pl.pallas_call(
        functools.partial(out_grads_body, parts),
        out_shape=[shape((wide, D), BF)] * parts,
        in_specs=vm(parts + 1),
        out_specs=vm(parts),
        compiler_params=limit(16),
        cost_estimate=cost(1e6, 1e5),
        name="out_grads",
    )(*pieces, d_a)


def attention_grads_body(parts, chunks, paired, place, xn_ref, proj_ref, *refs):
    terms, refs = refs[:parts], refs[parts:]
    out = refs[-1]
    wide = terms[0].shape[0]
    rows, taken = D // chunks, wide // chunks
    out[0, :, : 3 * wide] = dot(xn_ref[...], proj_ref[...], 0, 0).astype(out.dtype)
    total = terms[0][...].astype(F32)
    for k in range(1, parts):
        total = total + terms[k][...].astype(F32)
    for c in range(chunks):
        for b in range(D // wide):
            out[0, c * rows + b * taken : c * rows + (b + 1) * taken, 3 * wide :] = total[
                c * taken : (c + 1) * taken, b * wide : (b + 1) * wide
            ].astype(out.dtype)
    if paired:
        other, keep, sent = refs[:3]
        first = place[1] == 0
        keep[...] = jnp.where(first, out[...].astype(F32), other[...].astype(F32)).astype(BF)
        sent[...] = jnp.where(first, other[...].astype(F32), out[...].astype(F32)).astype(BF)


def attention_grads(place, xn, proj, terms, other):
    parts = len(terms)
    paired = other is not None
    array = shape((1, D, D), BF)
    outs = pl.pallas_call(
        functools.partial(attention_grads_body, parts, lax.axis_size("dp"), paired),
        out_shape=[array] * (2 if paired else 1),
        in_specs=[smem()] + vm(2 + parts + paired),
        out_specs=vm(2 if paired else 1),
        scratch_shapes=[pltpu.VMEM((1, D, D), F32)] if paired else [],
        compiler_params=limit(24),
        cost_estimate=cost(1e6, 1e5),
        name="attention_grads",
    )(place, xn, proj, *terms, *([other] if paired else []))
    return outs if paired else outs[0]


def attention_results(value, wide):
    rows = value.shape[0]
    taken = rows // (D // wide)
    return (
        jnp.stack([value[:, i * wide : (i + 1) * wide] for i in range(3)]),
        jnp.concatenate(
            [value[b * taken : (b + 1) * taken, 3 * wide :] for b in range(D // wide)], axis=1
        ),
    )


def shift(value, step):
    count = lax.axis_size("dp")
    return lax.ppermute(value, "dp", [(i, (i + step) % count) for i in range(count)])


def ring_call(body, name, at, groups, inputs, outputs):
    step = 2 if groups % 2 == 0 else 1
    in_specs = []
    for a, lead, entry in inputs:
        size = a.shape[1] if entry is None else a.shape[1] // 4
        in_specs.append(
            pl.BlockSpec(
                (step, size, a.shape[2]),
                lambda i, at, lead=lead, entry=entry: (
                    i + lead // step,
                    0 if entry is None else at[entry],
                    0,
                ),
            )
        )
    columns = inputs[0][0].shape[2]
    return pl.pallas_call(
        body,
        grid_spec=pltpu.PrefetchScalarGridSpec(
            num_scalar_prefetch=1,
            grid=(groups // step,),
            in_specs=in_specs,
            out_specs=[
                pl.BlockSpec((step, rows, columns), lambda i, at: (i, 0, 0)) for rows, _ in outputs
            ],
        ),
        out_shape=[shape((groups, rows, columns), kind) for rows, kind in outputs],
        compiler_params=limit(24),
        cost_estimate=cost(1e6, 1e5),
        name=name,
    )(at, *[a for a, _, _ in inputs])


def added(*refs):
    return functools.reduce(jnp.add, [r[...].astype(F32) for r in refs])


def ring_first_body(at, a, b, low, high):
    total = added(a, b).astype(BF)
    half = low.shape[1]
    low[...] = total[:, :half]
    high[...] = total[:, half:]


def ring_first(at, terms):
    if lax.axis_size("dp") != 4:
        return []
    size = terms[0].shape[1] // 4
    inputs = [(a, 0, 0) for a in terms]
    return ring_call(
        ring_first_body, "ring_first", at, terms[0].shape[0], inputs, [(size // 2, BF)] * 2
    )


def ring_second_body(at, a, b, c, d, ahead, behind, low, high):
    half = ahead.shape[1]
    total = added(a, b)
    low[:, :half] = (total[:, :half] + ahead[...].astype(F32)).astype(BF)
    low[:, half:] = total[:, half:].astype(BF)
    total = added(c, d)
    high[:, :half] = total[:, :half].astype(BF)
    high[:, half:] = (total[:, half:] + behind[...].astype(F32)).astype(BF)


def ring_second(at, terms, arrived, lead, groups):
    if not arrived:
        return []
    size = terms[0].shape[1] // 4
    inputs = [(a, lead, entry) for entry in (1, 2) for a in terms]
    inputs += [(a, lead, None) for a in arrived]
    return ring_call(ring_second_body, "ring_second", at, groups, inputs, [(size, BF)] * 2)


def ring_move(sent):
    return [shift(a, step) for a, step in zip(sent, (1, -1))]


def scattered(terms, lead, groups):
    total = functools.reduce(jnp.add, [a[lead : lead + groups].astype(F32) for a in terms])
    return lax.psum_scatter(total.astype(BF), "dp", scatter_dimension=1, tiled=True).astype(F32)


def ring_end_body(at, a, b, c, d, out):
    out[...] = added(a, b, c, d)


def ring_end(at, terms, arrived):
    groups = terms[0].shape[0]
    if not arrived:
        return scattered(terms, 0, groups)
    inputs = [(a, 0, 3) for a in terms] + [(a, 0, None) for a in arrived]
    return ring_call(
        ring_end_body, "ring_end", at, groups, inputs, [(terms[0].shape[1] // 4, F32)]
    )[0]


def ring_ends_body(at, *refs):
    keep, sent = refs[8:]
    sums = [added(*refs[:4]), added(*refs[4:8])]
    first = at[4] == 0
    keep[...] = jnp.where(first, sums[0], sums[1])
    sent[...] = jnp.where(first, sums[1], sums[0]).astype(BF)


def ring_ends(at, terms, arrived, lead, groups):
    if not arrived[0]:
        sums = [scattered(a, lead, groups) for a in terms]
        first = at[4] == 0
        return (
            jnp.where(first, sums[0], sums[1]),
            jnp.where(first, sums[1], sums[0]).astype(BF),
        )
    inputs = []
    for layer in range(2):
        inputs += [(a, lead, 3) for a in terms[layer]] + [(a, 0, None) for a in arrived[layer]]
    size = terms[0][0].shape[1] // 4
    return ring_call(ring_ends_body, "ring_ends", at, groups, inputs, [(size, F32), (size, BF)])


def phase(*values):
    return lax.optimization_barrier(values)


def sum_small(value, axis):
    count = lax.axis_size(axis)
    if count != 4:
        return lax.psum(value, axis)
    return (value + exchange(value, axis, 1)) + (
        exchange(value, axis, 2) + exchange(value, axis, 3)
    )


def local(
    inputs,
    norm_gains,
    attention_in,
    attention_out,
    bias_table,
    router_weight,
    up_weight,
    down_weight,
    routes,
    piece_starts,
    valid_mask,
    cotangent,
):
    s = lax.axis_index("section")
    t = lax.axis_index("tensor")
    z = lax.axis_index("dp")
    tensor = lax.axis_size("tensor")
    rows = inputs.shape[1]
    wide = attention_in.shape[3]
    heads = wide // HEAD_DIM
    first = s == 0

    def mine(array):
        return lax.dynamic_index_in_dim(array, s, 0, keepdims=False)

    def by_layer(own, other):
        return jnp.where(first, own, other), jnp.where(first, other, own)

    def swap(value):
        return jax.tree.map(lambda a: exchange(a, "section", 1), value)

    def pair(value):
        return value, swap(value)

    h0 = mine(inputs)
    g1 = mine(cotangent)
    place = [
        jnp.stack([t, s, jnp.where(s == layer, 0, 1)]).astype(jnp.int32) for layer in range(2)
    ]
    selects = [place[layer][2:] for layer in range(2)]
    dp_size = lax.axis_size("dp")
    at = jnp.stack([(z + i) % dp_size for i in (2, 1, 3, 0)] + [s]).astype(jnp.int32)
    order = jnp.where(first, jnp.array([2, 3, 0, 1]), jnp.array([0, 1, 2, 3])).astype(jnp.int32)
    hot = diagonal_one_hot()
    hot_rows = hot.transpose(2, 0, 1).reshape(BUCKETS, -1)

    gain_pair, table_pair = pair(norm_gains[0]), pair(bias_table[0].T)
    w_out_pair = pair(attention_out[0])

    def prepared(layer):
        return prepare(layer, place[layer], gain_pair, table_pair, hot_rows, valid_mask, rows)

    x_parts, first_prepared, gain_pair, table_pair, w_in_pair, w_out, route_pair, router_pair, up, down = phase(
        gather_parts(h0),
        prepared(0),
        gain_pair,
        table_pair,
        pair(jnp.swapaxes(attention_in[0], 1, 2).reshape(3 * wide, D)),
        by_layer(*w_out_pair),
        pair(routes[0, :, :, 0]),
        pair(router_weight[0].T),
        up_weight[0],
        down_weight[0],
    )

    gain, tile, valid_col, valid_own = first_prepared
    gains, tiles = [gain], [tile]
    hidden = [h0, None]
    saved, outputs, stats, w_out_parts = [], [], [], []
    for layer in range(2):
        kept, att_parts = fwd_attention(
            place[layer],
            piece_starts,
            valid_col,
            gains[layer],
            w_in_pair,
            tiles[layer],
            x_parts,
            layer == 0,
        )
        if layer == 0:
            w_out_parts.append(gather_parts(w_out[0]))
            up_pair, down_pair = pair(up), pair(down)
            att_parts, w_out_parts[0] = phase(att_parts, w_out_parts[0])
        else:
            g_parts = [g1] + [exchange(g1, "tensor", k) for k in range(1, tensor - 1)]
            att_parts, g_parts = phase(att_parts, g_parts)
        pieces = swap_parts(att_parts)
        mid, xn_mid, stat = after_attention(
            hidden[layer], gains[layer], valid_own, pieces, w_out_parts[layer]
        )
        if layer == 0:
            xn_mid, route_pair, router_pair, gain_pair, table_pair = phase(
                xn_mid, route_pair, router_pair, gain_pair, table_pair
            )
            targets = make_targets(place[0], route_pair, router_pair, tensor)
            gain, tile = prepared(1)
            gains.append(gain)
            tiles.append(tile)
        xn_parts = gather_parts(xn_mid)
        if layer == 0:
            xn_parts, targets, gains, tiles, up_pair, down_pair, w_out = phase(
                xn_parts, targets, gains, tiles, up_pair, down_pair, w_out
            )
        else:
            xn_parts, g1 = phase(xn_parts, g1)
        row, col, router = targets[layer::2]
        ex, y_parts = fwd_experts(selects[layer], row, col, router, up_pair, down_pair, xn_parts)
        saved.append([kept, pieces, mid, xn_mid, ex])
        if layer == 0:
            w_out_parts.append(gather_parts(w_out[1]))
            y_parts, w_out_parts[1] = phase(y_parts, w_out_parts[1])
            y_parts = swap_parts(y_parts)
            combined, out, xn_next, stat_more = after_experts(
                mid, ex[3], gains[1], valid_own, y_parts
            )
            outputs.append(out)
            stats.append((stat, stat_more))
            saved[0].append(combined)
            hidden[1] = out
            x_parts = gather_parts(xn_next)
        else:
            g_parts.append(exchange(g1, "tensor", tensor - 1))
            y_parts, g_parts, ex = phase(y_parts, g_parts, ex)

    fwd_y_parts = y_parts
    half = EXPERTS // 2
    small_1 = square_1 = None
    for layer in (1, 0):
        row, col, router = targets[layer::2]
        kept, pieces, mid, xn_mid, ex = saved[layer][:5]
        expert_in, act, slope, gate, probs = ex
        g = g_parts[0]
        (d_out, d_up), y_parts = bwd_experts(
            selects[layer], row, col, gate, slope, up_pair, down_pair, g_parts
        )
        if layer == 1:
            fwd_y_parts = swap_parts(fwd_y_parts)
            y_parts, d_out, d_up, fwd_y_parts = phase(y_parts, d_out, d_up, fwd_y_parts)
            combined, out, _, stat_more = after_experts(
                mid, gate, gains[1], valid_own, fwd_y_parts
            )
            outputs.append(out)
            stats.append((stat, stat_more))
        else:
            y_parts, d_out, d_up, out_terms_1, up_ring_1 = phase(
                y_parts, d_out, d_up, swap_parts(out_terms), ring_move(up_ring_1)
            )
            combined = saved[0][5]
            square_1 = attention_grads(place[1], saved[1][0][0], d_proj, out_terms_1, None)

        sent, keep = expert_grads(order, act, d_out, expert_in, d_up)
        y_parts, sent, keep, combined, square_1 = phase(
            swap_parts(y_parts), sent, keep, combined, square_1
        )

        (d_mid, d_a, grad_gain_mid, grad_router), d_pieces = middle_back(
            g,
            combined,
            probs,
            col,
            router,
            mid,
            gains[layer],
            xn_mid,
            y_parts,
            w_out_parts[layer],
        )
        d_pieces = swap_parts(d_pieces)
        out_terms = out_grads(pieces, d_a)
        terms = (keep, swap(sent))
        ring = ring_first(at, terms)
        d_pieces, out_terms, ring, terms = phase(d_pieces, out_terms, ring, terms)

        xn, qkv, turned, lse = kept
        (d_proj, diag, far, grad_gain_in), x_terms = bwd_attention(
            place[layer],
            piece_starts,
            valid_col,
            gains[layer],
            w_in_pair,
            tiles[layer],
            (xn, qkv, turned, lse),
            d_pieces,
        )
        if layer == 0:
            out_terms = swap_parts(out_terms)
        x_terms, ring, d_proj, diag, far, out_terms = phase(
            x_terms, ring_move(ring), d_proj, diag, far, out_terms
        )

        down_ring = ring_second(at, terms, ring, 0, half)
        up_ring = ring_second(at, terms, ring, half, half)
        if layer == 0:
            x_terms, down_ring = phase(x_terms, down_ring)
            down_ring = ring_move(down_ring)
        x_terms = swap_parts(x_terms)
        small = small_sums(
            place[0],
            diag,
            far,
            hot_rows,
            grad_gain_in,
            grad_gain_mid,
            grad_router,
            stats[layer],
            small_1,
        )
        if layer == 1:
            x_terms, down_ring, up_ring_1, small_1 = phase(x_terms, down_ring, up_ring, small)
            d_h_1, d_h_low = input_back(d_mid, hidden[1], gains[1], x_terms)
            g_parts = gather_parts(d_h_low)
            g_parts, down_ring_1, out_terms = phase(g_parts, ring_move(down_ring), out_terms)
            d_h_1, terms_1 = d_h_low, terms

    def kept_sent(values):
        return jnp.where(first, values[0], values[1]), jnp.where(first, values[1], values[0])

    def placed(own, received):
        return jnp.where(
            first,
            jnp.concatenate([own, received], axis=0),
            jnp.concatenate([received, own], axis=0),
        )

    square, sent = attention_grads(place[0], xn, d_proj, out_terms, square_1)
    x_terms, down_ring, up_ring, square, small = phase(
        x_terms, down_ring, up_ring, (square, swap(sent)), (small[0], swap(small[1]))
    )

    d_h = input_back(d_mid, hidden[0], gains[0], x_terms)[0]
    square_ring = ring_move(ring_first(at, square))
    small = small[0] + small[1]
    shared = sum_small(small[:8], "tensor")
    out_keep, sent = kept_sent(outputs)
    d_h_keep, d_h_sent = kept_sent((d_h, d_h_1.astype(F32)))
    up_ring, square_ring, shared, out_moved, d_h_moved = phase(
        ring_move(up_ring), square_ring, shared, swap(sent), swap(d_h_sent.astype(BF))
    )

    small = sum_small(jnp.concatenate([shared, small[8:]], axis=0), "dp")
    square_ring = ring_move(ring_second(at, square, square_ring, 0, 1))
    grad_w_in, grad_w_out = attention_results(ring_end(at, square, square_ring)[0], wide)
    layer_out = placed(out_keep[None], out_moved[None])
    input_grad = placed(d_h_keep[None], d_h_moved.astype(F32)[None])
    expert_results = []
    for lead, ring_0, ring_1 in ((0, down_ring, down_ring_1), (half, up_ring, up_ring_1)):
        keep, sent = ring_ends(at, (terms, terms_1), (ring_0, ring_1), lead, half)
        expert_results.append(placed(keep, swap(sent).astype(F32)))
    table = small[8 : 8 + heads, :BUCKETS].T
    share = BUCKETS // lax.axis_size("dp")
    stat = small[6]
    root_means = jnp.sqrt(stat[:3] / (stat[3] * D))
    return (
        layer_out[None],
        input_grad[None],
        small[None, 0:2],
        grad_w_in[None],
        grad_w_out[None],
        lax.dynamic_slice_in_dim(table, z * share, share, 0)[None],
        small[2:6].T[None],
        expert_results[1][None],
        expert_results[0][None],
        root_means[None],
    )


def solution(mesh):
    placed = (
        P("dp", "tensor", None),
        P("section", None, None),
        P("section", None, None, "tensor"),
        P("section", "tensor", None),
        P("section", None, "tensor"),
        P("section", None, None),
        P("section", None, None, "tensor"),
        P("section", None, "tensor", None),
        P("section", "dp", None, None),
        P("dp", None),
        P("dp", None),
        P("dp", "tensor", None),
    )
    return jax.shard_map(
        local,
        mesh=mesh,
        in_specs=placed,
        out_specs=(
            P("section", "dp", "tensor", None),
            P("section", "dp", "tensor", None),
            P("section", None, None),
            P("section", None, "dp", "tensor"),
            P("section", ("tensor", "dp"), None),
            P("section", "dp", "tensor"),
            P("section", None, None),
            P("section", None, "dp", "tensor"),
            P("section", None, ("tensor", "dp"), None),
            P("section", None),
        ),
        check_vma=False,
    )
```

time: 690 us -> 511 us (0.74)
  waiting for transfers between devices: 219 us -> 165 us
  matrix products: 49.4 us -> 0 us
  starting transfers between devices: 151 us -> 111 us
  local copies, waits for them, and re-layouts: 49.4 us -> 28.9 us
  other arithmetic: 30.8 us -> 11.4 us
  Pallas kernels: 179 us -> 187 us
    ppermute x24 -> x16, waiting for transfers between devices: 105 us -> 37.8 us  [shift(): lax.ppermute(value, 'dp', [(i, (i + step) % count) for i in range(count)])]
    dot_general x21 -> x0, matrix products: 49.4 us -> none  [the longest x8 26 us: one(): jnp.einsum('eca,ecb->eab', lax.dynamic_slice_in_dim(left, which * half, h...]
    ppermute x24 -> x16, starting transfers between devices: 71.9 us -> 27.7 us  [shift(): lax.ppermute(value, 'dp', [(i, (i + step) % count) for i in range(count)])]
    pallas_call x3 -> x22, Pallas kernels: 10.3 us -> 54.2 us  [the longest x2 22.1 us: expert_grads(): pl.pallas_call(expert_grads_body, grid_spec=pltpu.PrefetchScalarGridSpec(...]
    ppermute x82, waiting for transfers between devices: 114 us -> 127 us  [exchange(): return lax.ppermute(value, axis, [(i, i ^ mask) for i in range(count)])]
    slice x22 -> x3, local copies, waits for them, and re-layouts: 9.18 us -> 0.11 us  [the longest x1 0.11 us: attention_results(): value[b * taken:(b + 1) * taken, 3 * wide:]]
    unnamed x206 -> x269, local copies, waits for them, and re-layouts: 19.2 us -> 26.6 us
  transfers between devices with their start and end apart: 106 -> 98, of which waited for: 38 -> 36; matrix products, arithmetic and copies ran while one was open for 16% -> 3% of each run, Pallas kernels for 23% -> 36%
where the time goes in v1:
time: 511 us; the launch traced here: 506 us
  Pallas kernels  187 us (37%)
  waiting for transfers between devices  165 us (32%)
  starting transfers between devices  111 us (22%)
  local copies, waits for them, and re-layouts  28.9 us (6%)
  other arithmetic  11.4 us (2%)
    ppermute x82, waiting for transfers between devices, exchange(): return lax.ppermute(value, axis, [(i, i ^ mask) for i in range(count)])  127 us
    ppermute x82, starting transfers between devices, exchange(): return lax.ppermute(value, axis, [(i, i ^ mask) for i in range(count)])  83 us
    ppermute x16, waiting for transfers between devices, shift(): lax.ppermute(value, 'dp', [(i, (i + step) % count) for i in range(count)])  37.8 us
    pallas_call x2, Pallas kernels, bwd_attention(): pl.pallas_call(functools.partial(bwd_attention_body, parts), out_shape=[s...  35.5 us
    pallas_call x2, Pallas kernels, fwd_experts(): pl.pallas_call(functools.partial(fwd_experts_body, parts), grid_spec=pltp...  31.8 us
    pallas_call x2, Pallas kernels, bwd_experts(): pl.pallas_call(functools.partial(bwd_experts_body, parts), grid_spec=pltp...  29.7 us
    ppermute x16, starting transfers between devices, shift(): lax.ppermute(value, 'dp', [(i, (i + step) % count) for i in range(count)])  27.7 us
    unnamed x269, local copies, waits for them, and re-layouts  26.6 us
  transfers between devices with their start and end apart: 98, of which 36 were waited for; matrix products, arithmetic and copies ran while one was open for 3% of the time, Pallas kernels for 36%

profile of v1, /device:TPU:0, one launch (start us, length us, event | category | flops | bytes accessed | tf_op | source)
XLA Modules:
  0.0 506.4 jit_solution(1235314098101285745)
XLA Ops:
  16.4 9.4 %collective-permute-done.1.refs_9_ = bf16[256,768]{1,0:T(8,128)(2,1)S(1)} collective-permute-done((bf16[256,768]{1,0:T(8,128)(2,1)S(1)}, bf16[256,768]{1,0:T(8,128)(2,1)S(1)}, u32[]{:S(2)}, u32[]{:S(2)}) %collective-permute-start.1) | collective-permute-done | bytes 393248 | tf_op jit(solution)/shard_map/ppermute | solution.py:84
  31.0 12.8 %fwd_attention.2 = (bf16[1024,768]{1,0:T(8,128)(2,1)}, bf16[3,3,1024,64]{3,2,1,0:T(8,128)(2,1)}, bf16[2,192,1024]{2,1,0:T(8,128)(2,1)}, f32[3,1,1024]{2,1,0:T(1,...) custom-call(s32[3]{0:T(128)S(1)} %pad_add_fusion.place.refs_0_, ...), custom_call_target="tpu_custom_call" | custom-call | flops 8999999488 | bytes 10000000 | tf_op jit(solution)/shard_map/fwd_attention/pallas_call | solution.py:332
  59.5 5.7 %collective-permute-done.15.refs_9_ = bf16[256,768]{1,0:T(8,128)(2,1)S(1)} collective-permute-done((bf16[256,768]{1,0:T(8,128)(2,1)S(1)}, bf16[256,768]{1,0:T(8,128)(2,1)S(1)}, u32[]{:S(2)}, u32[]{:S(2)}) %collective-permute-start.15) | collective-permute-done | bytes 393248 | tf_op jit(solution)/shard_map/ppermute | solution.py:84
  65.2 6.6 %collective-permute-done.16.refs_10_ = bf16[256,768]{1,0:T(8,128)(2,1)S(1)} collective-permute-done((bf16[256,768]{1,0:T(8,128)(2,1)S(1)}, bf16[256,768]{1,0:T(8,128)(2,1)S(1)}, u32[]{:S(2)}, u32[]{:S(2)}) %collective-permute-start.16) | collective-permute-done | bytes 393248 | tf_op jit(solution)/shard_map/ppermute | solution.py:84
  75.3 15.9 %fwd_experts.2 = (bf16[4,320,768]{2,1,0:T(8,128)(2,1)}, bf16[4,320,768]{2,1,0:T(8,128)(2,1)}, f32[4,320,768]{2,1,0:T(8,128)}, f32[1024,1]{1,0:T(8,128)S(1)}, f32...) custom-call(s32[1]{0:T(128)} %bitcast.3.refs_0_, ...), custom_call_target="tpu_custom_call" | custom-call | flops 12000000000 | bytes 30000000 | tf_op jit(solution)/shard_map/fwd_experts/pallas_call | solution.py:606
  94.9 8.0 %collective-permute-done.23.refs_5_ = bf16[256,768]{1,0:T(8,128)(2,1)S(1)} collective-permute-done((bf16[256,768]{1,0:T(8,128)(2,1)S(1)}, bf16[256,768]{1,0:T(8,128)(2,1)S(1)}, u32[]{:S(2)}, u32[]{:S(2)}) %collective-permute-start.23) | collective-permute-done | bytes 393248 | tf_op jit(solution)/shard_map/ppermute | solution.py:84
  102.9 4.8 collective-permute-done.24.refs_6_
  115.8 5.5 %collective-permute-done.26.refs_8_ = bf16[256,768]{1,0:T(8,128)(2,1)S(1)} collective-permute-done((bf16[256,768]{1,0:T(8,128)(2,1)S(1)}, bf16[256,768]{1,0:T(8,128)(2,1)S(1)}, u32[]{:S(2)}, u32[]{:S(2)}) %collective-permute-start.26) | collective-permute-done | bytes 393248 | tf_op jit(solution)/shard_map/ppermute | solution.py:84
  121.3 7.4 %collective-permute-done.27.refs_9_ = bf16[256,768]{1,0:T(8,128)(2,1)S(1)} collective-permute-done((bf16[256,768]{1,0:T(8,128)(2,1)S(1)}, bf16[256,768]{1,0:T(8,128)(2,1)S(1)}, u32[]{:S(2)}, u32[]{:S(2)}) %collective-permute-start.27) | collective-permute-done | bytes 393248 | tf_op jit(solution)/shard_map/ppermute | solution.py:84
  128.8 12.1 %fwd_attention.3 = (bf16[1024,768]{1,0:T(8,128)(2,1)}, bf16[3,3,1024,64]{3,2,1,0:T(8,128)(2,1)}, bf16[2,192,1024]{2,1,0:T(8,128)(2,1)}, f32[3,1,1024]{2,1,0:T(1,...) custom-call(s32[3]{0:T(128)S(1)} %pad_add_fusion.2.place.refs_0_, ...), custom_call_target="tpu_custom_call" | custom-call | flops 8999999488 | bytes 10000000 | tf_op jit(solution)/shard_map/fwd_attention/pallas_call | solution.py:332
  146.7 4.8 collective-permute-done.32.refs_5_.refs_2_
  156.0 6.9 %collective-permute-done.34.refs_9_ = bf16[256,768]{1,0:T(8,128)(2,1)S(1)} collective-permute-done((bf16[256,768]{1,0:T(8,128)(2,1)S(1)}, bf16[256,768]{1,0:T(8,128)(2,1)S(1)}, u32[]{:S(2)}, u32[]{:S(2)}) %collective-permute-start.34) | collective-permute-done | bytes 393248 | tf_op jit(solution)/shard_map/ppermute | solution.py:84
  162.9 4.5 collective-permute-done.35.refs_10_
  169.1 15.9 %fwd_experts.3 = (bf16[4,320,768]{2,1,0:T(8,128)(2,1)}, bf16[4,320,768]{2,1,0:T(8,128)(2,1)}, f32[4,320,768]{2,1,0:T(8,128)}, f32[1024,1]{1,0:T(8,128)S(1)}, f32...) custom-call(s32[1]{0:T(128)} %bitcast.17.refs_0_, ...), custom_call_target="tpu_custom_call" | custom-call | flops 12000000000 | bytes 30000000 | tf_op jit(solution)/shard_map/fwd_experts/pallas_call | solution.py:606
  188.6 14.9 %bwd_experts.2 = (bf16[4,320,768]{2,1,0:T(8,128)(2,1)}, bf16[4,320,768]{2,1,0:T(8,128)(2,1)}, bf16[256,768]{1,0:T(8,128)(2,1)S(1)}, bf16[256,768]{1,0:T(8,128)(2...) custom-call(s32[1]{0:T(128)} %bitcast.17.refs_0_, s32[1,1024]{1,0:T(1,128)S(1)} %get-tuple-element.463.refs_1_, ...), custom_call_target="tpu_custom_call" | custom-call | flops 12000000000 | bytes 30000000 | tf_op jit(solution)/shard_map/bwd_experts/pallas_call | solution.py:683
  209.9 11.1 %expert_grads.2 = (bf16[2,2,768,768]{3,2,1,0:T(8,128)(2,1)}, bf16[2,2,768,768]{3,2,1,0:T(8,128)(2,1)}) custom-call(s32[4]{0:T(128)S(1)} %broadcast_select_fusion.3.order, bf16[4,320,768]{2,1,0:T(8,128)(2,1)} %get-tuple-element.482.act, bf16[4,320,768]{2,1,0:T(8,128)(2,1)} %get-tuple-element.513.d_out, bf16[4,320,768]{2,1,0:T(8,128)(2,1)} %get-tuple-element.481.expert_in, ...), custom_call_target="tpu_custom_call" | custom-call | flops 1000000 | bytes 100000 | tf_op jit(solution)/shard_map/expert_grads/pallas_call | solution.py:878
  246.0 17.4 %bwd_attention.2 = (bf16[1024,576]{1,0:T(8,128)(2,1)S(1)}, f32[18,128,128]{2,1,0:T(8,128)S(1)}, f32[3,8,256]{2,1,0:T(8,128)S(1)}, f32[1,768]{1,0:T(1,128)S(1)}, ...) custom-call(s32[3]{0:T(128)S(1)} %pad_add_fusion.2.place.refs_0_, ...), custom_call_target="tpu_custom_call" | custom-call | flops 17999998976 | bytes 10000000 | tf_op jit(solution)/shard_map/bwd_attention/pallas_call | solution.py:443
  263.4 4.1 collective-permute-done.49.behind
  279.6 7.3 %collective-permute-done.51.refs_5_ = bf16[256,768]{1,0:T(8,128)(2,1)S(1)} collective-permute-done((bf16[256,768]{1,0:T(8,128)(2,1)S(1)}, bf16[256,768]{1,0:T(8,128)(2,1)S(1)}, u32[]{:S(2)}, u32[]{:S(2)}) %collective-permute-start.51) | collective-permute-done | bytes 393248 | tf_op jit(solution)/shard_map/ppermute | solution.py:84
  295.5 8.6 %collective-permute-done.53.refs_10_ = bf16[256,768]{1,0:T(8,128)(2,1)S(1)} collective-permute-done((bf16[256,768]{1,0:T(8,128)(2,1)S(1)}, bf16[256,768]{1,0:T(8,128)(2,1)S(1)}, u32[]{:S(2)}, u32[]{:S(2)}) %collective-permute-start.53) | collective-permute-done | bytes 393248 | tf_op jit(solution)/shard_map/ppermute | solution.py:84
  304.3 6.4 %collective-permute-done.54.refs_11_ = bf16[256,768]{1,0:T(8,128)(2,1)S(1)} collective-permute-done((bf16[256,768]{1,0:T(8,128)(2,1)S(1)}, bf16[256,768]{1,0:T(8,128)(2,1)S(1)}, u32[]{:S(2)}, u32[]{:S(2)}) %collective-permute-start.54) | collective-permute-done | bytes 393248 | tf_op jit(solution)/shard_map/ppermute | solution.py:84
  311.0 6.7 %collective-permute-done.57.refs_7_ = bf16[2,192,768]{2,1,0:T(8,128)(2,1)S(1)} collective-permute-done((bf16[2,192,768]{2,1,0:T(8,128)(2,1)S(1)}, bf16[2,192,768]{2,1,0:T(8,128)(2,1)S(1)}, u32[]{:S(2)}, u32[]{:S(2)}) %collective-permute-start.57) | collective-permute-done | bytes 589856 | tf_op jit(solution)/shard_map/ppermute | solution.py:970
  322.0 14.8 %bwd_experts.3 = (bf16[4,320,768]{2,1,0:T(8,128)(2,1)}, bf16[4,320,768]{2,1,0:T(8,128)(2,1)}, bf16[256,768]{1,0:T(8,128)(2,1)S(1)}, bf16[256,768]{1,0:T(8,128)(2...) custom-call(s32[1]{0:T(128)} %bitcast.3.refs_0_, s32[1,1024]{1,0:T(1,128)S(1)} %copy-done.108, ...), custom_call_target="tpu_custom_call" | custom-call | flops 12000000000 | bytes 30000000 | tf_op jit(solution)/shard_map/bwd_experts/pallas_call | solution.py:683
  343.5 11.0 %expert_grads.3 = (bf16[2,2,768,768]{3,2,1,0:T(8,128)(2,1)}, bf16[2,2,768,768]{3,2,1,0:T(8,128)(2,1)}) custom-call(s32[4]{0:T(128)S(1)} %copy-done.65, bf16[4,320,768]{2,1,0:T(8,128)(2,1)} %get-tuple-element.609.act, bf16[4,320,768]{2,1,0:T(8,128)(2,1)} %get-tuple-element.610.d_out, bf16[4,320,768]{2,1,0:T(8,128)(2,1)} %get-tuple-element.611.expert_in, ...), custom_call_target="tpu_custom_call" | custom-call | flops 1000000 | bytes 100000 | tf_op jit(solution)/shard_map/expert_grads/pallas_call | solution.py:878
  356.5 4.5 collective-permute-done.64.refs_10_
  379.0 18.1 %bwd_attention.3 = (bf16[1024,576]{1,0:T(8,128)(2,1)S(1)}, f32[18,128,128]{2,1,0:T(8,128)S(1)}, f32[3,8,256]{2,1,0:T(8,128)S(1)}, f32[1,768]{1,0:T(1,128)S(1)}, ...) custom-call(s32[3]{0:T(128)S(1)} %pad_add_fusion.place.refs_0_, ...), custom_call_target="tpu_custom_call" | custom-call | flops 17999998976 | bytes 10000000 | tf_op jit(solution)/shard_map/bwd_attention/pallas_call | solution.py:443
  419.4 13.9 %collective-permute-done.76.refs_5_ = bf16[256,768]{1,0:T(8,128)(2,1)S(1)} collective-permute-done((bf16[256,768]{1,0:T(8,128)(2,1)S(1)}, bf16[256,768]{1,0:T(8,128)(2,1)S(1)}, u32[]{:S(2)}, u32[]{:S(2)}) %collective-permute-start.76) | collective-permute-done | bytes 393248 | tf_op jit(solution)/shard_map/ppermute | solution.py:84
  442.2 3.8 collective-permute-start.83
  456.5 4.1 collective-permute-start.85
  460.6 15.4 %collective-permute-done.84.ahead = bf16[1,96,768]{2,1,0:T(8,128)(2,1)S(1)} collective-permute-done((bf16[1,96,768]{2,1,0:T(8,128)(2,1)S(1)}, bf16[1,96,768]{2,1,0:T(8,128)(2,1)S(1)}, u32[]{:S(2)}, u32[]{:S(2)}) %collective-permute-start.84) | collective-permute-done | bytes 147488 | tf_op jit(solution)/shard_map/ppermute | solution.py:970
  489.3 3.7 collective-permute-start.95
  496.7 5.0 collective-permute-done.95.d
  (506 shorter events, 211.8 us)
Async XLA Ops:
  0.7 25.2 %collective-permute-start.5 = (bf16[576,768]{1,0:T(8,128)(2,1)}, bf16[576,768]{1,0:T(8,128)(2,1)}, u32[]{:S(2)}, u32[]{:S(2)}) collective-permute-start(bf16[576,768]{1,0:T(8,128)(2,1)} %bitcast.110), channel_id=1, source_target_pairs={{0,16},{16,0},{1,17},{17,1},{2,18},{18,2},{3,19},{19,3},{4,20},{20... | collective-permute-start | bytes 2654216 | tf_op jit(solution)/shard_map/ppermute | solution.py:84
  25.8 46.0 %collective-permute-start.18 = (bf16[4,768,768]{2,1,0:T(8,128)(2,1)}, bf16[4,768,768]{2,1,0:T(8,128)(2,1)}, u32[]{:S(2)}, u32[]{:S(2)}) collective-permute-start(bf16[4,768,768]{2,1,0:T(8,128)(2,1)} %bitcast.116), channel_id=1, source_target_pairs={{0,16},{16,0},{1,17},{17,1},{2,18},{18,2},{3,19},{19,3},{4,20},{20... | collective-permute-start | bytes 14155784 | tf_op jit(solution)/shard_map/ppermute | solution.py:84
  25.8 45.9 %collective-permute-start.19 = (bf16[4,768,768]{2,1,0:T(8,128)(2,1)}, bf16[4,768,768]{2,1,0:T(8,128)(2,1)}, u32[]{:S(2)}, u32[]{:S(2)}) collective-permute-start(bf16[4,768,768]{2,1,0:T(8,128)(2,1)} %bitcast.121), channel_id=1, source_target_pairs={{0,16},{16,0},{1,17},{17,1},{2,18},{18,2},{3,19},{19,3},{4,20},{20... | collective-permute-start | bytes 14155784 | tf_op jit(solution)/shard_map/ppermute | solution.py:84
  71.8 19.6 %collective-permute-start.20 = (bf16[192,768]{1,0:T(8,128)(2,1)S(1)}, bf16[192,768]{1,0:T(8,128)(2,1)S(1)}, u32[]{:S(2)}, u32[]{:S(2)}) collective-permute-start(bf16[192,768]{1,0:T(8,128)(2,1)S(1)} %get-tuple-element.458.refs_7_.refs_12_), channel_id=1, source_target_pairs={{0,4},{4,0},{8,12},{12,8},{1,5},{5,1},{9,13},{13,9},{2,6},{6,2},{1... | collective-permute-start | bytes 884744 | tf_op jit(solution)/shard_map/ppermute | solution.py:84
  112.8 28.1 %collective-permute-start.29 = (bf16[256,768]{1,0:T(8,128)(2,1)S(1)}, bf16[256,768]{1,0:T(8,128)(2,1)S(1)}, u32[]{:S(2)}, u32[]{:S(2)}) collective-permute-start(bf16[256,768]{1,0:T(8,128)(2,1)S(1)} %dynamic-slice_bitcast_fusion.refs_9_.refs_0_), channel_id=1, source_target_pairs={{0,4},{4,0},{8,12},{12,8},{1,5},{5,1},{9,13},{13,9},{2,6},{6,2},{1... | collective-permute-start | bytes 1179656 | tf_op jit(solution)/shard_map/ppermute | solution.py:84
  113.8 27.2 %collective-permute-start.30 = (bf16[256,768]{1,0:T(8,128)(2,1)S(1)}, bf16[256,768]{1,0:T(8,128)(2,1)S(1)}, u32[]{:S(2)}, u32[]{:S(2)}) collective-permute-start(bf16[256,768]{1,0:T(8,128)(2,1)S(1)} %dynamic-slice_bitcast_fusion.refs_9_.refs_0_), channel_id=1, source_target_pairs={{0,8},{4,12},{8,0},{12,4},{1,9},{5,13},{9,1},{13,5},{2,10},{6,14},... | collective-permute-start | bytes 1179656 | tf_op jit(solution)/shard_map/ppermute | solution.py:84
  186.4 20.0 %collective-permute-start.39 = (bf16[256,768]{1,0:T(8,128)(2,1)S(1)}, bf16[256,768]{1,0:T(8,128)(2,1)S(1)}, u32[]{:S(2)}, u32[]{:S(2)}) collective-permute-start(bf16[256,768]{1,0:T(8,128)(2,1)S(1)} %get-tuple-element.496), channel_id=1, source_target_pairs={{0,8},{4,12},{8,0},{12,4},{1,9},{5,13},{9,1},{13,5},{2,10},{6,14},... | collective-permute-start | bytes 1179656 | tf_op jit(solution)/shard_map/ppermute | solution.py:84
  186.9 19.5 %collective-permute-start.40 = (bf16[256,768]{1,0:T(8,128)(2,1)S(1)}, bf16[256,768]{1,0:T(8,128)(2,1)S(1)}, u32[]{:S(2)}, u32[]{:S(2)}) collective-permute-start(bf16[256,768]{1,0:T(8,128)(2,1)S(1)} %get-tuple-element.497), channel_id=1, source_target_pairs={{0,12},{4,8},{8,4},{12,0},{1,13},{5,9},{9,5},{13,1},{2,14},{6,10},... | collective-permute-start | bytes 1179656 | tf_op jit(solution)/shard_map/ppermute | solution.py:84
  238.2 25.3 %collective-permute-start.48 = (bf16[4,96,768]{2,1,0:T(8,128)(2,1)S(1)}, bf16[4,96,768]{2,1,0:T(8,128)(2,1)S(1)}, u32[]{:S(2)}, u32[]{:S(2)}) collective-permute-start(bf16[4,96,768]{2,1,0:T(8,128)(2,1)S(1)} %get-tuple-element.549), channel_id=1, source_target_pairs={{0,1},{1,2},{2,3},{3,0},{4,5},{5,6},{6,7},{7,4},{8,9},{9,10},{10,1... | collective-permute-start | bytes 1769480 | tf_op jit(solution)/shard_map/ppermute | solution.py:970
  239.8 27.7 %collective-permute-start.49 = (bf16[4,96,768]{2,1,0:T(8,128)(2,1)S(1)}, bf16[4,96,768]{2,1,0:T(8,128)(2,1)S(1)}, u32[]{:S(2)}, u32[]{:S(2)}) collective-permute-start(bf16[4,96,768]{2,1,0:T(8,128)(2,1)S(1)} %get-tuple-element.550), channel_id=1, source_target_pairs={{0,3},{1,0},{2,1},{3,2},{4,7},{5,4},{6,5},{7,6},{8,11},{9,8},{10,9... | collective-permute-start | bytes 1769480 | tf_op jit(solution)/shard_map/ppermute | solution.py:970
  286.8 24.1 %collective-permute-start.56 = (bf16[2,192,768]{2,1,0:T(8,128)(2,1)S(1)}, bf16[2,192,768]{2,1,0:T(8,128)(2,1)S(1)}, u32[]{:S(2)}, u32[]{:S(2)}) collective-permute-start(bf16[2,192,768]{2,1,0:T(8,128)(2,1)S(1)} %get-tuple-element.582), channel_id=1, source_target_pairs={{0,1},{1,2},{2,3},{3,0},{4,5},{5,6},{6,7},{7,4},{8,9},{9,10},{10,1... | collective-permute-start | bytes 1769480 | tf_op jit(solution)/shard_map/ppermute | solution.py:970
  288.8 28.8 %collective-permute-start.57 = (bf16[2,192,768]{2,1,0:T(8,128)(2,1)S(1)}, bf16[2,192,768]{2,1,0:T(8,128)(2,1)S(1)}, u32[]{:S(2)}, u32[]{:S(2)}) collective-permute-start(bf16[2,192,768]{2,1,0:T(8,128)(2,1)S(1)} %get-tuple-element.583), channel_id=1, source_target_pairs={{0,3},{1,0},{2,1},{3,2},{4,7},{5,4},{6,5},{7,6},{8,11},{9,8},{10,9... | collective-permute-start | bytes 1769480 | tf_op jit(solution)/shard_map/ppermute | solution.py:970
  304.1 32.7 %collective-permute-start.61 = (bf16[2,192,768]{2,1,0:T(8,128)(2,1)S(1)}, bf16[2,192,768]{2,1,0:T(8,128)(2,1)S(1)}, u32[]{:S(2)}, u32[]{:S(2)}) collective-permute-start(bf16[2,192,768]{2,1,0:T(8,128)(2,1)S(1)} %get-tuple-element.603), channel_id=1, source_target_pairs={{0,1},{1,2},{2,3},{3,0},{4,5},{5,6},{6,7},{7,4},{8,9},{9,10},{10,1... | collective-permute-start | bytes 1769480 | tf_op jit(solution)/shard_map/ppermute | solution.py:970
  310.7 29.2 %collective-permute-start.62 = (bf16[2,192,768]{2,1,0:T(8,128)(2,1)S(1)}, bf16[2,192,768]{2,1,0:T(8,128)(2,1)S(1)}, u32[]{:S(2)}, u32[]{:S(2)}) collective-permute-start(bf16[2,192,768]{2,1,0:T(8,128)(2,1)S(1)} %get-tuple-element.604), channel_id=1, source_target_pairs={{0,3},{1,0},{2,1},{3,2},{4,7},{5,4},{6,5},{7,6},{8,11},{9,8},{10,9... | collective-permute-start | bytes 1769480 | tf_op jit(solution)/shard_map/ppermute | solution.py:970
  318.5 21.4 %collective-permute-start.58 = (bf16[192,768]{1,0:T(8,128)(2,1)S(1)}, bf16[192,768]{1,0:T(8,128)(2,1)S(1)}, u32[]{:S(2)}, u32[]{:S(2)}) collective-permute-start(bf16[192,768]{1,0:T(8,128)(2,1)S(1)} %get-tuple-element.600), channel_id=1, source_target_pairs={{0,4},{4,0},{8,12},{12,8},{1,5},{5,1},{9,13},{13,9},{2,6},{6,2},{1... | collective-permute-start | bytes 884744 | tf_op jit(solution)/shard_map/ppermute | solution.py:84
  320.0 19.9 %collective-permute-start.59 = (bf16[192,768]{1,0:T(8,128)(2,1)S(1)}, bf16[192,768]{1,0:T(8,128)(2,1)S(1)}, u32[]{:S(2)}, u32[]{:S(2)}) collective-permute-start(bf16[192,768]{1,0:T(8,128)(2,1)S(1)} %get-tuple-element.601), channel_id=1, source_target_pairs={{0,8},{4,12},{8,0},{12,4},{1,9},{5,13},{9,1},{13,5},{2,10},{6,14},... | collective-permute-start | bytes 884744 | tf_op jit(solution)/shard_map/ppermute | solution.py:84
  371.6 25.5 %collective-permute-start.70 = (bf16[4,96,768]{2,1,0:T(8,128)(2,1)S(1)}, bf16[4,96,768]{2,1,0:T(8,128)(2,1)S(1)}, u32[]{:S(2)}, u32[]{:S(2)}) collective-permute-start(bf16[4,96,768]{2,1,0:T(8,128)(2,1)S(1)} %get-tuple-element.648), channel_id=1, source_target_pairs={{0,1},{1,2},{2,3},{3,0},{4,5},{5,6},{6,7},{7,4},{8,9},{9,10},{10,1... | collective-permute-start | bytes 1769480 | tf_op jit(solution)/shard_map/ppermute | solution.py:970
  373.8 26.6 %collective-permute-start.71 = (bf16[4,96,768]{2,1,0:T(8,128)(2,1)S(1)}, bf16[4,96,768]{2,1,0:T(8,128)(2,1)S(1)}, u32[]{:S(2)}, u32[]{:S(2)}) collective-permute-start(bf16[4,96,768]{2,1,0:T(8,128)(2,1)S(1)} %get-tuple-element.649), channel_id=1, source_target_pairs={{0,3},{1,0},{2,1},{3,2},{4,7},{5,4},{6,5},{7,6},{8,11},{9,8},{10,9... | collective-permute-start | bytes 1769480 | tf_op jit(solution)/shard_map/ppermute | solution.py:970
  375.4 21.6 %collective-permute-start.72 = (bf16[192,768]{1,0:T(8,128)(2,1)S(1)}, bf16[192,768]{1,0:T(8,128)(2,1)S(1)}, u32[]{:S(2)}, u32[]{:S(2)}) collective-permute-start(bf16[192,768]{1,0:T(8,128)(2,1)S(1)} %get-tuple-element.654), channel_id=1, source_target_pairs={{0,4},{4,0},{8,12},{12,8},{1,5},{5,1},{9,13},{13,9},{2,6},{6,2},{1... | collective-permute-start | bytes 884744 | tf_op jit(solution)/shard_map/ppermute | solution.py:84
  377.1 20.0 %collective-permute-start.73 = (bf16[192,768]{1,0:T(8,128)(2,1)S(1)}, bf16[192,768]{1,0:T(8,128)(2,1)S(1)}, u32[]{:S(2)}, u32[]{:S(2)}) collective-permute-start(bf16[192,768]{1,0:T(8,128)(2,1)S(1)} %get-tuple-element.655), channel_id=1, source_target_pairs={{0,8},{4,12},{8,0},{12,4},{1,9},{5,13},{9,1},{13,5},{2,10},{6,14},... | collective-permute-start | bytes 884744 | tf_op jit(solution)/shard_map/ppermute | solution.py:84
  377.4 19.7 %collective-permute-start.74 = (bf16[192,768]{1,0:T(8,128)(2,1)S(1)}, bf16[192,768]{1,0:T(8,128)(2,1)S(1)}, u32[]{:S(2)}, u32[]{:S(2)}) collective-permute-start(bf16[192,768]{1,0:T(8,128)(2,1)S(1)} %get-tuple-element.656), channel_id=1, source_target_pairs={{0,12},{4,8},{8,4},{12,0},{1,13},{5,9},{9,5},{13,1},{2,14},{6,10},... | collective-permute-start | bytes 884744 | tf_op jit(solution)/shard_map/ppermute | solution.py:84
  403.6 37.1 %collective-permute-start.80 = (bf16[1,768,768]{2,1,0:T(8,128)(2,1)}, bf16[1,768,768]{2,1,0:T(8,128)(2,1)S(1)}, u32[]{:S(2)}, u32[]{:S(2)}) collective-permute-start(bf16[1,768,768]{2,1,0:T(8,128)(2,1)} %get-tuple-element.682), channel_id=1, source_target_pairs={{0,16},{16,0},{1,17},{17,1},{2,18},{18,2},{3,19},{19,3},{4,20},{20... | collective-permute-start | bytes 3538952 | tf_op jit(solution)/shard_map/ppermute | solution.py:84
  406.5 34.2 %collective-permute-start.78 = (bf16[2,192,768]{2,1,0:T(8,128)(2,1)}, bf16[2,192,768]{2,1,0:T(8,128)(2,1)}, u32[]{:S(2)}, u32[]{:S(2)}) collective-permute-start(bf16[2,192,768]{2,1,0:T(8,128)(2,1)} %get-tuple-element.671), channel_id=1, source_target_pairs={{0,1},{1,2},{2,3},{3,0},{4,5},{5,6},{6,7},{7,4},{8,9},{9,10},{10,1... | collective-permute-start | bytes 1769480 | tf_op jit(solution)/shard_map/ppermute | solution.py:970
  406.8 33.9 %collective-permute-start.79 = (bf16[2,192,768]{2,1,0:T(8,128)(2,1)}, bf16[2,192,768]{2,1,0:T(8,128)(2,1)}, u32[]{:S(2)}, u32[]{:S(2)}) collective-permute-start(bf16[2,192,768]{2,1,0:T(8,128)(2,1)} %get-tuple-element.672), channel_id=1, source_target_pairs={{0,3},{1,0},{2,1},{3,2},{4,7},{5,4},{6,5},{7,6},{8,11},{9,8},{10,9... | collective-permute-start | bytes 1769480 | tf_op jit(solution)/shard_map/ppermute | solution.py:970
  413.7 19.6 %collective-permute-start.76 = (bf16[256,768]{1,0:T(8,128)(2,1)S(1)}, bf16[256,768]{1,0:T(8,128)(2,1)S(1)}, u32[]{:S(2)}, u32[]{:S(2)}) collective-permute-start(bf16[256,768]{1,0:T(8,128)(2,1)S(1)} %get-tuple-element.669), channel_id=1, source_target_pairs={{0,8},{4,12},{8,0},{12,4},{1,9},{5,13},{9,1},{13,5},{2,10},{6,14},... | collective-permute-start | bytes 1179656 | tf_op jit(solution)/shard_map/ppermute | solution.py:84
  417.0 23.7 %collective-permute-start.77 = (bf16[256,768]{1,0:T(8,128)(2,1)}, bf16[256,768]{1,0:T(8,128)(2,1)}, u32[]{:S(2)}, u32[]{:S(2)}) collective-permute-start(bf16[256,768]{1,0:T(8,128)(2,1)} %get-tuple-element.670), channel_id=1, source_target_pairs={{0,12},{4,8},{8,4},{12,0},{1,13},{5,9},{9,5},{13,1},{2,14},{6,10},... | collective-permute-start | bytes 1179656 | tf_op jit(solution)/shard_map/ppermute | solution.py:84
  442.2 34.2 %collective-permute-start.82 = (bf16[2,192,768]{2,1,0:T(8,128)(2,1)S(1)}, bf16[2,192,768]{2,1,0:T(8,128)(2,1)S(1)}, u32[]{:S(2)}, u32[]{:S(2)}) collective-permute-start(bf16[2,192,768]{2,1,0:T(8,128)(2,1)S(1)} %get-tuple-element.693), channel_id=1, source_target_pairs={{0,1},{1,2},{2,3},{3,0},{4,5},{5,6},{6,7},{7,4},{8,9},{9,10},{10,1... | collective-permute-start | bytes 1769480 | tf_op jit(solution)/shard_map/ppermute | solution.py:970
  442.2 34.2 %collective-permute-start.83 = (bf16[2,192,768]{2,1,0:T(8,128)(2,1)S(1)}, bf16[2,192,768]{2,1,0:T(8,128)(2,1)S(1)}, u32[]{:S(2)}, u32[]{:S(2)}) collective-permute-start(bf16[2,192,768]{2,1,0:T(8,128)(2,1)S(1)} %get-tuple-element.694), channel_id=1, source_target_pairs={{0,3},{1,0},{2,1},{3,2},{4,7},{5,4},{6,5},{7,6},{8,11},{9,8},{10,9... | collective-permute-start | bytes 1769480 | tf_op jit(solution)/shard_map/ppermute | solution.py:970
  451.3 25.1 %collective-permute-start.90 = (bf16[256,768]{1,0:T(8,128)(2,1)S(1)}, bf16[256,768]{1,0:T(8,128)(2,1)S(1)}, u32[]{:S(2)}, u32[]{:S(2)}) collective-permute-start(bf16[256,768]{1,0:T(8,128)(2,1)S(1)} %fusion), channel_id=1, source_target_pairs={{0,16},{16,0},{1,17},{17,1},{2,18},{18,2},{3,19},{19,3},{4,20},{20... | collective-permute-start | bytes 1179656 | tf_op jit(solution)/shard_map/ppermute | solution.py:84
  451.3 24.8 %collective-permute-start.84 = (bf16[1,96,768]{2,1,0:T(8,128)(2,1)S(1)}, bf16[1,96,768]{2,1,0:T(8,128)(2,1)S(1)}, u32[]{:S(2)}, u32[]{:S(2)}) collective-permute-start(bf16[1,96,768]{2,1,0:T(8,128)(2,1)S(1)} %get-tuple-element.697), channel_id=1, source_target_pairs={{0,1},{1,2},{2,3},{3,0},{4,5},{5,6},{6,7},{7,4},{8,9},{9,10},{10,1... | collective-permute-start | bytes 442376 | tf_op jit(solution)/shard_map/ppermute | solution.py:970
  456.5 19.9 %collective-permute-start.85 = (bf16[1,96,768]{2,1,0:T(8,128)(2,1)S(1)}, bf16[1,96,768]{2,1,0:T(8,128)(2,1)S(1)}, u32[]{:S(2)}, u32[]{:S(2)}) collective-permute-start(bf16[1,96,768]{2,1,0:T(8,128)(2,1)S(1)} %get-tuple-element.698), channel_id=1, source_target_pairs={{0,3},{1,0},{2,1},{3,2},{4,7},{5,4},{6,5},{7,6},{8,11},{9,8},{10,9... | collective-permute-start | bytes 442376 | tf_op jit(solution)/shard_map/ppermute | solution.py:970
  483.2 21.0 %collective-permute-start.96 = (bf16[2,192,768]{2,1,0:T(8,128)(2,1)S(1)}, bf16[2,192,768]{2,1,0:T(8,128)(2,1)S(1)}, u32[]{:S(2)}, u32[]{:S(2)}) collective-permute-start(bf16[2,192,768]{2,1,0:T(8,128)(2,1)S(1)} %get-tuple-element.719), channel_id=1, source_target_pairs={{0,16},{16,0},{1,17},{17,1},{2,18},{18,2},{3,19},{19,3},{4,20},{20... | collective-permute-start | bytes 1769480 | tf_op jit(solution)/shard_map/ppermute | solution.py:84
  (199 other events, 3019.0 us)

commit v2 on v1

--- a/solution.py
+++ b/solution.py
@@ -347,7 +347,7 @@
         compiler_params=limit(32),
         cost_estimate=cost(9e9, 1e7),
         name="fwd_attention",
-    )(place, starts, valid_col, gain, *w_pair, tiles, *x_parts)
+    )(place, starts, valid_col, gain, *[from_hbm(a) for a in (*w_pair, tiles)], *x_parts)
     return outs[:4], list(outs[4:])
 
 
@@ -443,12 +443,12 @@
     outs = pl.pallas_call(
         functools.partial(bwd_attention_body, parts),
         out_shape=[
-            shape((SEQ, 3 * wide), BF),
-            shape((heads * DIAGS, BAND, BAND), F32),
+            in_hbm((SEQ, 3 * wide), BF),
+            in_hbm((heads * DIAGS, BAND, BAND), F32),
             shape((heads, 8, QB), F32),
             shape((1, D), F32),
         ]
-        + [shape((rows, D), BF)] * parts,
+        + [in_hbm((rows, D), BF)] * parts,
         in_specs=[smem()] * 2 + vm(9 + parts),
         out_specs=vm(4 + parts),
         scratch_shapes=[
@@ -464,7 +464,16 @@
         compiler_params=limit(36),
         cost_estimate=cost(1.8e10, 1e7),
         name="bwd_attention",
-    )(place, starts, valid_col, gain, *w_pair, tiles, *saved, *d_parts)
+    )(
+        place,
+        starts,
+        valid_col,
+        gain,
+        *w_pair,
+        tiles,
+        *saved,
+        *d_parts,
+    )
     return outs[:4], list(outs[4:])
 
 
@@ -525,7 +534,7 @@
         compiler_params=limit(16),
         cost_estimate=cost(1e6, 1e5),
         name="small_sums",
-    )(place, tiles, far, hot, gain_in, gain_mid, router, *stats, *([other] if paired else []))
+    )(place, from_hbm(tiles), far, hot, gain_in, gain_mid, router, *stats, *([other] if paired else []))
     return outs if paired else outs[0]
 
 
@@ -541,16 +550,20 @@
     return dot((target_row[...] == slot).astype(BF), tokens_ref[...]).astype(BF)
 
 
+HALF = EXPERTS // 2
+
+
 def fwd_experts_body(parts, *refs):
-    sel, target_row, target_col, router, up_own, up_other, down_own, down_other = refs[:8]
-    x_refs = refs[8 : 8 + parts]
-    in_ref, act_ref, slope_ref, gate_ref, probs_ref = refs[8 + parts : 13 + parts]
+    sel, order, target_row, target_col, router, up_own, up_other, down_own, down_other = refs[:9]
+    x_refs = refs[9 : 9 + parts]
+    half_ref, slope_ref, gate_ref, probs_ref = refs[9 + parts : 13 + parts]
     out_refs = refs[13 + parts : 13 + 2 * parts]
     x_ref, slots_ref, up_ref, down_ref = refs[13 + 2 * parts :]
     rows = SEQ // parts
-    e = pl.program_id(0)
-
-    @pl.when(e == 0)
+    step = pl.program_id(0)
+    e = order[step]
+
+    @pl.when(step == 0)
     def _():
         lane = lax.broadcasted_iota(jnp.int32, (rows, 128), 1)
         for k in range(parts):
@@ -569,50 +582,54 @@
     choose(sel[0], up_own.at[0], up_other.at[0], up_ref)
     choose(sel[0], down_own.at[0], down_other.at[0], down_ref)
     expert_in = dispatch(e, target_row, x_ref)
-    in_ref[0] = expert_in
+    half_ref[0, 1] = expert_in
     up = dot(expert_in, up_ref[...])
     inner = np.sqrt(2 / np.pi).astype(np.float32)
     square = up * up
     bend = jnp.tanh(inner * (up * (1.0 + 0.044715 * square)))
     half = 0.5 * (1.0 + bend)
     act = (up * half).astype(BF)
-    act_ref[0] = act
+    half_ref[0, 0] = act
     slope_ref[0] = half + 0.5 * up * (1.0 - bend * bend) * (
         inner * (1.0 + 3 * 0.044715 * square)
     )
     slots_ref[pl.ds(pl.multiple_of(e * CAP, CAP), CAP), :] = dot(act, down_ref[...]).astype(BF)
 
-    @pl.when(e == EXPERTS - 1)
+    @pl.when(step == EXPERTS - 1)
     def _():
         combine(parts, rows, target_col, slots_ref, out_refs)
 
 
 def expert_specs(block):
-    own = pl.BlockSpec(block, lambda e, sel: (e * (1 - sel[0]), 0, 0))
-    other = pl.BlockSpec(block, lambda e, sel: (e * sel[0], 0, 0))
+    own = pl.BlockSpec(block, lambda i, sel, order: (order[i] * (1 - sel[0]), 0, 0))
+    other = pl.BlockSpec(block, lambda i, sel, order: (order[i] * sel[0], 0, 0))
     return [own, other]
 
 
+def half_spec(columns):
+    return pl.BlockSpec((1, 2, CAP, columns), lambda i, sel, order: (i, 0, 0, 0))
+
+
 def whole(dims):
-    return pl.BlockSpec(dims, lambda e, sel: (0,) * len(dims))
-
-
-def fwd_experts(select, target_row, target_col, router, up_pair, down_pair, x_parts):
+    return pl.BlockSpec(dims, lambda i, sel, order: (0,) * len(dims))
+
+
+def fwd_experts(select, order, target_row, target_col, router, up_pair, down_pair, x_parts):
     parts = len(x_parts)
     rows = SEQ // parts
     hidden = up_pair[0].shape[2]
-    each = pl.BlockSpec((1, CAP, D), lambda e, sel: (e, 0, 0))
-    each_hidden = pl.BlockSpec((1, CAP, hidden), lambda e, sel: (e, 0, 0))
+    each_hidden = pl.BlockSpec((1, CAP, hidden), lambda i, sel, order: (i, 0, 0))
     outs = pl.pallas_call(
         functools.partial(fwd_experts_body, parts),
         grid_spec=pltpu.PrefetchScalarGridSpec(
-            num_scalar_prefetch=1,
+            num_scalar_prefetch=2,
             grid=(EXPERTS,),
             in_specs=[whole((1, SEQ)), whole((SEQ, 1)), whole((128, D))]
             + expert_specs((1, D, hidden))
             + expert_specs((1, hidden, D))
             + [whole((rows, D))] * parts,
-            out_specs=[each, each_hidden, each_hidden, whole((SEQ, 1)), whole((rows, 128))]
+            out_specs=[half_spec(D)]
+            + [each_hidden, whole((SEQ, 1)), whole((rows, 128))]
             + [whole((rows, D))] * parts,
             scratch_shapes=[
                 pltpu.VMEM((SEQ, D), BF),
@@ -621,39 +638,41 @@
                 pltpu.VMEM((hidden, D), BF),
             ],
         ),
-        out_shape=[
-            in_hbm((EXPERTS, CAP, D), BF),
-            in_hbm((EXPERTS, CAP, hidden), BF),
+        out_shape=[in_hbm((EXPERTS, 2, CAP, D), BF)]
+        + [
             in_hbm((EXPERTS, CAP, hidden), F32),
             shape((SEQ, 1), F32),
             shape((rows, 128), F32),
         ]
         + [shape((rows, D), BF)] * parts,
-        compiler_params=limit(44),
+        compiler_params=limit(36),
         cost_estimate=cost(1.2e10, 3e7),
         name="fwd_experts",
     )(
         select,
+        order,
         target_row,
         target_col,
         router,
         *[from_hbm(a) for a in (*up_pair, *down_pair)],
         *x_parts,
     )
-    return outs[:5], list(outs[5:])
+    return outs[:4], list(outs[4:])
 
 
 def bwd_experts_body(parts, *refs):
-    sel, target_row, target_col, gate, slope_ref, up_own, up_other, down_own, down_other = refs[:9]
-    g_refs = refs[9 : 9 + parts]
-    refs = refs[9 + parts :]
-    dout_ref, dup_ref = refs[:2]
-    out_refs = refs[2 : 2 + parts]
-    g_ref, slots_ref, up_ref, down_ref = refs[2 + parts :]
+    sel, order, target_row, target_col, gate, slope_ref = refs[:6]
+    up_own, up_other, down_own, down_other = refs[6:10]
+    g_refs = refs[10 : 10 + parts]
+    refs = refs[10 + parts :]
+    half_ref = refs[0]
+    out_refs = refs[1 : 1 + parts]
+    g_ref, slots_ref, up_ref, down_ref = refs[1 + parts :]
     rows = SEQ // parts
-    e = pl.program_id(0)
-
-    @pl.when(e == 0)
+    step = pl.program_id(0)
+    e = order[step]
+
+    @pl.when(step == 0)
     def _():
         for k in range(parts):
             where = slice(k * rows, (k + 1) * rows)
@@ -662,34 +681,33 @@
     choose(sel[0], up_own.at[0], up_other.at[0], up_ref)
     choose(sel[0], down_own.at[0], down_other.at[0], down_ref)
     d_out = dispatch(e, target_row, g_ref)
-    dout_ref[0] = d_out
+    half_ref[0, 0] = d_out
     d_up = (slope_ref[0] * dot(d_out, down_ref[...], 1, 1)).astype(BF)
-    dup_ref[0] = d_up
+    half_ref[0, 1] = d_up
     slots_ref[pl.ds(pl.multiple_of(e * CAP, CAP), CAP), :] = dot(d_up, up_ref[...], 1, 1).astype(
         BF
     )
 
-    @pl.when(e == EXPERTS - 1)
+    @pl.when(step == EXPERTS - 1)
     def _():
         combine(parts, rows, target_col, slots_ref, out_refs)
 
 
-def bwd_experts(select, target_row, target_col, gate, slope, up_pair, down_pair, g_parts):
+def bwd_experts(select, order, target_row, target_col, gate, slope, up_pair, down_pair, g_parts):
     parts = len(g_parts)
     rows = SEQ // parts
     hidden = up_pair[0].shape[2]
-    each = pl.BlockSpec((1, CAP, D), lambda e, sel: (e, 0, 0))
-    each_hidden = pl.BlockSpec((1, CAP, hidden), lambda e, sel: (e, 0, 0))
+    each_hidden = pl.BlockSpec((1, CAP, hidden), lambda i, sel, order: (i, 0, 0))
     outs = pl.pallas_call(
         functools.partial(bwd_experts_body, parts),
         grid_spec=pltpu.PrefetchScalarGridSpec(
-            num_scalar_prefetch=1,
+            num_scalar_prefetch=2,
             grid=(EXPERTS,),
             in_specs=[whole((1, SEQ)), whole((SEQ, 1)), whole((SEQ, 1)), each_hidden]
             + expert_specs((1, D, hidden))
             + expert_specs((1, hidden, D))
             + [whole((rows, D))] * parts,
-            out_specs=[each, each_hidden] + [whole((rows, D))] * parts,
+            out_specs=[half_spec(D)] + [whole((rows, D))] * parts,
             scratch_shapes=[
                 pltpu.VMEM((SEQ, D), BF),
                 pltpu.VMEM((SLOTS, D), BF),
@@ -697,20 +715,20 @@
                 pltpu.VMEM((hidden, D), BF),
             ],
         ),
-        out_shape=[in_hbm((EXPERTS, CAP, D), BF), in_hbm((EXPERTS, CAP, hidden), BF)]
-        + [shape((rows, D), BF)] * parts,
-        compiler_params=limit(44),
+        out_shape=[in_hbm((EXPERTS, 2, CAP, D), BF)] + [shape((rows, D), BF)] * parts,
+        compiler_params=limit(36),
         cost_estimate=cost(1.2e10, 3e7),
         name="bwd_experts",
     )(
         select,
+        order,
         target_row,
         target_col,
         gate,
         *[from_hbm(a) for a in (slope, *up_pair, *down_pair)],
         *g_parts,
     )
-    return outs[:2], list(outs[2:])
+    return outs[0], list(outs[1:])
 
 
 def norm_back(vector, gain, grad):
@@ -830,7 +848,23 @@
         compiler_params=limit(24),
         cost_estimate=cost(2e9, 6e6),
         name="middle_back",
-    )(g, combined, probs, target_col, router, mid, gain, xn, *y_parts, *w_parts)
+    )(
+        *[
+            from_hbm(a)
+            for a in (
+                g,
+                combined,
+                probs,
+                target_col,
+                router,
+                mid,
+                gain,
+                xn,
+                *y_parts,
+                *w_parts,
+            )
+        ]
+    )
     return outs[:4], list(outs[4:])
 
 
@@ -860,40 +894,29 @@
     )(d_mid, h, gain, *y_parts)
 
 
-def expert_grads_body(order, act, d_out, expert_in, d_up, send_ref, keep_ref):
-    del order
-    for place, out in enumerate((send_ref, keep_ref)):
-
-        @pl.when(pl.program_id(0) // (EXPERTS // 2) == place)
-        def _():
-            out[0, 0] = dot(act[0], d_out[0], 0, 0).astype(BF)
-            out[1, 0] = dot(expert_in[0], d_up[0], 0, 0).astype(BF)
-
-
-def expert_grads(order, act, d_out, expert_in, d_up):
-    half = EXPERTS // 2
-    hidden = act.shape[2]
-    values = (act, d_out, expert_in, d_up)
-    block = (2, 1, hidden, D)
+def expert_grads_body(fwd_own, fwd_other, bwd_own, bwd_other, out):
+    for kind in range(2):
+        total = dot(fwd_own[0, kind], bwd_own[0, kind], 0, 0)
+        total = total + dot(fwd_other[0, kind], bwd_other[0, kind], 0, 0)
+        out[kind, 0] = total.astype(BF)
+
+
+def expert_grads(values):
+    columns = values[0].shape[3]
+    block = (1, 2, CAP, columns)
+    own = pl.BlockSpec(block, lambda i: (i + HALF, 0, 0, 0))
+    other = pl.BlockSpec(block, lambda i: (i, 0, 0, 0))
     outs = pl.pallas_call(
         expert_grads_body,
-        grid_spec=pltpu.PrefetchScalarGridSpec(
-            num_scalar_prefetch=1,
-            grid=(EXPERTS,),
-            in_specs=[
-                pl.BlockSpec((1,) + a.shape[1:], lambda e, order: (order[e], 0, 0)) for a in values
-            ],
-            out_specs=[
-                pl.BlockSpec(block, lambda e, order: (0, jnp.minimum(e, half - 1), 0, 0)),
-                pl.BlockSpec(block, lambda e, order: (0, jnp.maximum(e - half, 0), 0, 0)),
-            ],
-        ),
-        out_shape=[in_hbm((2, half, hidden, D), BF)] * 2,
+        grid=(HALF,),
+        in_specs=[own, other, own, other],
+        out_specs=pl.BlockSpec((2, 1, columns, columns), lambda i: (0, i, 0, 0)),
+        out_shape=in_hbm((2, HALF, columns, columns), BF),
         compiler_params=limit(28),
         cost_estimate=cost(1e6, 1e5),
         name="expert_grads",
-    )(order, *[from_hbm(a) for a in values])
-    return [a.reshape(2 * half, hidden, D) for a in outs]
+    )(from_hbm(values[0]), from_hbm(values[1]), from_hbm(values[2]), values[3])
+    return outs.reshape(2 * HALF, columns, columns)
 
 
 def out_grads_body(parts, *refs):
@@ -916,42 +939,70 @@
     )(*pieces, d_a)
 
 
-def attention_grads_body(parts, chunks, paired, place, xn_ref, proj_ref, *refs):
-    terms, refs = refs[:parts], refs[parts:]
-    out = refs[-1]
+def attention_grads_body(parts, chunks, place, xn_ref, proj_ref, *refs):
+    terms, (send_ref, keep_ref, out) = refs[:parts], refs[parts:]
     wide = terms[0].shape[0]
     rows, taken = D // chunks, wide // chunks
-    out[0, :, : 3 * wide] = dot(xn_ref[...], proj_ref[...], 0, 0).astype(out.dtype)
+    out[:, : 3 * wide] = dot(xn_ref[...], proj_ref[...], 0, 0)
     total = terms[0][...].astype(F32)
     for k in range(1, parts):
         total = total + terms[k][...].astype(F32)
     for c in range(chunks):
         for b in range(D // wide):
-            out[0, c * rows + b * taken : c * rows + (b + 1) * taken, 3 * wide :] = total[
+            out[c * rows + b * taken : c * rows + (b + 1) * taken, 3 * wide :] = total[
                 c * taken : (c + 1) * taken, b * wide : (b + 1) * wide
-            ].astype(out.dtype)
-    if paired:
-        other, keep, sent = refs[:3]
-        first = place[1] == 0
-        keep[...] = jnp.where(first, out[...].astype(F32), other[...].astype(F32)).astype(BF)
-        sent[...] = jnp.where(first, other[...].astype(F32), out[...].astype(F32)).astype(BF)
-
-
-def attention_grads(place, xn, proj, terms, other):
+            ]
+    first = place[1] == 0
+    half = D // 2
+    left, right = out[:, :half], out[:, half:]
+    keep_ref[:, :half] = jnp.where(first, left, right).astype(BF)
+    send_ref[:, :half] = jnp.where(first, right, left).astype(BF)
+
+
+def attention_grads(place, xn, proj, terms):
     parts = len(terms)
-    paired = other is not None
-    array = shape((1, D, D), BF)
-    outs = pl.pallas_call(
-        functools.partial(attention_grads_body, parts, lax.axis_size("dp"), paired),
-        out_shape=[array] * (2 if paired else 1),
-        in_specs=[smem()] + vm(2 + parts + paired),
-        out_specs=vm(2 if paired else 1),
-        scratch_shapes=[pltpu.VMEM((1, D, D), F32)] if paired else [],
+    return pl.pallas_call(
+        functools.partial(attention_grads_body, parts, lax.axis_size("dp")),
+        out_shape=[shape((D, D // 2), BF)] * 2,
+        in_specs=[smem()] + vm(2 + parts),
+        out_specs=vm(2),
+        scratch_shapes=[pltpu.VMEM((D, D), F32)],
         compiler_params=limit(24),
         cost_estimate=cost(1e6, 1e5),
         name="attention_grads",
-    )(place, xn, proj, *terms, *([other] if paired else []))
-    return outs if paired else outs[0]
+    )(place, from_hbm(xn), from_hbm(proj), *terms)
+
+
+def chunks_body(count, place, own, received, *outs):
+    rows = outs[0].shape[0]
+    for k in range(count):
+        where = natural(place[3], k, rows)
+        total = own[where, :].astype(F32) + received[where, :].astype(F32)
+        outs[k][...] = total.astype(outs[k].dtype)
+
+
+def scatter_small(place, own, received):
+    count = lax.axis_size("dp")
+    if count != 4:
+        total = (own.astype(F32) + received.astype(F32)).astype(BF)
+        return [total]
+    dims = (own.shape[0] // count, own.shape[1])
+    return pl.pallas_call(
+        functools.partial(chunks_body, count),
+        out_shape=[shape(dims, F32)] + [shape(dims, BF)] * (count - 1),
+        in_specs=[smem()] + vm(2),
+        out_specs=vm(count),
+        compiler_params=limit(16),
+        cost_estimate=cost(1e6, 1e5),
+        name="chunks",
+    )(place, own, received)
+
+
+def scatter_end(chunks):
+    if len(chunks) == 1:
+        return lax.psum_scatter(chunks[0], "dp", scatter_dimension=0, tiled=True).astype(F32)
+    others = [exchange(chunk, "dp", k).astype(F32) for k, chunk in enumerate(chunks) if k]
+    return functools.reduce(jnp.add, others, chunks[0])
 
 
 def attention_results(value, wide):
@@ -965,128 +1016,8 @@
     )
 
 
-def shift(value, step):
-    count = lax.axis_size("dp")
-    return lax.ppermute(value, "dp", [(i, (i + step) % count) for i in range(count)])
-
-
-def ring_call(body, name, at, groups, inputs, outputs):
-    step = 2 if groups % 2 == 0 else 1
-    in_specs = []
-    for a, lead, entry in inputs:
-        size = a.shape[1] if entry is None else a.shape[1] // 4
-        in_specs.append(
-            pl.BlockSpec(
-                (step, size, a.shape[2]),
-                lambda i, at, lead=lead, entry=entry: (
-                    i + lead // step,
-                    0 if entry is None else at[entry],
-                    0,
-                ),
-            )
-        )
-    columns = inputs[0][0].shape[2]
-    return pl.pallas_call(
-        body,
-        grid_spec=pltpu.PrefetchScalarGridSpec(
-            num_scalar_prefetch=1,
-            grid=(groups // step,),
-            in_specs=in_specs,
-            out_specs=[
-                pl.BlockSpec((step, rows, columns), lambda i, at: (i, 0, 0)) for rows, _ in outputs
-            ],
-        ),
-        out_shape=[shape((groups, rows, columns), kind) for rows, kind in outputs],
-        compiler_params=limit(24),
-        cost_estimate=cost(1e6, 1e5),
-        name=name,
-    )(at, *[a for a, _, _ in inputs])
-
-
-def added(*refs):
-    return functools.reduce(jnp.add, [r[...].astype(F32) for r in refs])
-
-
-def ring_first_body(at, a, b, low, high):
-    total = added(a, b).astype(BF)
-    half = low.shape[1]
-    low[...] = total[:, :half]
-    high[...] = total[:, half:]
-
-
-def ring_first(at, terms):
-    if lax.axis_size("dp") != 4:
-        return []
-    size = terms[0].shape[1] // 4
-    inputs = [(a, 0, 0) for a in terms]
-    return ring_call(
-        ring_first_body, "ring_first", at, terms[0].shape[0], inputs, [(size // 2, BF)] * 2
-    )
-
-
-def ring_second_body(at, a, b, c, d, ahead, behind, low, high):
-    half = ahead.shape[1]
-    total = added(a, b)
-    low[:, :half] = (total[:, :half] + ahead[...].astype(F32)).astype(BF)
-    low[:, half:] = total[:, half:].astype(BF)
-    total = added(c, d)
-    high[:, :half] = total[:, :half].astype(BF)
-    high[:, half:] = (total[:, half:] + behind[...].astype(F32)).astype(BF)
-
-
-def ring_second(at, terms, arrived, lead, groups):
-    if not arrived:
-        return []
-    size = terms[0].shape[1] // 4
-    inputs = [(a, lead, entry) for entry in (1, 2) for a in terms]
-    inputs += [(a, lead, None) for a in arrived]
-    return ring_call(ring_second_body, "ring_second", at, groups, inputs, [(size, BF)] * 2)
-
-
-def ring_move(sent):
-    return [shift(a, step) for a, step in zip(sent, (1, -1))]
-
-
-def scattered(terms, lead, groups):
-    total = functools.reduce(jnp.add, [a[lead : lead + groups].astype(F32) for a in terms])
-    return lax.psum_scatter(total.astype(BF), "dp", scatter_dimension=1, tiled=True).astype(F32)
-
-
-def ring_end_body(at, a, b, c, d, out):
-    out[...] = added(a, b, c, d)
-
-
-def ring_end(at, terms, arrived):
-    groups = terms[0].shape[0]
-    if not arrived:
-        return scattered(terms, 0, groups)
-    inputs = [(a, 0, 3) for a in terms] + [(a, 0, None) for a in arrived]
-    return ring_call(
-        ring_end_body, "ring_end", at, groups, inputs, [(terms[0].shape[1] // 4, F32)]
-    )[0]
-
-
-def ring_ends_body(at, *refs):
-    keep, sent = refs[8:]
-    sums = [added(*refs[:4]), added(*refs[4:8])]
-    first = at[4] == 0
-    keep[...] = jnp.where(first, sums[0], sums[1])
-    sent[...] = jnp.where(first, sums[1], sums[0]).astype(BF)
-
-
-def ring_ends(at, terms, arrived, lead, groups):
-    if not arrived[0]:
-        sums = [scattered(a, lead, groups) for a in terms]
-        first = at[4] == 0
-        return (
-            jnp.where(first, sums[0], sums[1]),
-            jnp.where(first, sums[1], sums[0]).astype(BF),
-        )
-    inputs = []
-    for layer in range(2):
-        inputs += [(a, lead, 3) for a in terms[layer]] + [(a, 0, None) for a in arrived[layer]]
-    size = terms[0][0].shape[1] // 4
-    return ring_call(ring_ends_body, "ring_ends", at, groups, inputs, [(size, F32), (size, BF)])
+def scatter_sum(value, dim):
+    return lax.psum_scatter(value, "dp", scatter_dimension=dim, tiled=True)
 
 
 def phase(*values):
@@ -1140,11 +1071,9 @@
     h0 = mine(inputs)
     g1 = mine(cotangent)
     place = [
-        jnp.stack([t, s, jnp.where(s == layer, 0, 1)]).astype(jnp.int32) for layer in range(2)
+        jnp.stack([t, s, jnp.where(s == layer, 0, 1), z]).astype(jnp.int32) for layer in range(2)
     ]
-    selects = [place[layer][2:] for layer in range(2)]
-    dp_size = lax.axis_size("dp")
-    at = jnp.stack([(z + i) % dp_size for i in (2, 1, 3, 0)] + [s]).astype(jnp.int32)
+    selects = [place[layer][2:3] for layer in range(2)]
     order = jnp.where(first, jnp.array([2, 3, 0, 1]), jnp.array([0, 1, 2, 3])).astype(jnp.int32)
     hot = diagonal_one_hot()
     hot_rows = hot.transpose(2, 0, 1).reshape(BUCKETS, -1)
@@ -1210,14 +1139,17 @@
         else:
             xn_parts, g1 = phase(xn_parts, g1)
         row, col, router = targets[layer::2]
-        ex, y_parts = fwd_experts(selects[layer], row, col, router, up_pair, down_pair, xn_parts)
-        saved.append([kept, pieces, mid, xn_mid, ex])
+        ex, y_parts = fwd_experts(
+            selects[layer], order, row, col, router, up_pair, down_pair, xn_parts
+        )
         if layer == 0:
             w_out_parts.append(gather_parts(w_out[1]))
-            y_parts, w_out_parts[1] = phase(y_parts, w_out_parts[1])
+            y_parts, w_out_parts[1], ex = phase(y_parts, w_out_parts[1], ex)
             y_parts = swap_parts(y_parts)
+            fwd_sent = [ex[0]]
+            saved.append([kept, pieces, mid, xn_mid, ex])
             combined, out, xn_next, stat_more = after_experts(
-                mid, ex[3], gains[1], valid_own, y_parts
+                mid, ex[2], gains[1], valid_own, y_parts
             )
             outputs.append(out)
             stats.append((stat, stat_more))
@@ -1227,37 +1159,39 @@
         else:
             g_parts.append(exchange(g1, "tensor", tensor - 1))
             y_parts, g_parts, ex = phase(y_parts, g_parts, ex)
+            fwd_sent.append(ex[0])
+            saved.append([kept, pieces, mid, xn_mid, ex])
 
     fwd_y_parts = y_parts
-    half = EXPERTS // 2
-    small_1 = square_1 = None
+    small_1, square_1, expert_sums = None, [], []
     for layer in (1, 0):
         row, col, router = targets[layer::2]
         kept, pieces, mid, xn_mid, ex = saved[layer][:5]
-        expert_in, act, slope, gate, probs = ex
+        fwd_halves, slope, gate, probs = ex
         g = g_parts[0]
-        (d_out, d_up), y_parts = bwd_experts(
-            selects[layer], row, col, gate, slope, up_pair, down_pair, g_parts
+        bwd_halves, y_parts = bwd_experts(
+            selects[layer], order, row, col, gate, slope, up_pair, down_pair, g_parts
         )
+        fwd_other = swap(fwd_sent[layer])
         if layer == 1:
-            fwd_y_parts = swap_parts(fwd_y_parts)
-            y_parts, d_out, d_up, fwd_y_parts = phase(y_parts, d_out, d_up, fwd_y_parts)
+            y_parts, bwd_halves, fwd_y_parts, fwd_other = phase(
+                y_parts, bwd_halves, swap_parts(fwd_y_parts), fwd_other
+            )
             combined, out, _, stat_more = after_experts(
                 mid, gate, gains[1], valid_own, fwd_y_parts
             )
             outputs.append(out)
             stats.append((stat, stat_more))
         else:
-            y_parts, d_out, d_up, out_terms_1, up_ring_1 = phase(
-                y_parts, d_out, d_up, swap_parts(out_terms), ring_move(up_ring_1)
+            y_parts, bwd_halves, fwd_other, square_1 = phase(
+                y_parts, bwd_halves, fwd_other, scatter_end(square_1)
             )
             combined = saved[0][5]
-            square_1 = attention_grads(place[1], saved[1][0][0], d_proj, out_terms_1, None)
-
-        sent, keep = expert_grads(order, act, d_out, expert_in, d_up)
-        y_parts, sent, keep, combined, square_1 = phase(
-            swap_parts(y_parts), sent, keep, combined, square_1
-        )
+
+        total = expert_grads((fwd_halves, fwd_other, bwd_halves, swap(bwd_halves)))
+        y_parts, total, combined = phase(swap_parts(y_parts), total, combined)
+        if layer == 0 or 'wa' == "wa":
+            expert_sums.append(scatter_sum(total, 1))
 
         (d_mid, d_a, grad_gain_mid, grad_router), d_pieces = middle_back(
             g,
@@ -1271,11 +1205,7 @@
             y_parts,
             w_out_parts[layer],
         )
-        d_pieces = swap_parts(d_pieces)
-        out_terms = out_grads(pieces, d_a)
-        terms = (keep, swap(sent))
-        ring = ring_first(at, terms)
-        d_pieces, out_terms, ring, terms = phase(d_pieces, out_terms, ring, terms)
+        d_pieces, out_terms = phase(swap_parts(d_pieces), out_grads(pieces, d_a))
 
         xn, qkv, turned, lse = kept
         (d_proj, diag, far, grad_gain_in), x_terms = bwd_attention(
@@ -1288,18 +1218,12 @@
             (xn, qkv, turned, lse),
             d_pieces,
         )
-        if layer == 0:
-            out_terms = swap_parts(out_terms)
-        x_terms, ring, d_proj, diag, far, out_terms = phase(
-            x_terms, ring_move(ring), d_proj, diag, far, out_terms
+        x_terms, d_proj, diag, far, out_terms = phase(
+            x_terms, d_proj, diag, far, swap_parts(out_terms)
         )
 
-        down_ring = ring_second(at, terms, ring, 0, half)
-        up_ring = ring_second(at, terms, ring, half, half)
-        if layer == 0:
-            x_terms, down_ring = phase(x_terms, down_ring)
-            down_ring = ring_move(down_ring)
         x_terms = swap_parts(x_terms)
+        sent, square = attention_grads(place[layer], xn, d_proj, out_terms)
         small = small_sums(
             place[0],
             diag,
@@ -1312,46 +1236,45 @@
             small_1,
         )
         if layer == 1:
-            x_terms, down_ring, up_ring_1, small_1 = phase(x_terms, down_ring, up_ring, small)
+            x_terms, small_1, sent, square = phase(x_terms, small, sent, square)
             d_h_1, d_h_low = input_back(d_mid, hidden[1], gains[1], x_terms)
-            g_parts = gather_parts(d_h_low)
-            g_parts, down_ring_1, out_terms = phase(g_parts, ring_move(down_ring), out_terms)
-            d_h_1, terms_1 = d_h_low, terms
+            g_parts, square_1 = phase(
+                gather_parts(d_h_low), scatter_small(place[1], square, swap(sent))
+            )
+            d_h_1 = d_h_low
 
     def kept_sent(values):
         return jnp.where(first, values[0], values[1]), jnp.where(first, values[1], values[0])
 
-    def placed(own, received):
+    def placed(own, received, axis=0):
         return jnp.where(
             first,
-            jnp.concatenate([own, received], axis=0),
-            jnp.concatenate([received, own], axis=0),
+            jnp.concatenate([own, received], axis=axis),
+            jnp.concatenate([received, own], axis=axis),
         )
 
-    square, sent = attention_grads(place[0], xn, d_proj, out_terms, square_1)
-    x_terms, down_ring, up_ring, square, small = phase(
-        x_terms, down_ring, up_ring, (square, swap(sent)), (small[0], swap(small[1]))
-    )
+    x_terms, square, sent, small = phase(x_terms, square, sent, small)
 
     d_h = input_back(d_mid, hidden[0], gains[0], x_terms)[0]
-    square_ring = ring_move(ring_first(at, square))
+    out_keep, out_sent = kept_sent(outputs)
+    d_h_keep, d_h_sent = kept_sent((d_h, d_h_1.astype(F32)))
+    out_moved, d_h_moved, small, square = phase(
+        swap(out_sent),
+        swap(d_h_sent.astype(BF)),
+        (small[0], swap(small[1])),
+        scatter_small(place[0], square, swap(sent)),
+    )
     small = small[0] + small[1]
-    shared = sum_small(small[:8], "tensor")
-    out_keep, sent = kept_sent(outputs)
-    d_h_keep, d_h_sent = kept_sent((d_h, d_h_1.astype(F32)))
-    up_ring, square_ring, shared, out_moved, d_h_moved = phase(
-        ring_move(up_ring), square_ring, shared, swap(sent), swap(d_h_sent.astype(BF))
-    )
-
+    small, shared, square_0 = phase(small, sum_small(small[:8], "tensor"), scatter_end(square))
     small = sum_small(jnp.concatenate([shared, small[8:]], axis=0), "dp")
-    square_ring = ring_move(ring_second(at, square, square_ring, 0, 1))
-    grad_w_in, grad_w_out = attention_results(ring_end(at, square, square_ring)[0], wide)
+
     layer_out = placed(out_keep[None], out_moved[None])
     input_grad = placed(d_h_keep[None], d_h_moved.astype(F32)[None])
-    expert_results = []
-    for lead, ring_0, ring_1 in ((0, down_ring, down_ring_1), (half, up_ring, up_ring_1)):
-        keep, sent = ring_ends(at, (terms, terms_1), (ring_0, ring_1), lead, half)
-        expert_results.append(placed(keep, swap(sent).astype(F32)))
+    keep, sent = kept_sent((square_0, square_1))
+    square = placed(keep, swap(sent.astype(BF)).astype(F32), axis=1)
+    grad_w_in, grad_w_out = attention_results(square, wide)
+    keep, sent = kept_sent(expert_sums[::-1])
+    experts = placed(*[a.astype(F32).reshape(2, HALF, -1, D) for a in (keep, swap(sent))], axis=1)
     table = small[8 : 8 + heads, :BUCKETS].T
     share = BUCKETS // lax.axis_size("dp")
     stat = small[6]
@@ -1364,8 +1287,8 @@
         grad_w_out[None],
         lax.dynamic_slice_in_dim(table, z * share, share, 0)[None],
         small[2:6].T[None],
-        expert_results[1][None],
-        expert_results[0][None],
+        experts[1][None],
+        experts[0][None],
         root_means[None],
     )
 

time: 511 us -> 489 us (0.957)
  starting transfers between devices: 111 us -> 91.8 us
  between operations: 3.53 us -> 16.5 us
  Pallas kernels: 187 us -> 178 us
  waiting for transfers between devices: 165 us -> 159 us
    ppermute x16 -> x0, waiting for transfers between devices: 37.8 us -> none  [shift(): lax.ppermute(value, 'dp', [(i, (i + step) % count) for i in range(count)])]
    ppermute x82 -> x91, waiting for transfers between devices: 127 us -> 159 us  [exchange(): return lax.ppermute(value, axis, [(i, i ^ mask) for i in range(count)])]
    ppermute x16 -> x0, starting transfers between devices: 27.7 us -> none  [shift(): lax.ppermute(value, 'dp', [(i, (i + step) % count) for i in range(count)])]
    pallas_call x15 -> x6, Pallas kernels: 75.1 us -> 55.1 us  [the longest x2 36.6 us: bwd_attention(): pl.pallas_call(functools.partial(bwd_attention_body, parts), out_shape=[i...]
    ppermute x82 -> x91, starting transfers between devices: 83 us -> 91.7 us  [exchange(): return lax.ppermute(value, axis, [(i, i ^ mask) for i in range(count)])]
    unnamed x269 -> x221, local copies, waits for them, and re-layouts: 26.6 us -> 20.1 us
    pallas_call x2, Pallas kernels: 3.16 us -> 8.52 us  [middle_back(): pl.pallas_call(functools.partial(middle_back_body, parts), out_shape=[sha...]
  transfers between devices with their start and end apart: 98 -> 93, of which waited for: 36 -> 43; matrix products, arithmetic and copies ran while one was open for 3% -> 4% of each run, Pallas kernels for 36% -> 36%
where the time goes in v2:
time: 489 us; the launch traced here: 484 us
  Pallas kernels  178 us (36%)
  waiting for transfers between devices  159 us (33%)
  starting transfers between devices  91.8 us (19%)
  local copies, waits for them, and re-layouts  24.9 us (5%)
  between operations  16.5 us (3%)
  other arithmetic  13.7 us (3%)
    ppermute x91, waiting for transfers between devices, exchange(): return lax.ppermute(value, axis, [(i, i ^ mask) for i in range(count)])  159 us
    ppermute x91, starting transfers between devices, exchange(): return lax.ppermute(value, axis, [(i, i ^ mask) for i in range(count)])  91.7 us
    pallas_call x2, Pallas kernels, bwd_attention(): pl.pallas_call(functools.partial(bwd_attention_body, parts), out_shape=[i...  36.6 us
    pallas_call x2, Pallas kernels, fwd_experts(): pl.pallas_call(functools.partial(fwd_experts_body, parts), grid_spec=pltp...  33.3 us
    pallas_call x2, Pallas kernels, bwd_experts(): pl.pallas_call(functools.partial(bwd_experts_body, parts), grid_spec=pltp...  30.9 us
    pallas_call x2, Pallas kernels, fwd_attention(): pl.pallas_call(functools.partial(fwd_attention_body, parts, norm_inside),...  26.1 us
    unnamed x221, local copies, waits for them, and re-layouts  20.1 us
    pallas_call x2, Pallas kernels, expert_grads(): pl.pallas_call(expert_grads_body, grid=(HALF,), in_specs=[own, other, own...  17.1 us
  transfers between devices with their start and end apart: 93, of which 43 were waited for; matrix products, arithmetic and copies ran while one was open for 4% of the time, Pallas kernels for 36%

profile of v2, /device:TPU:0, one launch (start us, length us, event | category | flops | bytes accessed | tf_op | source)
XLA Modules:
  0.0 483.7 jit_solution(12364245564656233498)
XLA Ops:
  23.0 9.4 %collective-permute-done.1.refs_9_ = bf16[256,768]{1,0:T(8,128)(2,1)S(1)} collective-permute-done((bf16[256,768]{1,0:T(8,128)(2,1)S(1)}, bf16[256,768]{1,0:T(8,128)(2,1)S(1)}, u32[]{:S(2)}, u32[]{:S(2)}) %collective-permute-start.1) | collective-permute-done | bytes 393248 | tf_op jit(solution)/shard_map/ppermute | solution.py:84
  38.8 13.5 %fwd_attention.2 = (bf16[1024,768]{1,0:T(8,128)(2,1)}, bf16[3,3,1024,64]{3,2,1,0:T(8,128)(2,1)}, bf16[2,192,1024]{2,1,0:T(8,128)(2,1)}, f32[3,1,1024]{2,1,0:T(1,...) custom-call(s32[4]{0:T(128)S(1)} %add_add_fusion.2.place.refs_0_, ...), custom_call_target="tpu_custom_call" | custom-call | flops 8999999488 | bytes 10000000 | tf_op jit(solution)/shard_map/fwd_attention/pallas_call | solution.py:332
  69.1 4.7 collective-permute-done.15.refs_10_
  73.8 6.7 %collective-permute-done.16.refs_11_ = bf16[256,768]{1,0:T(8,128)(2,1)} collective-permute-done((bf16[256,768]{1,0:T(8,128)(2,1)S(1)}, bf16[256,768]{1,0:T(8,128)(2,1)}, u32[]{:S(2)}, u32[]{:S(2)}) %collective-permute-start.16) | collective-permute-done | bytes 393248 | tf_op jit(solution)/shard_map/ppermute | solution.py:84
  84.1 16.8 %fwd_experts.2 = (bf16[4,2,320,768]{3,2,1,0:T(8,128)(2,1)}, f32[4,320,768]{2,1,0:T(8,128)}, f32[1024,1]{1,0:T(8,128)S(1)}, f32[256,128]{1,0:T(8,128)S(1)}, bf16[...) custom-call(s32[1]{0:T(128)} %bitcast.3.refs_0_, ...), custom_call_target="tpu_custom_call" | custom-call | flops 12000000000 | bytes 30000000 | tf_op jit(solution)/shard_map/fwd_experts/pallas_call | solution.py:622
  108.0 8.3 %collective-permute-done.23.refs_5_ = bf16[256,768]{1,0:T(8,128)(2,1)S(1)} collective-permute-done((bf16[256,768]{1,0:T(8,128)(2,1)S(1)}, bf16[256,768]{1,0:T(8,128)(2,1)S(1)}, u32[]{:S(2)}, u32[]{:S(2)}) %collective-permute-start.23) | collective-permute-done | bytes 393248 | tf_op jit(solution)/shard_map/ppermute | solution.py:84
  116.3 5.3 %collective-permute-done.24.refs_6_ = bf16[256,768]{1,0:T(8,128)(2,1)S(1)} collective-permute-done((bf16[256,768]{1,0:T(8,128)(2,1)S(1)}, bf16[256,768]{1,0:T(8,128)(2,1)S(1)}, u32[]{:S(2)}, u32[]{:S(2)}) %collective-permute-start.24) | collective-permute-done | bytes 393248 | tf_op jit(solution)/shard_map/ppermute | solution.py:84
  128.9 5.5 %collective-permute-done.26.refs_8_ = bf16[256,768]{1,0:T(8,128)(2,1)S(1)} collective-permute-done((bf16[256,768]{1,0:T(8,128)(2,1)S(1)}, bf16[256,768]{1,0:T(8,128)(2,1)S(1)}, u32[]{:S(2)}, u32[]{:S(2)}) %collective-permute-start.26) | collective-permute-done | bytes 393248 | tf_op jit(solution)/shard_map/ppermute | solution.py:84
  134.4 7.7 %collective-permute-done.27.refs_9_ = bf16[256,768]{1,0:T(8,128)(2,1)S(1)} collective-permute-done((bf16[256,768]{1,0:T(8,128)(2,1)S(1)}, bf16[256,768]{1,0:T(8,128)(2,1)S(1)}, u32[]{:S(2)}, u32[]{:S(2)}) %collective-permute-start.27) | collective-permute-done | bytes 393248 | tf_op jit(solution)/shard_map/ppermute | solution.py:84
  142.1 12.6 %fwd_attention.3 = (bf16[1024,768]{1,0:T(8,128)(2,1)}, bf16[3,3,1024,64]{3,2,1,0:T(8,128)(2,1)}, bf16[2,192,1024]{2,1,0:T(8,128)(2,1)}, f32[3,1,1024]{2,1,0:T(1,...) custom-call(s32[4]{0:T(128)S(1)} %add_add_fusion.3.place.refs_0_, ...), custom_call_target="tpu_custom_call" | custom-call | flops 8999999488 | bytes 10000000 | tf_op jit(solution)/shard_map/fwd_attention/pallas_call | solution.py:332
  160.5 5.8 %collective-permute-done.32.refs_5_.refs_2_ = bf16[192,256]{1,0:T(8,128)(2,1)S(1)} collective-permute-done((bf16[192,256]{1,0:T(8,128)(2,1)S(1)}, bf16[192,256]{1,0:T(8,128)(2,1)S(1)}, u32[]{:S(2)}, u32[]{:S(2)}) %collective-permute-start.32) | collective-permute-done | bytes 98336 | tf_op jit(solution)/shard_map/ppermute | solution.py:84
  171.3 6.0 %collective-permute-done.34.refs_10_ = bf16[256,768]{1,0:T(8,128)(2,1)S(1)} collective-permute-done((bf16[256,768]{1,0:T(8,128)(2,1)S(1)}, bf16[256,768]{1,0:T(8,128)(2,1)S(1)}, u32[]{:S(2)}, u32[]{:S(2)}) %collective-permute-start.34) | collective-permute-done | bytes 393248 | tf_op jit(solution)/shard_map/ppermute | solution.py:84
  177.3 5.3 %collective-permute-done.35.refs_11_ = bf16[256,768]{1,0:T(8,128)(2,1)S(1)} collective-permute-done((bf16[256,768]{1,0:T(8,128)(2,1)S(1)}, bf16[256,768]{1,0:T(8,128)(2,1)S(1)}, u32[]{:S(2)}, u32[]{:S(2)}) %collective-permute-start.35) | collective-permute-done | bytes 393248 | tf_op jit(solution)/shard_map/ppermute | solution.py:84
  183.9 16.5 %fwd_experts.3 = (bf16[4,2,320,768]{3,2,1,0:T(8,128)(2,1)}, f32[4,320,768]{2,1,0:T(8,128)}, f32[1024,1]{1,0:T(8,128)S(1)}, f32[256,128]{1,0:T(8,128)S(1)}, bf16[...) custom-call(s32[1]{0:T(128)} %bitcast.18.refs_0_, ...), custom_call_target="tpu_custom_call" | custom-call | flops 12000000000 | bytes 30000000 | tf_op jit(solution)/shard_map/fwd_experts/pallas_call | solution.py:622
  204.6 15.5 %bwd_experts.2 = (bf16[4,2,320,768]{3,2,1,0:T(8,128)(2,1)}, bf16[256,768]{1,0:T(8,128)(2,1)S(1)}, bf16[256,768]{1,0:T(8,128)(2,1)S(1)}, bf16[256,768]{1,0:T(8,128)(2,1)S(1)}, bf16[256,768]{1,0:T(8,128)(2,1)S(1)}) custom-call(s32[1]{0:T(128)} %bitcast.18.refs_0_, s32[4]{0:T(128)S(1)} %broadcast_select_fusion.6.refs_1_, ...), custom_call_target="tpu_custom_call" | custom-call | flops 12000000000 | bytes 30000000 | tf_op jit(solution)/shard_map/bwd_experts/pallas_call | solution.py:701
  228.6 8.5 %expert_grads.2 = bf16[2,2,768,768]{3,2,1,0:T(8,128)(2,1)} custom-call(bf16[4,2,320,768]{3,2,1,0:T(8,128)(2,1)} %get-tuple-element.462.fwd_own, bf16[4,2,320,768]{3,2,1,0:T(8,128)(2,1)} %copy-done.98, bf16[4,2,320,768]{3,2,1,0:T(8,128)(2,1)} %get-tuple-element.473.bwd_own, bf16[4,2,320,768]{3,2,1,0:T(8,128)(2,1)S(1)} %collective-permute-done.46.bwd_other), custom_call_target="tpu_custom_call" | custom-call | flops 1000000 | bytes 100000 | tf_op jit(solution)/shard_map/expert_grads/pallas_call | solution.py:909
  237.2 3.8 collective-permute-done.44.refs_10_
  243.4 4.3 middle_back.2
  261.4 18.3 %bwd_attention.2 = (bf16[1024,576]{1,0:T(8,128)(2,1)}, f32[18,128,128]{2,1,0:T(8,128)}, f32[3,8,256]{2,1,0:T(8,128)S(1)}, f32[1,768]{1,0:T(1,128)S(1)}, bf16[256...) custom-call(s32[4]{0:T(128)S(1)} %add_add_fusion.3.place.refs_0_, ...), custom_call_target="tpu_custom_call" | custom-call | flops 17999998976 | bytes 10000000 | tf_op jit(solution)/shard_map/bwd_attention/pallas_call | solution.py:443
  292.1 4.2 collective-permute-done.54.refs_5_
  302.6 7.7 %collective-permute-done.56.refs_11_ = bf16[256,768]{1,0:T(8,128)(2,1)S(1)} collective-permute-done((bf16[256,768]{1,0:T(8,128)(2,1)S(1)}, bf16[256,768]{1,0:T(8,128)(2,1)S(1)}, u32[]{:S(2)}, u32[]{:S(2)}) %collective-permute-start.56) | collective-permute-done | bytes 393248 | tf_op jit(solution)/shard_map/ppermute | solution.py:84
  310.3 7.6 %collective-permute-done.57.refs_12_ = bf16[256,768]{1,0:T(8,128)(2,1)S(1)} collective-permute-done((bf16[256,768]{1,0:T(8,128)(2,1)S(1)}, bf16[256,768]{1,0:T(8,128)(2,1)S(1)}, u32[]{:S(2)}, u32[]{:S(2)}) %collective-permute-start.57) | collective-permute-done | bytes 393248 | tf_op jit(solution)/shard_map/ppermute | solution.py:84
  319.4 3.5 collective-permute-start.63
  323.8 15.4 %bwd_experts.3 = (bf16[4,2,320,768]{3,2,1,0:T(8,128)(2,1)}, bf16[256,768]{1,0:T(8,128)(2,1)S(1)}, bf16[256,768]{1,0:T(8,128)(2,1)S(1)}, bf16[256,768]{1,0:T(8,128)(2,1)S(1)}, bf16[256,768]{1,0:T(8,128)(2,1)S(1)}) custom-call(s32[1]{0:T(128)} %bitcast.3.refs_0_, s32[4]{0:T(128)S(1)} %copy-done.84, s32[1,1024]{1,0:T(1,128)S(1)} %copy-done.79, ...), custom_call_target="tpu_custom_call" | custom-call | flops 12000000000 | bytes 30000000 | tf_op jit(solution)/shard_map/bwd_experts/pallas_call | solution.py:701
  346.6 3.4 collective-permute-done.67.bwd_other
  350.0 8.6 %expert_grads.3 = bf16[2,2,768,768]{3,2,1,0:T(8,128)(2,1)} custom-call(bf16[4,2,320,768]{3,2,1,0:T(8,128)(2,1)} %get-tuple-element.549.fwd_own, bf16[4,2,320,768]{3,2,1,0:T(8,128)(2,1)} %copy-done.97, bf16[4,2,320,768]{3,2,1,0:T(8,128)(2,1)} %get-tuple-element.559.bwd_own, bf16[4,2,320,768]{3,2,1,0:T(8,128)(2,1)S(1)} %collective-permute-done.67.bwd_other), custom_call_target="tpu_custom_call" | custom-call | flops 1000000 | bytes 100000 | tf_op jit(solution)/shard_map/expert_grads/pallas_call | solution.py:909
  358.6 5.5 %collective-permute-done.65.refs_10_ = bf16[256,768]{1,0:T(8,128)(2,1)S(1)} collective-permute-done((bf16[256,768]{1,0:T(8,128)(2,1)S(1)}, bf16[256,768]{1,0:T(8,128)(2,1)S(1)}, u32[]{:S(2)}, u32[]{:S(2)}) %collective-permute-start.65) | collective-permute-done | bytes 393248 | tf_op jit(solution)/shard_map/ppermute | solution.py:84
  365.8 4.3 middle_back.3
  383.2 18.3 %bwd_attention.3 = (bf16[1024,576]{1,0:T(8,128)(2,1)}, f32[18,128,128]{2,1,0:T(8,128)}, f32[3,8,256]{2,1,0:T(8,128)S(1)}, f32[1,768]{1,0:T(1,128)S(1)}, bf16[256...) custom-call(s32[4]{0:T(128)S(1)} %add_add_fusion.2.place.refs_0_, ...), custom_call_target="tpu_custom_call" | custom-call | flops 17999998976 | bytes 10000000 | tf_op jit(solution)/shard_map/bwd_attention/pallas_call | solution.py:443
  413.9 5.9 %collective-permute-done.75.refs_5_ = bf16[256,768]{1,0:T(8,128)(2,1)S(1)} collective-permute-done((bf16[256,768]{1,0:T(8,128)(2,1)}, bf16[256,768]{1,0:T(8,128)(2,1)S(1)}, u32[]{:S(2)}, u32[]{:S(2)}) %collective-permute-start.75) | collective-permute-done | bytes 393248 | tf_op jit(solution)/shard_map/ppermute | solution.py:84
  439.6 17.6 %collective-permute-done.84 = bf16[192,384]{1,0:T(8,128)(2,1)S(1)} collective-permute-done((bf16[192,384]{1,0:T(8,128)(2,1)S(1)}, bf16[192,384]{1,0:T(8,128)(2,1)S(1)}, u32[]{:S(2)}, u32[]{:S(2)}) %collective-permute-start.84) | collective-permute-done | bytes 147488 | tf_op jit(solution)/shard_map/ppermute | solution.py:84
  461.4 3.6 collective-permute-done.87
  (445 shorter events, 187.1 us)
Async XLA Ops:
  7.2 460.0 %reduce-scatter.5.cloned.1.call-start = ((), (), s32[]{:S(2)}) async-start(), calls=%async_computation.3 | async-start | bytes 5898240 | tf_op jit(solution)/shard_map/reduce_scatter | solution.py:1020
  7.2 25.9 %collective-permute-start.5 = (bf16[576,768]{1,0:T(8,128)(2,1)}, bf16[576,768]{1,0:T(8,128)(2,1)S(1)}, u32[]{:S(2)}, u32[]{:S(2)}) collective-permute-start(bf16[576,768]{1,0:T(8,128)(2,1)} %bitcast.76), channel_id=1, source_target_pairs={{0,16},{16,0},{1,17},{17,1},{2,18},{18,2},{3,19},{19,3},{4,20},{20... | collective-permute-start | bytes 2654216 | tf_op jit(solution)/shard_map/ppermute | solution.py:84
  13.1 19.3 %collective-permute-start.1 = (bf16[256,768]{1,0:T(8,128)(2,1)S(1)}, bf16[256,768]{1,0:T(8,128)(2,1)S(1)}, u32[]{:S(2)}, u32[]{:S(2)}) collective-permute-start(bf16[256,768]{1,0:T(8,128)(2,1)S(1)} %dynamic-slice_bitcast_fusion.1.refs_7_.refs_0_.refs_1_), channel_id=1, source_target_pairs={{0,8},{4,12},{8,0},{12,4},{1,9},{5,13},{9,1},{13,5},{2,10},{6,14},... | collective-permute-start | bytes 1179656 | tf_op jit(solution)/shard_map/ppermute | solution.py:84
  33.1 47.4 %collective-permute-start.18 = (bf16[4,768,768]{2,1,0:T(8,128)(2,1)}, bf16[4,768,768]{2,1,0:T(8,128)(2,1)}, u32[]{:S(2)}, u32[]{:S(2)}) collective-permute-start(bf16[4,768,768]{2,1,0:T(8,128)(2,1)} %bitcast.86), channel_id=1, source_target_pairs={{0,16},{16,0},{1,17},{17,1},{2,18},{18,2},{3,19},{19,3},{4,20},{20... | collective-permute-start | bytes 14155784 | tf_op jit(solution)/shard_map/ppermute | solution.py:84
  33.1 47.4 %collective-permute-start.19 = (bf16[4,768,768]{2,1,0:T(8,128)(2,1)}, bf16[4,768,768]{2,1,0:T(8,128)(2,1)}, u32[]{:S(2)}, u32[]{:S(2)}) collective-permute-start(bf16[4,768,768]{2,1,0:T(8,128)(2,1)} %bitcast.91), channel_id=1, source_target_pairs={{0,16},{16,0},{1,17},{17,1},{2,18},{18,2},{3,19},{19,3},{4,20},{20... | collective-permute-start | bytes 14155784 | tf_op jit(solution)/shard_map/ppermute | solution.py:84
  33.6 19.4 %collective-permute-start.9 = (bf16[192,768]{1,0:T(8,128)(2,1)S(1)}, bf16[192,768]{1,0:T(8,128)(2,1)S(1)}, u32[]{:S(2)}, u32[]{:S(2)}) collective-permute-start(bf16[192,768]{1,0:T(8,128)(2,1)S(1)} %get-tuple-element.351.refs_7_.refs_12_), channel_id=1, source_target_pairs={{0,4},{4,0},{8,12},{12,8},{1,5},{5,1},{9,13},{13,9},{2,6},{6,2},{1... | collective-permute-start | bytes 884744 | tf_op jit(solution)/shard_map/ppermute | solution.py:84
  80.5 23.9 %collective-permute-start.20 = (bf16[192,768]{1,0:T(8,128)(2,1)S(1)}, bf16[192,768]{1,0:T(8,128)(2,1)S(1)}, u32[]{:S(2)}, u32[]{:S(2)}) collective-permute-start(bf16[192,768]{1,0:T(8,128)(2,1)S(1)} %get-tuple-element.422.refs_7_.refs_12_), channel_id=1, source_target_pairs={{0,4},{4,0},{8,12},{12,8},{1,5},{5,1},{9,13},{13,9},{2,6},{6,2},{1... | collective-permute-start | bytes 884744 | tf_op jit(solution)/shard_map/ppermute | solution.py:84
  81.3 23.1 %collective-permute-start.21 = (bf16[192,768]{1,0:T(8,128)(2,1)S(1)}, bf16[192,768]{1,0:T(8,128)(2,1)S(1)}, u32[]{:S(2)}, u32[]{:S(2)}) collective-permute-start(bf16[192,768]{1,0:T(8,128)(2,1)S(1)} %get-tuple-element.422.refs_7_.refs_12_), channel_id=1, source_target_pairs={{0,8},{4,12},{8,0},{12,4},{1,9},{5,13},{9,1},{13,5},{2,10},{6,14},... | collective-permute-start | bytes 884744 | tf_op jit(solution)/shard_map/ppermute | solution.py:84
  82.6 21.8 %collective-permute-start.22 = (bf16[192,768]{1,0:T(8,128)(2,1)S(1)}, bf16[192,768]{1,0:T(8,128)(2,1)S(1)}, u32[]{:S(2)}, u32[]{:S(2)}) collective-permute-start(bf16[192,768]{1,0:T(8,128)(2,1)S(1)} %get-tuple-element.422.refs_7_.refs_12_), channel_id=1, source_target_pairs={{0,12},{4,8},{8,4},{12,0},{1,13},{5,9},{9,5},{13,1},{2,14},{6,10},... | collective-permute-start | bytes 884744 | tf_op jit(solution)/shard_map/ppermute | solution.py:84
  123.5 18.6 %collective-permute-start.27 = (bf16[256,768]{1,0:T(8,128)(2,1)S(1)}, bf16[256,768]{1,0:T(8,128)(2,1)S(1)}, u32[]{:S(2)}, u32[]{:S(2)}) collective-permute-start(bf16[256,768]{1,0:T(8,128)(2,1)S(1)} %get-tuple-element.413.refs_7_), channel_id=1, source_target_pairs={{0,8},{4,12},{8,0},{12,4},{1,9},{5,13},{9,1},{13,5},{2,10},{6,14},... | collective-permute-start | bytes 1179656 | tf_op jit(solution)/shard_map/ppermute | solution.py:84
  125.9 28.9 %collective-permute-start.29 = (bf16[256,768]{1,0:T(8,128)(2,1)S(1)}, bf16[256,768]{1,0:T(8,128)(2,1)S(1)}, u32[]{:S(2)}, u32[]{:S(2)}) collective-permute-start(bf16[256,768]{1,0:T(8,128)(2,1)S(1)} %dynamic-slice_bitcast_fusion.refs_10_.refs_0_), channel_id=1, source_target_pairs={{0,4},{4,0},{8,12},{12,8},{1,5},{5,1},{9,13},{13,9},{2,6},{6,2},{1... | collective-permute-start | bytes 1179656 | tf_op jit(solution)/shard_map/ppermute | solution.py:84
  127.1 27.6 %collective-permute-start.30 = (bf16[256,768]{1,0:T(8,128)(2,1)S(1)}, bf16[256,768]{1,0:T(8,128)(2,1)S(1)}, u32[]{:S(2)}, u32[]{:S(2)}) collective-permute-start(bf16[256,768]{1,0:T(8,128)(2,1)S(1)} %dynamic-slice_bitcast_fusion.refs_10_.refs_0_), channel_id=1, source_target_pairs={{0,8},{4,12},{8,0},{12,4},{1,9},{5,13},{9,1},{13,5},{2,10},{6,14},... | collective-permute-start | bytes 1179656 | tf_op jit(solution)/shard_map/ppermute | solution.py:84
  182.6 18.5 %collective-permute-start.37 = (bf16[256,768]{1,0:T(8,128)(2,1)S(1)}, bf16[256,768]{1,0:T(8,128)(2,1)S(1)}, u32[]{:S(2)}, u32[]{:S(2)}) collective-permute-start(bf16[256,768]{1,0:T(8,128)(2,1)S(1)} %dynamic-slice_bitcast_fusion.refs_10_.refs_0_), channel_id=1, source_target_pairs={{0,12},{4,8},{8,4},{12,0},{1,13},{5,9},{9,5},{13,1},{2,14},{6,10},... | collective-permute-start | bytes 1179656 | tf_op jit(solution)/shard_map/ppermute | solution.py:84
  201.0 20.5 %collective-permute-start.41 = (bf16[4,2,320,768]{3,2,1,0:T(8,128)(2,1)}, bf16[4,2,320,768]{3,2,1,0:T(8,128)(2,1)S(1)}, u32[]{:S(2)}, u32[]{:S(2)}) collective-permute-start(bf16[4,2,320,768]{3,2,1,0:T(8,128)(2,1)} %get-tuple-element.462.fwd_own), channel_id=1, source_target_pairs={{0,16},{16,0},{1,17},{17,1},{2,18},{18,2},{3,19},{19,3},{4,20},{20... | collective-permute-start | bytes 11796488 | tf_op jit(solution)/shard_map/ppermute | solution.py:84
  201.0 20.4 %collective-permute-start.38 = (bf16[256,768]{1,0:T(8,128)(2,1)S(1)}, bf16[256,768]{1,0:T(8,128)(2,1)S(1)}, u32[]{:S(2)}, u32[]{:S(2)}) collective-permute-start(bf16[256,768]{1,0:T(8,128)(2,1)S(1)} %get-tuple-element.459), channel_id=1, source_target_pairs={{0,4},{4,0},{8,12},{12,8},{1,5},{5,1},{9,13},{13,9},{2,6},{6,2},{1... | collective-permute-start | bytes 1179656 | tf_op jit(solution)/shard_map/ppermute | solution.py:84
  201.9 19.6 %collective-permute-start.39 = (bf16[256,768]{1,0:T(8,128)(2,1)S(1)}, bf16[256,768]{1,0:T(8,128)(2,1)S(1)}, u32[]{:S(2)}, u32[]{:S(2)}) collective-permute-start(bf16[256,768]{1,0:T(8,128)(2,1)S(1)} %get-tuple-element.460), channel_id=1, source_target_pairs={{0,8},{4,12},{8,0},{12,4},{1,9},{5,13},{9,1},{13,5},{2,10},{6,14},... | collective-permute-start | bytes 1179656 | tf_op jit(solution)/shard_map/ppermute | solution.py:84
  223.8 18.6 %collective-permute-start.45 = (bf16[256,768]{1,0:T(8,128)(2,1)S(1)}, bf16[256,768]{1,0:T(8,128)(2,1)S(1)}, u32[]{:S(2)}, u32[]{:S(2)}) collective-permute-start(bf16[256,768]{1,0:T(8,128)(2,1)S(1)} %get-tuple-element.471), channel_id=1, source_target_pairs={{0,12},{4,8},{8,4},{12,0},{1,13},{5,9},{9,5},{13,1},{2,14},{6,10},... | collective-permute-start | bytes 1179656 | tf_op jit(solution)/shard_map/ppermute | solution.py:84
  243.3 223.8 %reduce-scatter.3.cloned.1.call-start = ((), (), s32[]{:S(2)}) async-start(), calls=%async_computation.2 | async-start | bytes 5898240 | tf_op jit(solution)/shard_map/reduce_scatter | solution.py:1020
  251.2 91.8 %collective-permute-start.60 = (bf16[4,2,320,768]{3,2,1,0:T(8,128)(2,1)}, bf16[4,2,320,768]{3,2,1,0:T(8,128)(2,1)S(1)}, u32[]{:S(2)}, u32[]{:S(2)}) collective-permute-start(bf16[4,2,320,768]{3,2,1,0:T(8,128)(2,1)} %get-tuple-element.549.fwd_own), channel_id=1, source_target_pairs={{0,16},{16,0},{1,17},{17,1},{2,18},{18,2},{3,19},{19,3},{4,20},{20... | collective-permute-start | bytes 11796488 | tf_op jit(solution)/shard_map/ppermute | solution.py:84
  256.7 23.1 %collective-permute-start.50 = (bf16[192,768]{1,0:T(8,128)(2,1)S(1)}, bf16[192,768]{1,0:T(8,128)(2,1)S(1)}, u32[]{:S(2)}, u32[]{:S(2)}) collective-permute-start(bf16[192,768]{1,0:T(8,128)(2,1)S(1)} %get-tuple-element.507), channel_id=1, source_target_pairs={{0,4},{4,0},{8,12},{12,8},{1,5},{5,1},{9,13},{13,9},{2,6},{6,2},{1... | collective-permute-start | bytes 884744 | tf_op jit(solution)/shard_map/ppermute | solution.py:84
  257.4 22.3 %collective-permute-start.51 = (bf16[192,768]{1,0:T(8,128)(2,1)S(1)}, bf16[192,768]{1,0:T(8,128)(2,1)S(1)}, u32[]{:S(2)}, u32[]{:S(2)}) collective-permute-start(bf16[192,768]{1,0:T(8,128)(2,1)S(1)} %get-tuple-element.508), channel_id=1, source_target_pairs={{0,8},{4,12},{8,0},{12,4},{1,9},{5,13},{9,1},{13,5},{2,10},{6,14},... | collective-permute-start | bytes 884744 | tf_op jit(solution)/shard_map/ppermute | solution.py:84
  258.9 20.8 %collective-permute-start.52 = (bf16[192,768]{1,0:T(8,128)(2,1)S(1)}, bf16[192,768]{1,0:T(8,128)(2,1)S(1)}, u32[]{:S(2)}, u32[]{:S(2)}) collective-permute-start(bf16[192,768]{1,0:T(8,128)(2,1)S(1)} %get-tuple-element.509), channel_id=1, source_target_pairs={{0,12},{4,8},{8,4},{12,0},{1,13},{5,9},{9,5},{13,1},{2,14},{6,10},... | collective-permute-start | bytes 884744 | tf_op jit(solution)/shard_map/ppermute | solution.py:84
  300.7 18.7 %collective-permute-start.58 = (bf16[256,768]{1,0:T(8,128)(2,1)S(1)}, bf16[256,768]{1,0:T(8,128)(2,1)S(1)}, u32[]{:S(2)}, u32[]{:S(2)}) collective-permute-start(bf16[256,768]{1,0:T(8,128)(2,1)S(1)} %get-tuple-element.539.refs_10_.refs_0_), channel_id=1, source_target_pairs={{0,12},{4,8},{8,4},{12,0},{1,13},{5,9},{9,5},{13,1},{2,14},{6,10},... | collective-permute-start | bytes 1179656 | tf_op jit(solution)/shard_map/ppermute | solution.py:84
  319.4 19.8 %collective-permute-start.63 = (bf16[192,384]{1,0:T(8,128)(2,1)S(1)}, bf16[192,384]{1,0:T(8,128)(2,1)S(1)}, u32[]{:S(2)}, u32[]{:S(2)}) collective-permute-start(bf16[192,384]{1,0:T(8,128)(2,1)S(1)} %get-tuple-element.553), channel_id=1, source_target_pairs={{0,3},{1,2},{2,1},{3,0},{4,7},{5,6},{6,5},{7,4},{8,11},{9,10},{10,... | collective-permute-start | bytes 442376 | tf_op jit(solution)/shard_map/ppermute | solution.py:84
  322.9 19.3 %collective-permute-start.62 = (bf16[192,384]{1,0:T(8,128)(2,1)S(1)}, bf16[192,384]{1,0:T(8,128)(2,1)S(1)}, u32[]{:S(2)}, u32[]{:S(2)}) collective-permute-start(bf16[192,384]{1,0:T(8,128)(2,1)S(1)} %get-tuple-element.552), channel_id=1, source_target_pairs={{0,2},{1,3},{2,0},{3,1},{4,6},{5,7},{6,4},{7,5},{8,10},{9,11},{10,... | collective-permute-start | bytes 442376 | tf_op jit(solution)/shard_map/ppermute | solution.py:84
  322.9 19.3 %collective-permute-start.61 = (bf16[192,384]{1,0:T(8,128)(2,1)S(1)}, bf16[192,384]{1,0:T(8,128)(2,1)S(1)}, u32[]{:S(2)}, u32[]{:S(2)}) collective-permute-start(bf16[192,384]{1,0:T(8,128)(2,1)S(1)} %get-tuple-element.551), channel_id=1, source_target_pairs={{0,1},{1,0},{2,3},{3,2},{4,5},{5,4},{6,7},{7,6},{8,9},{9,8},{10,11... | collective-permute-start | bytes 442376 | tf_op jit(solution)/shard_map/ppermute | solution.py:84
  344.6 19.6 %collective-permute-start.65 = (bf16[256,768]{1,0:T(8,128)(2,1)S(1)}, bf16[256,768]{1,0:T(8,128)(2,1)S(1)}, u32[]{:S(2)}, u32[]{:S(2)}) collective-permute-start(bf16[256,768]{1,0:T(8,128)(2,1)S(1)} %get-tuple-element.556), channel_id=1, source_target_pairs={{0,8},{4,12},{8,0},{12,4},{1,9},{5,13},{9,1},{13,5},{2,10},{6,14},... | collective-permute-start | bytes 1179656 | tf_op jit(solution)/shard_map/ppermute | solution.py:84
  378.5 23.0 %collective-permute-start.71 = (bf16[192,768]{1,0:T(8,128)(2,1)S(1)}, bf16[192,768]{1,0:T(8,128)(2,1)S(1)}, u32[]{:S(2)}, u32[]{:S(2)}) collective-permute-start(bf16[192,768]{1,0:T(8,128)(2,1)S(1)} %get-tuple-element.595), channel_id=1, source_target_pairs={{0,4},{4,0},{8,12},{12,8},{1,5},{5,1},{9,13},{13,9},{2,6},{6,2},{1... | collective-permute-start | bytes 884744 | tf_op jit(solution)/shard_map/ppermute | solution.py:84
  379.9 21.6 %collective-permute-start.72 = (bf16[192,768]{1,0:T(8,128)(2,1)S(1)}, bf16[192,768]{1,0:T(8,128)(2,1)S(1)}, u32[]{:S(2)}, u32[]{:S(2)}) collective-permute-start(bf16[192,768]{1,0:T(8,128)(2,1)S(1)} %get-tuple-element.596), channel_id=1, source_target_pairs={{0,8},{4,12},{8,0},{12,4},{1,9},{5,13},{9,1},{13,5},{2,10},{6,14},... | collective-permute-start | bytes 884744 | tf_op jit(solution)/shard_map/ppermute | solution.py:84
  380.9 20.7 %collective-permute-start.73 = (bf16[192,768]{1,0:T(8,128)(2,1)S(1)}, bf16[192,768]{1,0:T(8,128)(2,1)S(1)}, u32[]{:S(2)}, u32[]{:S(2)}) collective-permute-start(bf16[192,768]{1,0:T(8,128)(2,1)S(1)} %get-tuple-element.597), channel_id=1, source_target_pairs={{0,12},{4,8},{8,4},{12,0},{1,13},{5,9},{9,5},{13,1},{2,14},{6,10},... | collective-permute-start | bytes 884744 | tf_op jit(solution)/shard_map/ppermute | solution.py:84
  429.2 28.0 %collective-permute-start.84 = (bf16[192,384]{1,0:T(8,128)(2,1)S(1)}, bf16[192,384]{1,0:T(8,128)(2,1)S(1)}, u32[]{:S(2)}, u32[]{:S(2)}) collective-permute-start(bf16[192,384]{1,0:T(8,128)(2,1)S(1)} %get-tuple-element.638), channel_id=1, source_target_pairs={{0,2},{1,3},{2,0},{3,1},{4,6},{5,7},{6,4},{7,5},{8,10},{9,11},{10,... | collective-permute-start | bytes 442376 | tf_op jit(solution)/shard_map/ppermute | solution.py:84
  433.6 23.5 %collective-permute-start.83 = (bf16[192,384]{1,0:T(8,128)(2,1)S(1)}, bf16[192,384]{1,0:T(8,128)(2,1)S(1)}, u32[]{:S(2)}, u32[]{:S(2)}) collective-permute-start(bf16[192,384]{1,0:T(8,128)(2,1)S(1)} %get-tuple-element.637), channel_id=1, source_target_pairs={{0,1},{1,0},{2,3},{3,2},{4,5},{5,4},{6,7},{7,6},{8,9},{9,8},{10,11... | collective-permute-start | bytes 442376 | tf_op jit(solution)/shard_map/ppermute | solution.py:84
  (170 other events, 2607.0 us)
Sparse Core Ops, SparseCore 0:
  243.3 90.8 reduce-scatter.4
  365.8 92.8 reduce-scatter.2

commit v3 on v2

--- a/solution.py
+++ b/solution.py
@@ -77,6 +77,16 @@
     @pl.when(select != 0)
     def _():
         to_ref[...] = other_ref[...]
+
+
+def either(select, step, own, other):
+    @pl.when(select == 0)
+    def _():
+        step(*own)
+
+    @pl.when(select != 0)
+    def _():
+        step(*other)
 
 
 def exchange(value, axis, mask):
@@ -418,7 +428,7 @@
             dq_ref[lanes, columns] = dq * HEAD_DIM**-0.5
             return carry
 
-        lax.fori_loop(0, heads, one_head, 0)
+        lax.fori_loop(0, heads, one_head, 0, unroll=True)
 
     for first in range(0, SEQ, rows):
         where = slice(first, first + rows)
@@ -558,7 +568,7 @@
     x_refs = refs[9 : 9 + parts]
     half_ref, slope_ref, gate_ref, probs_ref = refs[9 + parts : 13 + parts]
     out_refs = refs[13 + parts : 13 + 2 * parts]
-    x_ref, slots_ref, up_ref, down_ref = refs[13 + 2 * parts :]
+    x_ref, slots_ref = refs[13 + 2 * parts :]
     rows = SEQ // parts
     step = pl.program_id(0)
     e = order[step]
@@ -579,21 +589,22 @@
             if k == 0:
                 probs_ref[...] = probs
 
-    choose(sel[0], up_own.at[0], up_other.at[0], up_ref)
-    choose(sel[0], down_own.at[0], down_other.at[0], down_ref)
-    expert_in = dispatch(e, target_row, x_ref)
-    half_ref[0, 1] = expert_in
-    up = dot(expert_in, up_ref[...])
-    inner = np.sqrt(2 / np.pi).astype(np.float32)
-    square = up * up
-    bend = jnp.tanh(inner * (up * (1.0 + 0.044715 * square)))
-    half = 0.5 * (1.0 + bend)
-    act = (up * half).astype(BF)
-    half_ref[0, 0] = act
-    slope_ref[0] = half + 0.5 * up * (1.0 - bend * bend) * (
-        inner * (1.0 + 3 * 0.044715 * square)
-    )
-    slots_ref[pl.ds(pl.multiple_of(e * CAP, CAP), CAP), :] = dot(act, down_ref[...]).astype(BF)
+    def one_expert(up_ref, down_ref):
+        expert_in = dispatch(e, target_row, x_ref)
+        half_ref[0, 1] = expert_in
+        up = dot(expert_in, up_ref[0])
+        inner = np.sqrt(2 / np.pi).astype(np.float32)
+        square = up * up
+        bend = jnp.tanh(inner * (up * (1.0 + 0.044715 * square)))
+        half = 0.5 * (1.0 + bend)
+        act = (up * half).astype(BF)
+        half_ref[0, 0] = act
+        slope_ref[0] = half + 0.5 * up * (1.0 - bend * bend) * (
+            inner * (1.0 + 3 * 0.044715 * square)
+        )
+        slots_ref[pl.ds(pl.multiple_of(e * CAP, CAP), CAP), :] = dot(act, down_ref[0]).astype(BF)
+
+    either(sel[0], one_expert, (up_own, down_own), (up_other, down_other))
 
     @pl.when(step == EXPERTS - 1)
     def _():
@@ -634,8 +645,6 @@
             scratch_shapes=[
                 pltpu.VMEM((SEQ, D), BF),
                 pltpu.VMEM((SLOTS, D), BF),
-                pltpu.VMEM((D, hidden), BF),
-                pltpu.VMEM((hidden, D), BF),
             ],
         ),
         out_shape=[in_hbm((EXPERTS, 2, CAP, D), BF)]
@@ -667,7 +676,7 @@
     refs = refs[10 + parts :]
     half_ref = refs[0]
     out_refs = refs[1 : 1 + parts]
-    g_ref, slots_ref, up_ref, down_ref = refs[1 + parts :]
+    g_ref, slots_ref = refs[1 + parts :]
     rows = SEQ // parts
     step = pl.program_id(0)
     e = order[step]
@@ -678,15 +687,16 @@
             where = slice(k * rows, (k + 1) * rows)
             g_ref[where, :] = (gate[where, :] * g_refs[k][...].astype(F32)).astype(BF)
 
-    choose(sel[0], up_own.at[0], up_other.at[0], up_ref)
-    choose(sel[0], down_own.at[0], down_other.at[0], down_ref)
-    d_out = dispatch(e, target_row, g_ref)
-    half_ref[0, 0] = d_out
-    d_up = (slope_ref[0] * dot(d_out, down_ref[...], 1, 1)).astype(BF)
-    half_ref[0, 1] = d_up
-    slots_ref[pl.ds(pl.multiple_of(e * CAP, CAP), CAP), :] = dot(d_up, up_ref[...], 1, 1).astype(
-        BF
-    )
+    def one_expert(up_ref, down_ref):
+        d_out = dispatch(e, target_row, g_ref)
+        half_ref[0, 0] = d_out
+        d_up = (slope_ref[0] * dot(d_out, down_ref[0], 1, 1)).astype(BF)
+        half_ref[0, 1] = d_up
+        slots_ref[pl.ds(pl.multiple_of(e * CAP, CAP), CAP), :] = dot(d_up, up_ref[0], 1, 1).astype(
+            BF
+        )
+
+    either(sel[0], one_expert, (up_own, down_own), (up_other, down_other))
 
     @pl.when(step == EXPERTS - 1)
     def _():
@@ -711,8 +721,6 @@
             scratch_shapes=[
                 pltpu.VMEM((SEQ, D), BF),
                 pltpu.VMEM((SLOTS, D), BF),
-                pltpu.VMEM((D, hidden), BF),
-                pltpu.VMEM((hidden, D), BF),
             ],
         ),
         out_shape=[in_hbm((EXPERTS, 2, CAP, D), BF)] + [shape((rows, D), BF)] * parts,
@@ -896,9 +904,9 @@
 
 def expert_grads_body(fwd_own, fwd_other, bwd_own, bwd_other, out):
     for kind in range(2):
-        total = dot(fwd_own[0, kind], bwd_own[0, kind], 0, 0)
-        total = total + dot(fwd_other[0, kind], bwd_other[0, kind], 0, 0)
-        out[kind, 0] = total.astype(BF)
+        left = jnp.concatenate([fwd_own[0, kind], fwd_other[0, kind]], axis=0)
+        right = jnp.concatenate([bwd_own[0, kind], bwd_other[0, kind]], axis=0)
+        out[kind, 0] = dot(left, right, 0, 0).astype(BF)
 
 
 def expert_grads(values):
@@ -998,11 +1006,18 @@
     )(place, own, received)
 
 
-def scatter_end(chunks):
+def scatter_move(chunks):
+    return [chunks[0]] + [exchange(chunk, "dp", k) for k, chunk in enumerate(chunks) if k]
+
+
+def scatter_total(chunks):
     if len(chunks) == 1:
         return lax.psum_scatter(chunks[0], "dp", scatter_dimension=0, tiled=True).astype(F32)
-    others = [exchange(chunk, "dp", k).astype(F32) for k, chunk in enumerate(chunks) if k]
-    return functools.reduce(jnp.add, others, chunks[0])
+    return functools.reduce(jnp.add, [chunk.astype(F32) for chunk in chunks])
+
+
+def scatter_end(chunks):
+    return scatter_total(scatter_move(chunks))
 
 
 def attention_results(value, wide):
@@ -1014,6 +1029,43 @@
             [value[b * taken : (b + 1) * taken, 3 * wide :] for b in range(D // wide)], axis=1
         ),
     )
+
+
+def expert_results_body(place, own_0, moved_0, own_1, moved_1, down_ref, up_ref):
+    i = pl.program_id(0)
+    first = place[1] == 0
+    own = (i < HALF) == first
+
+    def put(value):
+        down_ref[...] = value[0].astype(F32)
+        up_ref[...] = value[1].astype(F32)
+
+    for layer, own_ref, moved_ref in ((0, own_0, moved_0), (1, own_1, moved_1)):
+        kept = first == (layer == 0)
+        pl.when(kept & own)(functools.partial(put, own_ref))
+        pl.when(kept & jnp.logical_not(own))(functools.partial(put, moved_ref))
+
+
+def expert_results(place, sums, moved):
+    rows, columns = sums[0].shape[1:]
+    shaped = [
+        a.reshape(2, HALF, rows, columns) for pair in zip(sums, moved) for a in pair
+    ]
+    block = pl.BlockSpec((2, 1, rows, columns), lambda i, place: (0, i % HALF, 0, 0))
+    out = pl.BlockSpec((1, rows, columns), lambda i, place: (i, 0, 0))
+    return pl.pallas_call(
+        expert_results_body,
+        grid_spec=pltpu.PrefetchScalarGridSpec(
+            num_scalar_prefetch=1,
+            grid=(EXPERTS,),
+            in_specs=[block] * 4,
+            out_specs=[out, out],
+        ),
+        out_shape=[shape((EXPERTS, rows, columns), F32)] * 2,
+        compiler_params=limit(24),
+        cost_estimate=cost(1e6, 1e5),
+        name="expert_results",
+    )(place, *shaped)
 
 
 def scatter_sum(value, dim):
@@ -1184,14 +1236,13 @@
             stats.append((stat, stat_more))
         else:
             y_parts, bwd_halves, fwd_other, square_1 = phase(
-                y_parts, bwd_halves, fwd_other, scatter_end(square_1)
+                y_parts, bwd_halves, fwd_other, scatter_move(square_1)
             )
             combined = saved[0][5]
 
         total = expert_grads((fwd_halves, fwd_other, bwd_halves, swap(bwd_halves)))
         y_parts, total, combined = phase(swap_parts(y_parts), total, combined)
-        if layer == 0 or 'wa' == "wa":
-            expert_sums.append(scatter_sum(total, 1))
+        expert_sums.append(scatter_sum(total, 1))
 
         (d_mid, d_a, grad_gain_mid, grad_router), d_pieces = middle_back(
             g,
@@ -1258,35 +1309,44 @@
     d_h = input_back(d_mid, hidden[0], gains[0], x_terms)[0]
     out_keep, out_sent = kept_sent(outputs)
     d_h_keep, d_h_sent = kept_sent((d_h, d_h_1.astype(F32)))
-    out_moved, d_h_moved, small, square = phase(
+    small = small[0] + swap(small[1])
+    sum_1, sum_0 = expert_sums
+    out_moved, d_h_moved, small, shared, square, moved_1 = phase(
         swap(out_sent),
         swap(d_h_sent.astype(BF)),
-        (small[0], swap(small[1])),
+        small,
+        sum_small(small[:8], "tensor"),
         scatter_small(place[0], square, swap(sent)),
+        lax.ppermute(sum_1, "section", [(0, 1)]),
     )
-    small = small[0] + small[1]
-    small, shared, square_0 = phase(small, sum_small(small[:8], "tensor"), scatter_end(square))
     small = sum_small(jnp.concatenate([shared, small[8:]], axis=0), "dp")
-
-    layer_out = placed(out_keep[None], out_moved[None])
-    input_grad = placed(d_h_keep[None], d_h_moved.astype(F32)[None])
-    keep, sent = kept_sent((square_0, square_1))
-    square = placed(keep, swap(sent.astype(BF)).astype(F32), axis=1)
-    grad_w_in, grad_w_out = attention_results(square, wide)
-    keep, sent = kept_sent(expert_sums[::-1])
-    experts = placed(*[a.astype(F32).reshape(2, HALF, -1, D) for a in (keep, swap(sent))], axis=1)
     table = small[8 : 8 + heads, :BUCKETS].T
     share = BUCKETS // lax.axis_size("dp")
     stat = small[6]
-    root_means = jnp.sqrt(stat[:3] / (stat[3] * D))
+    layer_out = placed(out_keep[None], out_moved[None])
+    input_grad = placed(d_h_keep[None], d_h_moved.astype(F32)[None])
+    square_0, layer_out, input_grad, grad_gain, grad_table, grad_router, root_means = phase(
+        scatter_end(square),
+        layer_out,
+        input_grad,
+        small[0:2],
+        lax.dynamic_slice_in_dim(table, z * share, share, 0),
+        small[2:6].T,
+        jnp.sqrt(stat[:3] / (stat[3] * D)),
+    )
+    keep, sent = kept_sent((square_0, scatter_total(square_1)))
+    square = placed(keep, swap(sent.astype(BF)).astype(F32), axis=1)
+    grad_w_in, grad_w_out = attention_results(square, wide)
+    moved_0 = lax.ppermute(sum_0, "section", [(1, 0)])
+    experts = expert_results(place[0], (sum_0, sum_1), (moved_0, moved_1))
     return (
         layer_out[None],
         input_grad[None],
-        small[None, 0:2],
+        grad_gain[None],
         grad_w_in[None],
         grad_w_out[None],
-        lax.dynamic_slice_in_dim(table, z * share, share, 0)[None],
-        small[2:6].T[None],
+        grad_table[None],
+        grad_router[None],
         experts[1][None],
         experts[0][None],
         root_means[None],

time: 489 us -> 484 us (0.990)
  other arithmetic: 13.7 us -> 6.39 us
  starting transfers between devices: 91.8 us -> 97.3 us
    unnamed x221 -> x245, local copies, waits for them, and re-layouts: 20.1 us -> 23.3 us
    ppermute x91 -> x90, starting transfers between devices: 91.7 us -> 94.6 us  [exchange(): return lax.ppermute(value, axis, [(i, i ^ mask) for i in range(count)])]
    ppermute x91 -> x90, waiting for transfers between devices: 159 us -> 158 us  [exchange(): return lax.ppermute(value, axis, [(i, i ^ mask) for i in range(count)])]
  transfers between devices with their start and end apart: 93 -> 94, of which waited for: 43 -> 41; matrix products, arithmetic and copies ran while one was open for 4% -> 2% of each run, Pallas kernels for 36% -> 36%
where the time goes in v3:
time: 484 us; the launch traced here: 479 us
  Pallas kernels  175 us (36%)
  waiting for transfers between devices  158 us (33%)
  starting transfers between devices  97.3 us (20%)
  local copies, waits for them, and re-layouts  25.4 us (5%)
  between operations  16.5 us (3%)
  other arithmetic  6.39 us (1%)
    ppermute x90, waiting for transfers between devices, exchange(): return lax.ppermute(value, axis, [(i, i ^ mask) for i in range(count)])  158 us
    ppermute x90, starting transfers between devices, exchange(): return lax.ppermute(value, axis, [(i, i ^ mask) for i in range(count)])  94.6 us
    pallas_call x2, Pallas kernels, fwd_experts(): pl.pallas_call(functools.partial(fwd_experts_body, parts), grid_spec=pltp...  32.8 us
    pallas_call x2, Pallas kernels, bwd_attention(): pl.pallas_call(functools.partial(bwd_attention_body, parts), out_shape=[i...  32.5 us
    pallas_call x2, Pallas kernels, bwd_experts(): pl.pallas_call(functools.partial(bwd_experts_body, parts), grid_spec=pltp...  29.7 us
    pallas_call x2, Pallas kernels, fwd_attention(): pl.pallas_call(functools.partial(fwd_attention_body, parts, norm_inside),...  26.5 us
    unnamed x245, local copies, waits for them, and re-layouts  23.3 us
    pallas_call x2, Pallas kernels, expert_grads(): pl.pallas_call(expert_grads_body, grid=(HALF,), in_specs=[own, other, own...  14.6 us
  transfers between devices with their start and end apart: 94, of which 41 were waited for; matrix products, arithmetic and copies ran while one was open for 2% of the time, Pallas kernels for 36%

profile of v3, /device:TPU:0, one launch (start us, length us, event | category | flops | bytes accessed | tf_op | source)
XLA Modules:
  0.0 478.6 jit_solution(11974171756802183808)
XLA Ops:
  23.1 9.4 %collective-permute-done.1.refs_9_ = bf16[256,768]{1,0:T(8,128)(2,1)} collective-permute-done((bf16[256,768]{1,0:T(8,128)(2,1)S(1)}, bf16[256,768]{1,0:T(8,128)(2,1)}, u32[]{:S(2)}, u32[]{:S(2)}) %collective-permute-start.1) | collective-permute-done | bytes 393248 | tf_op jit(solution)/shard_map/ppermute | solution.py:94
  37.2 14.0 %fwd_attention.2 = (bf16[1024,768]{1,0:T(8,128)(2,1)}, bf16[3,3,1024,64]{3,2,1,0:T(8,128)(2,1)}, bf16[2,192,1024]{2,1,0:T(8,128)(2,1)}, f32[3,1,1024]{2,1,0:T(1,...) custom-call(s32[4]{0:T(128)S(1)} %add_add_fusion.2.place.refs_0_, ...), custom_call_target="tpu_custom_call" | custom-call | flops 8999999488 | bytes 10000000 | tf_op jit(solution)/shard_map/fwd_attention/pallas_call | solution.py:342
  68.3 4.8 collective-permute-done.15.refs_10_
  73.1 6.6 %collective-permute-done.16.refs_11_ = bf16[256,768]{1,0:T(8,128)(2,1)} collective-permute-done((bf16[256,768]{1,0:T(8,128)(2,1)S(1)}, bf16[256,768]{1,0:T(8,128)(2,1)}, u32[]{:S(2)}, u32[]{:S(2)}) %collective-permute-start.16) | collective-permute-done | bytes 393248 | tf_op jit(solution)/shard_map/ppermute | solution.py:94
  83.2 16.8 %fwd_experts.2 = (bf16[4,2,320,768]{3,2,1,0:T(8,128)(2,1)}, f32[4,320,768]{2,1,0:T(8,128)}, f32[1024,1]{1,0:T(8,128)S(1)}, f32[256,128]{1,0:T(8,128)S(1)}, bf16[...) custom-call(s32[1]{0:T(128)} %bitcast.3.refs_0_, ...), custom_call_target="tpu_custom_call" | custom-call | flops 12000000000 | bytes 30000000 | tf_op jit(solution)/shard_map/fwd_experts/pallas_call | solution.py:633
  106.5 8.0 %collective-permute-done.23.refs_5_ = bf16[256,768]{1,0:T(8,128)(2,1)S(1)} collective-permute-done((bf16[256,768]{1,0:T(8,128)(2,1)S(1)}, bf16[256,768]{1,0:T(8,128)(2,1)S(1)}, u32[]{:S(2)}, u32[]{:S(2)}) %collective-permute-start.23) | collective-permute-done | bytes 393248 | tf_op jit(solution)/shard_map/ppermute | solution.py:94
  114.5 4.5 collective-permute-done.24.refs_6_
  127.3 5.6 %collective-permute-done.26.refs_8_ = bf16[256,768]{1,0:T(8,128)(2,1)S(1)} collective-permute-done((bf16[256,768]{1,0:T(8,128)(2,1)S(1)}, bf16[256,768]{1,0:T(8,128)(2,1)S(1)}, u32[]{:S(2)}, u32[]{:S(2)}) %collective-permute-start.26) | collective-permute-done | bytes 393248 | tf_op jit(solution)/shard_map/ppermute | solution.py:94
  132.9 7.4 %collective-permute-done.27.refs_9_ = bf16[256,768]{1,0:T(8,128)(2,1)S(1)} collective-permute-done((bf16[256,768]{1,0:T(8,128)(2,1)S(1)}, bf16[256,768]{1,0:T(8,128)(2,1)S(1)}, u32[]{:S(2)}, u32[]{:S(2)}) %collective-permute-start.27) | collective-permute-done | bytes 393248 | tf_op jit(solution)/shard_map/ppermute | solution.py:94
  140.3 12.6 %fwd_attention.3 = (bf16[1024,768]{1,0:T(8,128)(2,1)}, bf16[3,3,1024,64]{3,2,1,0:T(8,128)(2,1)}, bf16[2,192,1024]{2,1,0:T(8,128)(2,1)}, f32[3,1,1024]{2,1,0:T(1,...) custom-call(s32[4]{0:T(128)S(1)} %add_add_fusion.3.place.refs_0_, ...), custom_call_target="tpu_custom_call" | custom-call | flops 8999999488 | bytes 10000000 | tf_op jit(solution)/shard_map/fwd_attention/pallas_call | solution.py:342
  158.8 5.3 %collective-permute-done.32.refs_5_.refs_2_ = bf16[192,256]{1,0:T(8,128)(2,1)S(1)} collective-permute-done((bf16[192,256]{1,0:T(8,128)(2,1)S(1)}, bf16[192,256]{1,0:T(8,128)(2,1)S(1)}, u32[]{:S(2)}, u32[]{:S(2)}) %collective-permute-start.32) | collective-permute-done | bytes 98336 | tf_op jit(solution)/shard_map/ppermute | solution.py:94
  169.0 6.4 %collective-permute-done.34.refs_10_ = bf16[256,768]{1,0:T(8,128)(2,1)S(1)} collective-permute-done((bf16[256,768]{1,0:T(8,128)(2,1)S(1)}, bf16[256,768]{1,0:T(8,128)(2,1)S(1)}, u32[]{:S(2)}, u32[]{:S(2)}) %collective-permute-start.34) | collective-permute-done | bytes 393248 | tf_op jit(solution)/shard_map/ppermute | solution.py:94
  175.3 4.6 collective-permute-done.35.refs_11_
  181.6 16.0 %fwd_experts.3 = (bf16[4,2,320,768]{3,2,1,0:T(8,128)(2,1)}, f32[4,320,768]{2,1,0:T(8,128)}, f32[1024,1]{1,0:T(8,128)S(1)}, f32[256,128]{1,0:T(8,128)S(1)}, bf16[...) custom-call(s32[1]{0:T(128)} %bitcast.18.refs_0_, ...), custom_call_target="tpu_custom_call" | custom-call | flops 12000000000 | bytes 30000000 | tf_op jit(solution)/shard_map/fwd_experts/pallas_call | solution.py:633
  201.9 14.9 %bwd_experts.2 = (bf16[4,2,320,768]{3,2,1,0:T(8,128)(2,1)}, bf16[256,768]{1,0:T(8,128)(2,1)S(1)}, bf16[256,768]{1,0:T(8,128)(2,1)S(1)}, bf16[256,768]{1,0:T(8,128)(2,1)S(1)}, bf16[256,768]{1,0:T(8,128)(2,1)S(1)}) custom-call(s32[1]{0:T(128)} %bitcast.18.refs_0_, s32[4]{0:T(128)S(1)} %broadcast_select_fusion.4.refs_1_, ...), custom_call_target="tpu_custom_call" | custom-call | flops 12000000000 | bytes 30000000 | tf_op jit(solution)/shard_map/bwd_experts/pallas_call | solution.py:711
  226.2 7.3 %expert_grads.2 = bf16[2,2,768,768]{3,2,1,0:T(8,128)(2,1)} custom-call(bf16[4,2,320,768]{3,2,1,0:T(8,128)(2,1)} %get-tuple-element.472.fwd_own, bf16[4,2,320,768]{3,2,1,0:T(8,128)(2,1)} %copy-done.106, bf16[4,2,320,768]{3,2,1,0:T(8,128)(2,1)} %get-tuple-element.483.bwd_own, bf16[4,2,320,768]{3,2,1,0:T(8,128)(2,1)S(1)} %collective-permute-done.46.bwd_other), custom_call_target="tpu_custom_call" | custom-call | flops 1000000 | bytes 100000 | tf_op jit(solution)/shard_map/expert_grads/pallas_call | solution.py:917
  233.5 6.3 %collective-permute-done.44.refs_10_ = bf16[256,768]{1,0:T(8,128)(2,1)S(1)} collective-permute-done((bf16[256,768]{1,0:T(8,128)(2,1)S(1)}, bf16[256,768]{1,0:T(8,128)(2,1)S(1)}, u32[]{:S(2)}, u32[]{:S(2)}) %collective-permute-start.44) | collective-permute-done | bytes 393248 | tf_op jit(solution)/shard_map/ppermute | solution.py:94
  241.6 4.3 middle_back.2
  258.9 16.3 %bwd_attention.2 = (bf16[1024,576]{1,0:T(8,128)(2,1)}, f32[18,128,128]{2,1,0:T(8,128)}, f32[3,8,256]{2,1,0:T(8,128)S(1)}, f32[1,768]{1,0:T(1,128)S(1)}, bf16[256...) custom-call(s32[4]{0:T(128)S(1)} %add_add_fusion.3.place.refs_0_, ...), custom_call_target="tpu_custom_call" | custom-call | flops 17999998976 | bytes 10000000 | tf_op jit(solution)/shard_map/bwd_attention/pallas_call | solution.py:453
  279.2 3.4 attention_grads.2
  287.5 7.4 %collective-permute-done.54.refs_5_ = bf16[256,768]{1,0:T(8,128)(2,1)S(1)} collective-permute-done((bf16[256,768]{1,0:T(8,128)(2,1)}, bf16[256,768]{1,0:T(8,128)(2,1)S(1)}, u32[]{:S(2)}, u32[]{:S(2)}) %collective-permute-start.54) | collective-permute-done | bytes 393248 | tf_op jit(solution)/shard_map/ppermute | solution.py:94
  300.5 7.7 %collective-permute-done.56.refs_11_ = bf16[256,768]{1,0:T(8,128)(2,1)S(1)} collective-permute-done((bf16[256,768]{1,0:T(8,128)(2,1)S(1)}, bf16[256,768]{1,0:T(8,128)(2,1)S(1)}, u32[]{:S(2)}, u32[]{:S(2)}) %collective-permute-start.56) | collective-permute-done | bytes 393248 | tf_op jit(solution)/shard_map/ppermute | solution.py:94
  308.2 8.7 %collective-permute-done.57.refs_12_ = bf16[256,768]{1,0:T(8,128)(2,1)S(1)} collective-permute-done((bf16[256,768]{1,0:T(8,128)(2,1)S(1)}, bf16[256,768]{1,0:T(8,128)(2,1)S(1)}, u32[]{:S(2)}, u32[]{:S(2)}) %collective-permute-start.57) | collective-permute-done | bytes 393248 | tf_op jit(solution)/shard_map/ppermute | solution.py:94
  321.6 14.8 %bwd_experts.3 = (bf16[4,2,320,768]{3,2,1,0:T(8,128)(2,1)}, bf16[256,768]{1,0:T(8,128)(2,1)S(1)}, bf16[256,768]{1,0:T(8,128)(2,1)S(1)}, bf16[256,768]{1,0:T(8,128)(2,1)S(1)}, bf16[256,768]{1,0:T(8,128)(2,1)S(1)}) custom-call(s32[1]{0:T(128)} %bitcast.3.refs_0_, s32[4]{0:T(128)S(1)} %copy-done.92, s32[1,1024]{1,0:T(1,128)S(1)} %copy-done.87, ...), custom_call_target="tpu_custom_call" | custom-call | flops 12000000000 | bytes 30000000 | tf_op jit(solution)/shard_map/bwd_experts/pallas_call | solution.py:711
  341.0 3.5 collective-permute-done.67.bwd_other
  344.5 7.3 %expert_grads.3 = bf16[2,2,768,768]{3,2,1,0:T(8,128)(2,1)} custom-call(bf16[4,2,320,768]{3,2,1,0:T(8,128)(2,1)} %get-tuple-element.559.fwd_own, bf16[4,2,320,768]{3,2,1,0:T(8,128)(2,1)} %copy-done.105, bf16[4,2,320,768]{3,2,1,0:T(8,128)(2,1)} %get-tuple-element.569.bwd_own, bf16[4,2,320,768]{3,2,1,0:T(8,128)(2,1)S(1)} %collective-permute-done.67.bwd_other), custom_call_target="tpu_custom_call" | custom-call | flops 1000000 | bytes 100000 | tf_op jit(solution)/shard_map/expert_grads/pallas_call | solution.py:917
  351.8 6.8 %collective-permute-done.65.refs_10_ = bf16[256,768]{1,0:T(8,128)(2,1)S(1)} collective-permute-done((bf16[256,768]{1,0:T(8,128)(2,1)S(1)}, bf16[256,768]{1,0:T(8,128)(2,1)S(1)}, u32[]{:S(2)}, u32[]{:S(2)}) %collective-permute-start.65) | collective-permute-done | bytes 393248 | tf_op jit(solution)/shard_map/ppermute | solution.py:94
  360.3 4.2 middle_back.3
  376.7 16.2 %bwd_attention.3 = (bf16[1024,576]{1,0:T(8,128)(2,1)}, f32[18,128,128]{2,1,0:T(8,128)}, f32[3,8,256]{2,1,0:T(8,128)S(1)}, f32[1,768]{1,0:T(1,128)S(1)}, bf16[256...) custom-call(s32[4]{0:T(128)S(1)} %add_add_fusion.2.place.refs_0_, ...), custom_call_target="tpu_custom_call" | custom-call | flops 17999998976 | bytes 10000000 | tf_op jit(solution)/shard_map/bwd_attention/pallas_call | solution.py:453
  438.3 4.7 collective-permute-done.87
  446.0 14.8 %collective-permute-done.85 = bf16[192,384]{1,0:T(8,128)(2,1)S(1)} collective-permute-done((bf16[192,384]{1,0:T(8,128)(2,1)S(1)}, bf16[192,384]{1,0:T(8,128)(2,1)S(1)}, u32[]{:S(2)}, u32[]{:S(2)}) %collective-permute-start.85) | collective-permute-done | bytes 147488 | tf_op jit(solution)/shard_map/ppermute | solution.py:94
  467.9 3.7 expert_results.1
  (466 shorter events, 187.9 us)
Async XLA Ops:
  7.2 391.6 %reduce-scatter.3.cloned.1.call-start = ((), (), s32[]{:S(2)}) async-start(), calls=%async_computation.2 | async-start | bytes 5898240 | tf_op jit(solution)/shard_map/reduce_scatter | solution.py:1072
  7.2 25.3 %collective-permute-start.5 = (bf16[576,768]{1,0:T(8,128)(2,1)}, bf16[576,768]{1,0:T(8,128)(2,1)}, u32[]{:S(2)}, u32[]{:S(2)}) collective-permute-start(bf16[576,768]{1,0:T(8,128)(2,1)} %bitcast.84), channel_id=1, source_target_pairs={{0,16},{16,0},{1,17},{17,1},{2,18},{18,2},{3,19},{19,3},{4,20},{20... | collective-permute-start | bytes 2654216 | tf_op jit(solution)/shard_map/ppermute | solution.py:94
  13.1 19.4 %collective-permute-start.1 = (bf16[256,768]{1,0:T(8,128)(2,1)S(1)}, bf16[256,768]{1,0:T(8,128)(2,1)}, u32[]{:S(2)}, u32[]{:S(2)}) collective-permute-start(bf16[256,768]{1,0:T(8,128)(2,1)S(1)} %dynamic-slice_bitcast_fusion.1.refs_7_.refs_0_.refs_1_), channel_id=1, source_target_pairs={{0,8},{4,12},{8,0},{12,4},{1,9},{5,13},{9,1},{13,5},{2,10},{6,14},... | collective-permute-start | bytes 1179656 | tf_op jit(solution)/shard_map/ppermute | solution.py:94
  32.5 47.1 %collective-permute-start.18 = (bf16[4,768,768]{2,1,0:T(8,128)(2,1)}, bf16[4,768,768]{2,1,0:T(8,128)(2,1)}, u32[]{:S(2)}, u32[]{:S(2)}) collective-permute-start(bf16[4,768,768]{2,1,0:T(8,128)(2,1)} %bitcast.98), channel_id=1, source_target_pairs={{0,16},{16,0},{1,17},{17,1},{2,18},{18,2},{3,19},{19,3},{4,20},{20... | collective-permute-start | bytes 14155784 | tf_op jit(solution)/shard_map/ppermute | solution.py:94
  32.5 47.1 %collective-permute-start.19 = (bf16[4,768,768]{2,1,0:T(8,128)(2,1)}, bf16[4,768,768]{2,1,0:T(8,128)(2,1)}, u32[]{:S(2)}, u32[]{:S(2)}) collective-permute-start(bf16[4,768,768]{2,1,0:T(8,128)(2,1)} %bitcast.103), channel_id=1, source_target_pairs={{0,16},{16,0},{1,17},{17,1},{2,18},{18,2},{3,19},{19,3},{4,20},{20... | collective-permute-start | bytes 14155784 | tf_op jit(solution)/shard_map/ppermute | solution.py:94
  33.0 18.8 %collective-permute-start.9 = (bf16[192,768]{1,0:T(8,128)(2,1)S(1)}, bf16[192,768]{1,0:T(8,128)(2,1)S(1)}, u32[]{:S(2)}, u32[]{:S(2)}) collective-permute-start(bf16[192,768]{1,0:T(8,128)(2,1)S(1)} %get-tuple-element.361.refs_7_.refs_12_), channel_id=1, source_target_pairs={{0,4},{4,0},{8,12},{12,8},{1,5},{5,1},{9,13},{13,9},{2,6},{6,2},{1... | collective-permute-start | bytes 884744 | tf_op jit(solution)/shard_map/ppermute | solution.py:94
  79.7 23.2 %collective-permute-start.20 = (bf16[192,768]{1,0:T(8,128)(2,1)S(1)}, bf16[192,768]{1,0:T(8,128)(2,1)S(1)}, u32[]{:S(2)}, u32[]{:S(2)}) collective-permute-start(bf16[192,768]{1,0:T(8,128)(2,1)S(1)} %get-tuple-element.432.refs_7_.refs_12_), channel_id=1, source_target_pairs={{0,4},{4,0},{8,12},{12,8},{1,5},{5,1},{9,13},{13,9},{2,6},{6,2},{1... | collective-permute-start | bytes 884744 | tf_op jit(solution)/shard_map/ppermute | solution.py:94
  80.6 22.3 %collective-permute-start.21 = (bf16[192,768]{1,0:T(8,128)(2,1)S(1)}, bf16[192,768]{1,0:T(8,128)(2,1)S(1)}, u32[]{:S(2)}, u32[]{:S(2)}) collective-permute-start(bf16[192,768]{1,0:T(8,128)(2,1)S(1)} %get-tuple-element.432.refs_7_.refs_12_), channel_id=1, source_target_pairs={{0,8},{4,12},{8,0},{12,4},{1,9},{5,13},{9,1},{13,5},{2,10},{6,14},... | collective-permute-start | bytes 884744 | tf_op jit(solution)/shard_map/ppermute | solution.py:94
  81.8 21.1 %collective-permute-start.22 = (bf16[192,768]{1,0:T(8,128)(2,1)S(1)}, bf16[192,768]{1,0:T(8,128)(2,1)S(1)}, u32[]{:S(2)}, u32[]{:S(2)}) collective-permute-start(bf16[192,768]{1,0:T(8,128)(2,1)S(1)} %get-tuple-element.432.refs_7_.refs_12_), channel_id=1, source_target_pairs={{0,12},{4,8},{8,4},{12,0},{1,13},{5,9},{9,5},{13,1},{2,14},{6,10},... | collective-permute-start | bytes 884744 | tf_op jit(solution)/shard_map/ppermute | solution.py:94
  121.6 18.7 %collective-permute-start.27 = (bf16[256,768]{1,0:T(8,128)(2,1)S(1)}, bf16[256,768]{1,0:T(8,128)(2,1)S(1)}, u32[]{:S(2)}, u32[]{:S(2)}) collective-permute-start(bf16[256,768]{1,0:T(8,128)(2,1)S(1)} %get-tuple-element.423.refs_7_), channel_id=1, source_target_pairs={{0,8},{4,12},{8,0},{12,4},{1,9},{5,13},{9,1},{13,5},{2,10},{6,14},... | collective-permute-start | bytes 1179656 | tf_op jit(solution)/shard_map/ppermute | solution.py:94
  124.4 28.5 %collective-permute-start.29 = (bf16[256,768]{1,0:T(8,128)(2,1)S(1)}, bf16[256,768]{1,0:T(8,128)(2,1)S(1)}, u32[]{:S(2)}, u32[]{:S(2)}) collective-permute-start(bf16[256,768]{1,0:T(8,128)(2,1)S(1)} %dynamic-slice_bitcast_fusion.refs_10_.refs_0_), channel_id=1, source_target_pairs={{0,4},{4,0},{8,12},{12,8},{1,5},{5,1},{9,13},{13,9},{2,6},{6,2},{1... | collective-permute-start | bytes 1179656 | tf_op jit(solution)/shard_map/ppermute | solution.py:94
  125.3 27.6 %collective-permute-start.30 = (bf16[256,768]{1,0:T(8,128)(2,1)S(1)}, bf16[256,768]{1,0:T(8,128)(2,1)S(1)}, u32[]{:S(2)}, u32[]{:S(2)}) collective-permute-start(bf16[256,768]{1,0:T(8,128)(2,1)S(1)} %dynamic-slice_bitcast_fusion.refs_10_.refs_0_), channel_id=1, source_target_pairs={{0,8},{4,12},{8,0},{12,4},{1,9},{5,13},{9,1},{13,5},{2,10},{6,14},... | collective-permute-start | bytes 1179656 | tf_op jit(solution)/shard_map/ppermute | solution.py:94
  198.3 20.9 %collective-permute-start.41 = (bf16[4,2,320,768]{3,2,1,0:T(8,128)(2,1)}, bf16[4,2,320,768]{3,2,1,0:T(8,128)(2,1)S(1)}, u32[]{:S(2)}, u32[]{:S(2)}) collective-permute-start(bf16[4,2,320,768]{3,2,1,0:T(8,128)(2,1)} %get-tuple-element.472.fwd_own), channel_id=1, source_target_pairs={{0,16},{16,0},{1,17},{17,1},{2,18},{18,2},{3,19},{19,3},{4,20},{20... | collective-permute-start | bytes 11796488 | tf_op jit(solution)/shard_map/ppermute | solution.py:94
  198.3 19.7 %collective-permute-start.38 = (bf16[256,768]{1,0:T(8,128)(2,1)S(1)}, bf16[256,768]{1,0:T(8,128)(2,1)S(1)}, u32[]{:S(2)}, u32[]{:S(2)}) collective-permute-start(bf16[256,768]{1,0:T(8,128)(2,1)S(1)} %get-tuple-element.469), channel_id=1, source_target_pairs={{0,4},{4,0},{8,12},{12,8},{1,5},{5,1},{9,13},{13,9},{2,6},{6,2},{1... | collective-permute-start | bytes 1179656 | tf_op jit(solution)/shard_map/ppermute | solution.py:94
  199.6 18.5 %collective-permute-start.39 = (bf16[256,768]{1,0:T(8,128)(2,1)S(1)}, bf16[256,768]{1,0:T(8,128)(2,1)S(1)}, u32[]{:S(2)}, u32[]{:S(2)}) collective-permute-start(bf16[256,768]{1,0:T(8,128)(2,1)S(1)} %get-tuple-element.470), channel_id=1, source_target_pairs={{0,8},{4,12},{8,0},{12,4},{1,9},{5,13},{9,1},{13,5},{2,10},{6,14},... | collective-permute-start | bytes 1179656 | tf_op jit(solution)/shard_map/ppermute | solution.py:94
  200.3 18.9 %collective-permute-start.40 = (bf16[256,768]{1,0:T(8,128)(2,1)S(1)}, bf16[256,768]{1,0:T(8,128)(2,1)S(1)}, u32[]{:S(2)}, u32[]{:S(2)}) collective-permute-start(bf16[256,768]{1,0:T(8,128)(2,1)S(1)} %get-tuple-element.471), channel_id=1, source_target_pairs={{0,12},{4,8},{8,4},{12,0},{1,13},{5,9},{9,5},{13,1},{2,14},{6,10},... | collective-permute-start | bytes 1179656 | tf_op jit(solution)/shard_map/ppermute | solution.py:94
  220.2 19.6 %collective-permute-start.44 = (bf16[256,768]{1,0:T(8,128)(2,1)S(1)}, bf16[256,768]{1,0:T(8,128)(2,1)S(1)}, u32[]{:S(2)}, u32[]{:S(2)}) collective-permute-start(bf16[256,768]{1,0:T(8,128)(2,1)S(1)} %get-tuple-element.480), channel_id=1, source_target_pairs={{0,8},{4,12},{8,0},{12,4},{1,9},{5,13},{9,1},{13,5},{2,10},{6,14},... | collective-permute-start | bytes 1179656 | tf_op jit(solution)/shard_map/ppermute | solution.py:94
  241.4 219.5 %reduce-scatter.5.cloned.1.call-start = ((), (), s32[]{:S(2)}) async-start(), calls=%async_computation.3 | async-start | bytes 5898240 | tf_op jit(solution)/shard_map/reduce_scatter | solution.py:1072
  241.5 94.9 %collective-permute-start.60 = (bf16[4,2,320,768]{3,2,1,0:T(8,128)(2,1)}, bf16[4,2,320,768]{3,2,1,0:T(8,128)(2,1)S(1)}, u32[]{:S(2)}, u32[]{:S(2)}) collective-permute-start(bf16[4,2,320,768]{3,2,1,0:T(8,128)(2,1)} %get-tuple-element.559.fwd_own), channel_id=1, source_target_pairs={{0,16},{16,0},{1,17},{17,1},{2,18},{18,2},{3,19},{19,3},{4,20},{20... | collective-permute-start | bytes 11796488 | tf_op jit(solution)/shard_map/ppermute | solution.py:94
  255.3 19.8 %collective-permute-start.50 = (bf16[192,768]{1,0:T(8,128)(2,1)S(1)}, bf16[192,768]{1,0:T(8,128)(2,1)S(1)}, u32[]{:S(2)}, u32[]{:S(2)}) collective-permute-start(bf16[192,768]{1,0:T(8,128)(2,1)S(1)} %get-tuple-element.517), channel_id=1, source_target_pairs={{0,4},{4,0},{8,12},{12,8},{1,5},{5,1},{9,13},{13,9},{2,6},{6,2},{1... | collective-permute-start | bytes 884744 | tf_op jit(solution)/shard_map/ppermute | solution.py:94
  256.3 18.8 %collective-permute-start.51 = (bf16[192,768]{1,0:T(8,128)(2,1)S(1)}, bf16[192,768]{1,0:T(8,128)(2,1)S(1)}, u32[]{:S(2)}, u32[]{:S(2)}) collective-permute-start(bf16[192,768]{1,0:T(8,128)(2,1)S(1)} %get-tuple-element.518), channel_id=1, source_target_pairs={{0,8},{4,12},{8,0},{12,4},{1,9},{5,13},{9,1},{13,5},{2,10},{6,14},... | collective-permute-start | bytes 884744 | tf_op jit(solution)/shard_map/ppermute | solution.py:94
  276.2 18.7 %collective-permute-start.54 = (bf16[256,768]{1,0:T(8,128)(2,1)}, bf16[256,768]{1,0:T(8,128)(2,1)S(1)}, u32[]{:S(2)}, u32[]{:S(2)}) collective-permute-start(bf16[256,768]{1,0:T(8,128)(2,1)} %get-tuple-element.522), channel_id=1, source_target_pairs={{0,8},{4,12},{8,0},{12,4},{1,9},{5,13},{9,1},{13,5},{2,10},{6,14},... | collective-permute-start | bytes 1179656 | tf_op jit(solution)/shard_map/ppermute | solution.py:94
  297.3 19.7 %collective-permute-start.57 = (bf16[256,768]{1,0:T(8,128)(2,1)S(1)}, bf16[256,768]{1,0:T(8,128)(2,1)S(1)}, u32[]{:S(2)}, u32[]{:S(2)}) collective-permute-start(bf16[256,768]{1,0:T(8,128)(2,1)S(1)} %get-tuple-element.549.refs_10_.refs_0_), channel_id=1, source_target_pairs={{0,8},{4,12},{8,0},{12,4},{1,9},{5,13},{9,1},{13,5},{2,10},{6,14},... | collective-permute-start | bytes 1179656 | tf_op jit(solution)/shard_map/ppermute | solution.py:94
  298.1 18.8 %collective-permute-start.58 = (bf16[256,768]{1,0:T(8,128)(2,1)S(1)}, bf16[256,768]{1,0:T(8,128)(2,1)S(1)}, u32[]{:S(2)}, u32[]{:S(2)}) collective-permute-start(bf16[256,768]{1,0:T(8,128)(2,1)S(1)} %get-tuple-element.549.refs_10_.refs_0_), channel_id=1, source_target_pairs={{0,12},{4,8},{8,4},{12,0},{1,13},{5,9},{9,5},{13,1},{2,14},{6,10},... | collective-permute-start | bytes 1179656 | tf_op jit(solution)/shard_map/ppermute | solution.py:94
  316.9 19.5 %collective-permute-start.61 = (bf16[192,384]{1,0:T(8,128)(2,1)S(1)}, bf16[192,384]{1,0:T(8,128)(2,1)S(1)}, u32[]{:S(2)}, u32[]{:S(2)}) collective-permute-start(bf16[192,384]{1,0:T(8,128)(2,1)S(1)} %get-tuple-element.561), channel_id=1, source_target_pairs={{0,1},{1,0},{2,3},{3,2},{4,5},{5,4},{6,7},{7,6},{8,9},{9,8},{10,11... | collective-permute-start | bytes 442376 | tf_op jit(solution)/shard_map/ppermute | solution.py:94
  338.9 19.7 %collective-permute-start.65 = (bf16[256,768]{1,0:T(8,128)(2,1)S(1)}, bf16[256,768]{1,0:T(8,128)(2,1)S(1)}, u32[]{:S(2)}, u32[]{:S(2)}) collective-permute-start(bf16[256,768]{1,0:T(8,128)(2,1)S(1)} %get-tuple-element.566), channel_id=1, source_target_pairs={{0,8},{4,12},{8,0},{12,4},{1,9},{5,13},{9,1},{13,5},{2,10},{6,14},... | collective-permute-start | bytes 1179656 | tf_op jit(solution)/shard_map/ppermute | solution.py:94
  373.1 19.8 %collective-permute-start.71 = (bf16[192,768]{1,0:T(8,128)(2,1)S(1)}, bf16[192,768]{1,0:T(8,128)(2,1)S(1)}, u32[]{:S(2)}, u32[]{:S(2)}) collective-permute-start(bf16[192,768]{1,0:T(8,128)(2,1)S(1)} %get-tuple-element.605), channel_id=1, source_target_pairs={{0,4},{4,0},{8,12},{12,8},{1,5},{5,1},{9,13},{13,9},{2,6},{6,2},{1... | collective-permute-start | bytes 884744 | tf_op jit(solution)/shard_map/ppermute | solution.py:94
  374.4 19.2 %collective-permute-start.72 = (bf16[192,768]{1,0:T(8,128)(2,1)S(1)}, bf16[192,768]{1,0:T(8,128)(2,1)S(1)}, u32[]{:S(2)}, u32[]{:S(2)}) collective-permute-start(bf16[192,768]{1,0:T(8,128)(2,1)S(1)} %get-tuple-element.606), channel_id=1, source_target_pairs={{0,8},{4,12},{8,0},{12,4},{1,9},{5,13},{9,1},{13,5},{2,10},{6,14},... | collective-permute-start | bytes 884744 | tf_op jit(solution)/shard_map/ppermute | solution.py:94
  375.4 18.9 %collective-permute-start.73 = (bf16[192,768]{1,0:T(8,128)(2,1)S(1)}, bf16[192,768]{1,0:T(8,128)(2,1)S(1)}, u32[]{:S(2)}, u32[]{:S(2)}) collective-permute-start(bf16[192,768]{1,0:T(8,128)(2,1)S(1)} %get-tuple-element.607), channel_id=1, source_target_pairs={{0,12},{4,8},{8,4},{12,0},{1,13},{5,9},{9,5},{13,1},{2,14},{6,10},... | collective-permute-start | bytes 884744 | tf_op jit(solution)/shard_map/ppermute | solution.py:94
  398.8 28.0 %collective-permute-start.83 = (bf16[4,192,768]{2,1,0:T(8,128)(2,1)}, bf16[4,192,768]{2,1,0:T(8,128)(2,1)S(1)}, u32[]{:S(2)}, u32[]{:S(2)}) collective-permute-start(bf16[4,192,768]{2,1,0:T(8,128)(2,1)} %reduce-scatter.3.cloned.1.call-done), channel_id=1, source_target_pairs={{0,16},{1,17},{2,18},{3,19},{4,20},{5,21},{6,22},{7,23},{8,24},{9,... | collective-permute-start | bytes 3538952 | tf_op jit(solution)/shard_map/ppermute | solution.py:1320
  433.0 27.9 %collective-permute-start.85 = (bf16[192,384]{1,0:T(8,128)(2,1)S(1)}, bf16[192,384]{1,0:T(8,128)(2,1)S(1)}, u32[]{:S(2)}, u32[]{:S(2)}) collective-permute-start(bf16[192,384]{1,0:T(8,128)(2,1)S(1)} %get-tuple-element.645), channel_id=1, source_target_pairs={{0,2},{1,3},{2,0},{3,1},{4,6},{5,7},{6,4},{7,5},{8,10},{9,11},{10,... | collective-permute-start | bytes 442376 | tf_op jit(solution)/shard_map/ppermute | solution.py:94
  438.0 22.8 %collective-permute-start.84 = (bf16[192,384]{1,0:T(8,128)(2,1)S(1)}, bf16[192,384]{1,0:T(8,128)(2,1)S(1)}, u32[]{:S(2)}, u32[]{:S(2)}) collective-permute-start(bf16[192,384]{1,0:T(8,128)(2,1)S(1)} %get-tuple-element.644), channel_id=1, source_target_pairs={{0,1},{1,0},{2,3},{3,2},{4,5},{5,4},{6,7},{7,6},{8,9},{9,8},{10,11... | collective-permute-start | bytes 442376 | tf_op jit(solution)/shard_map/ppermute | solution.py:94
  (183 other events, 2727.5 us)
Sparse Core Ops, SparseCore 0:
  241.4 91.5 reduce-scatter.2
  360.3 94.6 reduce-scatter.4

commit v4 on v3

--- a/solution.py
+++ b/solution.py
@@ -201,8 +201,7 @@
         scratch[...] = row_refs[layer][...].astype(F32)
         turned = jnp.broadcast_to(scratch[...], (128, SEQ)).T
         col_refs[layer][...] = turned[:, :1].astype(jnp.int32)
-        router_refs[layer][...] = jnp.zeros_like(router_refs[layer])
-        router_refs[layer][:EXPERTS, :] = jnp.where(
+        router_refs[layer][...] = jnp.where(
             own, own_router[...].astype(F32), other_router[...].astype(F32)
         ).astype(BF)
 
@@ -1144,7 +1143,7 @@
         pair(jnp.swapaxes(attention_in[0], 1, 2).reshape(3 * wide, D)),
         by_layer(*w_out_pair),
         pair(routes[0, :, :, 0]),
-        pair(router_weight[0].T),
+        pair(jnp.pad(router_weight[0].T, ((0, 128 - EXPERTS), (0, 0)))),
         up_weight[0],
         down_weight[0],
     )

time: 484 us -> 485 us (level)
    unnamed x245 -> x247, local copies, waits for them, and re-layouts: 23.3 us -> 23.2 us
  transfers between devices with their start and end apart: 94 -> 94, of which waited for: 41 -> 41; matrix products, arithmetic and copies ran while one was open for 2% -> 2% of each run, Pallas kernels for 36% -> 35%
where the time goes in v4:
time: 485 us; the launch traced here: 479 us
  Pallas kernels  175 us (36%)
  waiting for transfers between devices  158 us (33%)
  starting transfers between devices  98.1 us (20%)
  local copies, waits for them, and re-layouts  26 us (5%)
  between operations  16.4 us (3%)
  other arithmetic  6.44 us (1%)
    ppermute x90, waiting for transfers between devices, exchange(): return lax.ppermute(value, axis, [(i, i ^ mask) for i in range(count)])  158 us
    ppermute x90, starting transfers between devices, exchange(): return lax.ppermute(value, axis, [(i, i ^ mask) for i in range(count)])  95.4 us
    pallas_call x2, Pallas kernels, fwd_experts(): pl.pallas_call(functools.partial(fwd_experts_body, parts), grid_spec=pltp...  33 us
    pallas_call x2, Pallas kernels, bwd_attention(): pl.pallas_call(functools.partial(bwd_attention_body, parts), out_shape=[i...  30.9 us
    pallas_call x2, Pallas kernels, bwd_experts(): pl.pallas_call(functools.partial(bwd_experts_body, parts), grid_spec=pltp...  29.7 us
    pallas_call x2, Pallas kernels, fwd_attention(): pl.pallas_call(functools.partial(fwd_attention_body, parts, norm_inside),...  26.5 us
    unnamed x247, local copies, waits for them, and re-layouts  23.2 us
    pallas_call x2, Pallas kernels, expert_grads(): pl.pallas_call(expert_grads_body, grid=(HALF,), in_specs=[own, other, own...  14.6 us
  transfers between devices with their start and end apart: 94, of which 41 were waited for; matrix products, arithmetic and copies ran while one was open for 2% of the time, Pallas kernels for 35%

profile of v4, /device:TPU:0, one launch (start us, length us, event | category | flops | bytes accessed | tf_op | source)
XLA Modules:
  0.0 479.4 jit_solution(7008799255130664310)
XLA Ops:
  23.1 9.5 %collective-permute-done.1.refs_9_ = bf16[256,768]{1,0:T(8,128)(2,1)} collective-permute-done((bf16[256,768]{1,0:T(8,128)(2,1)S(1)}, bf16[256,768]{1,0:T(8,128)(2,1)}, u32[]{:S(2)}, u32[]{:S(2)}) %collective-permute-start.1) | collective-permute-done | bytes 393248 | tf_op jit(solution)/shard_map/ppermute | solution.py:94
  36.6 14.0 %fwd_attention.2 = (bf16[1024,768]{1,0:T(8,128)(2,1)}, bf16[3,3,1024,64]{3,2,1,0:T(8,128)(2,1)}, bf16[2,192,1024]{2,1,0:T(8,128)(2,1)}, f32[3,1,1024]{2,1,0:T(1,...) custom-call(s32[4]{0:T(128)S(1)} %add_add_fusion.2.place.refs_0_, ...), custom_call_target="tpu_custom_call" | custom-call | flops 8999999488 | bytes 10000000 | tf_op jit(solution)/shard_map/fwd_attention/pallas_call | solution.py:341
  68.9 4.9 %collective-permute-done.15.refs_10_ = bf16[256,768]{1,0:T(8,128)(2,1)} collective-permute-done((bf16[256,768]{1,0:T(8,128)(2,1)}, bf16[256,768]{1,0:T(8,128)(2,1)}, u32[]{:S(2)}, u32[]{:S(2)}) %collective-permute-start.15) | collective-permute-done | bytes 393248 | tf_op jit(solution)/shard_map/ppermute | solution.py:94
  73.8 6.6 %collective-permute-done.16.refs_11_ = bf16[256,768]{1,0:T(8,128)(2,1)} collective-permute-done((bf16[256,768]{1,0:T(8,128)(2,1)}, bf16[256,768]{1,0:T(8,128)(2,1)}, u32[]{:S(2)}, u32[]{:S(2)}) %collective-permute-start.16) | collective-permute-done | bytes 393248 | tf_op jit(solution)/shard_map/ppermute | solution.py:94
  84.0 16.9 %fwd_experts.2 = (bf16[4,2,320,768]{3,2,1,0:T(8,128)(2,1)}, f32[4,320,768]{2,1,0:T(8,128)}, f32[1024,1]{1,0:T(8,128)S(1)}, f32[256,128]{1,0:T(8,128)S(1)}, bf16[...) custom-call(s32[1]{0:T(128)} %bitcast.3.refs_0_, ...), custom_call_target="tpu_custom_call" | custom-call | flops 12000000000 | bytes 30000000 | tf_op jit(solution)/shard_map/fwd_experts/pallas_call | solution.py:632
  106.6 8.0 %collective-permute-done.23.refs_5_ = bf16[256,768]{1,0:T(8,128)(2,1)S(1)} collective-permute-done((bf16[256,768]{1,0:T(8,128)(2,1)S(1)}, bf16[256,768]{1,0:T(8,128)(2,1)S(1)}, u32[]{:S(2)}, u32[]{:S(2)}) %collective-permute-start.23) | collective-permute-done | bytes 393248 | tf_op jit(solution)/shard_map/ppermute | solution.py:94
  114.6 5.5 %collective-permute-done.24.refs_6_ = bf16[256,768]{1,0:T(8,128)(2,1)S(1)} collective-permute-done((bf16[256,768]{1,0:T(8,128)(2,1)S(1)}, bf16[256,768]{1,0:T(8,128)(2,1)S(1)}, u32[]{:S(2)}, u32[]{:S(2)}) %collective-permute-start.24) | collective-permute-done | bytes 393248 | tf_op jit(solution)/shard_map/ppermute | solution.py:94
  127.8 5.1 %collective-permute-done.26.refs_8_ = bf16[256,768]{1,0:T(8,128)(2,1)S(1)} collective-permute-done((bf16[256,768]{1,0:T(8,128)(2,1)S(1)}, bf16[256,768]{1,0:T(8,128)(2,1)S(1)}, u32[]{:S(2)}, u32[]{:S(2)}) %collective-permute-start.26) | collective-permute-done | bytes 393248 | tf_op jit(solution)/shard_map/ppermute | solution.py:94
  132.9 7.5 %collective-permute-done.27.refs_9_ = bf16[256,768]{1,0:T(8,128)(2,1)S(1)} collective-permute-done((bf16[256,768]{1,0:T(8,128)(2,1)S(1)}, bf16[256,768]{1,0:T(8,128)(2,1)S(1)}, u32[]{:S(2)}, u32[]{:S(2)}) %collective-permute-start.27) | collective-permute-done | bytes 393248 | tf_op jit(solution)/shard_map/ppermute | solution.py:94
  140.4 12.6 %fwd_attention.3 = (bf16[1024,768]{1,0:T(8,128)(2,1)}, bf16[3,3,1024,64]{3,2,1,0:T(8,128)(2,1)}, bf16[2,192,1024]{2,1,0:T(8,128)(2,1)}, f32[3,1,1024]{2,1,0:T(1,...) custom-call(s32[4]{0:T(128)S(1)} %add_add_fusion.3.place.refs_0_, ...), custom_call_target="tpu_custom_call" | custom-call | flops 8999999488 | bytes 10000000 | tf_op jit(solution)/shard_map/fwd_attention/pallas_call | solution.py:341
  158.8 5.5 %collective-permute-done.32.refs_5_.refs_2_ = bf16[192,256]{1,0:T(8,128)(2,1)S(1)} collective-permute-done((bf16[192,256]{1,0:T(8,128)(2,1)S(1)}, bf16[192,256]{1,0:T(8,128)(2,1)S(1)}, u32[]{:S(2)}, u32[]{:S(2)}) %collective-permute-start.32) | collective-permute-done | bytes 98336 | tf_op jit(solution)/shard_map/ppermute | solution.py:94
  169.3 6.5 %collective-permute-done.34.refs_10_ = bf16[256,768]{1,0:T(8,128)(2,1)S(1)} collective-permute-done((bf16[256,768]{1,0:T(8,128)(2,1)S(1)}, bf16[256,768]{1,0:T(8,128)(2,1)S(1)}, u32[]{:S(2)}, u32[]{:S(2)}) %collective-permute-start.34) | collective-permute-done | bytes 393248 | tf_op jit(solution)/shard_map/ppermute | solution.py:94
  175.8 4.4 collective-permute-done.35.refs_11_
  181.8 16.1 %fwd_experts.3 = (bf16[4,2,320,768]{3,2,1,0:T(8,128)(2,1)}, f32[4,320,768]{2,1,0:T(8,128)}, f32[1024,1]{1,0:T(8,128)S(1)}, f32[256,128]{1,0:T(8,128)S(1)}, bf16[...) custom-call(s32[1]{0:T(128)} %bitcast.17.refs_0_, ...), custom_call_target="tpu_custom_call" | custom-call | flops 12000000000 | bytes 30000000 | tf_op jit(solution)/shard_map/fwd_experts/pallas_call | solution.py:632
  202.1 14.9 %bwd_experts.2 = (bf16[4,2,320,768]{3,2,1,0:T(8,128)(2,1)}, bf16[256,768]{1,0:T(8,128)(2,1)S(1)}, bf16[256,768]{1,0:T(8,128)(2,1)S(1)}, bf16[256,768]{1,0:T(8,128)(2,1)S(1)}, bf16[256,768]{1,0:T(8,128)(2,1)S(1)}) custom-call(s32[1]{0:T(128)} %bitcast.17.refs_0_, s32[4]{0:T(128)S(1)} %broadcast_select_fusion.4.refs_1_, ...), custom_call_target="tpu_custom_call" | custom-call | flops 12000000000 | bytes 30000000 | tf_op jit(solution)/shard_map/bwd_experts/pallas_call | solution.py:710
  226.8 7.3 %expert_grads.2 = bf16[2,2,768,768]{3,2,1,0:T(8,128)(2,1)} custom-call(bf16[4,2,320,768]{3,2,1,0:T(8,128)(2,1)} %get-tuple-element.472.fwd_own, bf16[4,2,320,768]{3,2,1,0:T(8,128)(2,1)} %copy-done.107, bf16[4,2,320,768]{3,2,1,0:T(8,128)(2,1)} %get-tuple-element.483.bwd_own, bf16[4,2,320,768]{3,2,1,0:T(8,128)(2,1)S(1)} %collective-permute-done.46.bwd_other), custom_call_target="tpu_custom_call" | custom-call | flops 1000000 | bytes 100000 | tf_op jit(solution)/shard_map/expert_grads/pallas_call | solution.py:916
  234.1 5.9 %collective-permute-done.44.refs_10_ = bf16[256,768]{1,0:T(8,128)(2,1)S(1)} collective-permute-done((bf16[256,768]{1,0:T(8,128)(2,1)S(1)}, bf16[256,768]{1,0:T(8,128)(2,1)S(1)}, u32[]{:S(2)}, u32[]{:S(2)}) %collective-permute-start.44) | collective-permute-done | bytes 393248 | tf_op jit(solution)/shard_map/ppermute | solution.py:94
  241.8 4.3 middle_back.2
  260.6 15.5 %bwd_attention.2 = (bf16[1024,576]{1,0:T(8,128)(2,1)}, f32[18,128,128]{2,1,0:T(8,128)}, f32[3,8,256]{2,1,0:T(8,128)S(1)}, f32[1,768]{1,0:T(1,128)S(1)}, bf16[256...) custom-call(s32[4]{0:T(128)S(1)} %add_add_fusion.3.place.refs_0_, ...), custom_call_target="tpu_custom_call" | custom-call | flops 17999998976 | bytes 10000000 | tf_op jit(solution)/shard_map/bwd_attention/pallas_call | solution.py:452
  288.4 6.9 %collective-permute-done.54.refs_5_ = bf16[256,768]{1,0:T(8,128)(2,1)S(1)} collective-permute-done((bf16[256,768]{1,0:T(8,128)(2,1)}, bf16[256,768]{1,0:T(8,128)(2,1)S(1)}, u32[]{:S(2)}, u32[]{:S(2)}) %collective-permute-start.54) | collective-permute-done | bytes 393248 | tf_op jit(solution)/shard_map/ppermute | solution.py:94
  300.9 7.7 %collective-permute-done.56.refs_11_ = bf16[256,768]{1,0:T(8,128)(2,1)S(1)} collective-permute-done((bf16[256,768]{1,0:T(8,128)(2,1)S(1)}, bf16[256,768]{1,0:T(8,128)(2,1)S(1)}, u32[]{:S(2)}, u32[]{:S(2)}) %collective-permute-start.56) | collective-permute-done | bytes 393248 | tf_op jit(solution)/shard_map/ppermute | solution.py:94
  308.6 7.7 %collective-permute-done.57.refs_12_ = bf16[256,768]{1,0:T(8,128)(2,1)S(1)} collective-permute-done((bf16[256,768]{1,0:T(8,128)(2,1)S(1)}, bf16[256,768]{1,0:T(8,128)(2,1)S(1)}, u32[]{:S(2)}, u32[]{:S(2)}) %collective-permute-start.57) | collective-permute-done | bytes 393248 | tf_op jit(solution)/shard_map/ppermute | solution.py:94
  322.3 14.8 %bwd_experts.3 = (bf16[4,2,320,768]{3,2,1,0:T(8,128)(2,1)}, bf16[256,768]{1,0:T(8,128)(2,1)S(1)}, bf16[256,768]{1,0:T(8,128)(2,1)S(1)}, bf16[256,768]{1,0:T(8,128)(2,1)S(1)}, bf16[256,768]{1,0:T(8,128)(2,1)S(1)}) custom-call(s32[1]{0:T(128)} %bitcast.3.refs_0_, s32[4]{0:T(128)S(1)} %copy-done.93, s32[1,1024]{1,0:T(1,128)S(1)} %copy-done.88, ...), custom_call_target="tpu_custom_call" | custom-call | flops 12000000000 | bytes 30000000 | tf_op jit(solution)/shard_map/bwd_experts/pallas_call | solution.py:710
  341.3 3.5 collective-permute-done.67.bwd_other
  344.8 7.3 %expert_grads.3 = bf16[2,2,768,768]{3,2,1,0:T(8,128)(2,1)} custom-call(bf16[4,2,320,768]{3,2,1,0:T(8,128)(2,1)} %get-tuple-element.559.fwd_own, bf16[4,2,320,768]{3,2,1,0:T(8,128)(2,1)} %copy-done.106, bf16[4,2,320,768]{3,2,1,0:T(8,128)(2,1)} %get-tuple-element.569.bwd_own, bf16[4,2,320,768]{3,2,1,0:T(8,128)(2,1)S(1)} %collective-permute-done.67.bwd_other), custom_call_target="tpu_custom_call" | custom-call | flops 1000000 | bytes 100000 | tf_op jit(solution)/shard_map/expert_grads/pallas_call | solution.py:916
  352.2 6.8 %collective-permute-done.65.refs_10_ = bf16[256,768]{1,0:T(8,128)(2,1)S(1)} collective-permute-done((bf16[256,768]{1,0:T(8,128)(2,1)S(1)}, bf16[256,768]{1,0:T(8,128)(2,1)S(1)}, u32[]{:S(2)}, u32[]{:S(2)}) %collective-permute-start.65) | collective-permute-done | bytes 393248 | tf_op jit(solution)/shard_map/ppermute | solution.py:94
  360.6 4.2 middle_back.3
  377.0 15.4 %bwd_attention.3 = (bf16[1024,576]{1,0:T(8,128)(2,1)}, f32[18,128,128]{2,1,0:T(8,128)}, f32[3,8,256]{2,1,0:T(8,128)S(1)}, f32[1,768]{1,0:T(1,128)S(1)}, bf16[256...) custom-call(s32[4]{0:T(128)S(1)} %add_add_fusion.2.place.refs_0_, ...), custom_call_target="tpu_custom_call" | custom-call | flops 17999998976 | bytes 10000000 | tf_op jit(solution)/shard_map/bwd_attention/pallas_call | solution.py:452
  403.5 3.4 attention_grads.3
  437.8 5.0 %collective-permute-done.87 = f32[16,768]{1,0:T(8,128)S(1)} collective-permute-done((f32[16,768]{1,0:T(8,128)S(1)}, f32[16,768]{1,0:T(8,128)S(1)}, u32[]{:S(2)}, u32[]{:S(2)}) %collective-permute-start.87) | collective-permute-done | bytes 49184 | tf_op jit(solution)/shard_map/ppermute | solution.py:94
  445.8 15.9 %collective-permute-done.85 = bf16[192,384]{1,0:T(8,128)(2,1)S(1)} collective-permute-done((bf16[192,384]{1,0:T(8,128)(2,1)S(1)}, bf16[192,384]{1,0:T(8,128)(2,1)S(1)}, u32[]{:S(2)}, u32[]{:S(2)}) %collective-permute-start.85) | collective-permute-done | bytes 147488 | tf_op jit(solution)/shard_map/ppermute | solution.py:94
  468.7 3.7 expert_results.1
  (469 shorter events, 189.8 us)
Async XLA Ops:
  7.2 391.1 %reduce-scatter.3.cloned.1.call-start = ((), (), s32[]{:S(2)}) async-start(), calls=%async_computation.2 | async-start | bytes 5898240 | tf_op jit(solution)/shard_map/reduce_scatter | solution.py:1071
  7.3 25.3 %collective-permute-start.5 = (bf16[576,768]{1,0:T(8,128)(2,1)}, bf16[576,768]{1,0:T(8,128)(2,1)S(1)}, u32[]{:S(2)}, u32[]{:S(2)}) collective-permute-start(bf16[576,768]{1,0:T(8,128)(2,1)} %bitcast.82), channel_id=1, source_target_pairs={{0,16},{16,0},{1,17},{17,1},{2,18},{18,2},{3,19},{19,3},{4,20},{20... | collective-permute-start | bytes 2654216 | tf_op jit(solution)/shard_map/ppermute | solution.py:94
  13.1 19.4 %collective-permute-start.1 = (bf16[256,768]{1,0:T(8,128)(2,1)S(1)}, bf16[256,768]{1,0:T(8,128)(2,1)}, u32[]{:S(2)}, u32[]{:S(2)}) collective-permute-start(bf16[256,768]{1,0:T(8,128)(2,1)S(1)} %dynamic-slice_bitcast_fusion.1.refs_7_.refs_0_.refs_1_), channel_id=1, source_target_pairs={{0,8},{4,12},{8,0},{12,4},{1,9},{5,13},{9,1},{13,5},{2,10},{6,14},... | collective-permute-start | bytes 1179656 | tf_op jit(solution)/shard_map/ppermute | solution.py:94
  32.6 47.8 %collective-permute-start.18 = (bf16[4,768,768]{2,1,0:T(8,128)(2,1)}, bf16[4,768,768]{2,1,0:T(8,128)(2,1)}, u32[]{:S(2)}, u32[]{:S(2)}) collective-permute-start(bf16[4,768,768]{2,1,0:T(8,128)(2,1)} %bitcast.97), channel_id=1, source_target_pairs={{0,16},{16,0},{1,17},{17,1},{2,18},{18,2},{3,19},{19,3},{4,20},{20... | collective-permute-start | bytes 14155784 | tf_op jit(solution)/shard_map/ppermute | solution.py:94
  32.6 47.7 %collective-permute-start.19 = (bf16[4,768,768]{2,1,0:T(8,128)(2,1)}, bf16[4,768,768]{2,1,0:T(8,128)(2,1)}, u32[]{:S(2)}, u32[]{:S(2)}) collective-permute-start(bf16[4,768,768]{2,1,0:T(8,128)(2,1)} %bitcast.102), channel_id=1, source_target_pairs={{0,16},{16,0},{1,17},{17,1},{2,18},{18,2},{3,19},{19,3},{4,20},{20... | collective-permute-start | bytes 14155784 | tf_op jit(solution)/shard_map/ppermute | solution.py:94
  33.1 18.9 %collective-permute-start.9 = (bf16[192,768]{1,0:T(8,128)(2,1)S(1)}, bf16[192,768]{1,0:T(8,128)(2,1)S(1)}, u32[]{:S(2)}, u32[]{:S(2)}) collective-permute-start(bf16[192,768]{1,0:T(8,128)(2,1)S(1)} %get-tuple-element.361.refs_7_.refs_12_), channel_id=1, source_target_pairs={{0,4},{4,0},{8,12},{12,8},{1,5},{5,1},{9,13},{13,9},{2,6},{6,2},{1... | collective-permute-start | bytes 884744 | tf_op jit(solution)/shard_map/ppermute | solution.py:94
  80.4 22.6 %collective-permute-start.20 = (bf16[192,768]{1,0:T(8,128)(2,1)S(1)}, bf16[192,768]{1,0:T(8,128)(2,1)S(1)}, u32[]{:S(2)}, u32[]{:S(2)}) collective-permute-start(bf16[192,768]{1,0:T(8,128)(2,1)S(1)} %get-tuple-element.432.refs_7_.refs_12_), channel_id=1, source_target_pairs={{0,4},{4,0},{8,12},{12,8},{1,5},{5,1},{9,13},{13,9},{2,6},{6,2},{1... | collective-permute-start | bytes 884744 | tf_op jit(solution)/shard_map/ppermute | solution.py:94
  81.3 21.7 %collective-permute-start.21 = (bf16[192,768]{1,0:T(8,128)(2,1)S(1)}, bf16[192,768]{1,0:T(8,128)(2,1)S(1)}, u32[]{:S(2)}, u32[]{:S(2)}) collective-permute-start(bf16[192,768]{1,0:T(8,128)(2,1)S(1)} %get-tuple-element.432.refs_7_.refs_12_), channel_id=1, source_target_pairs={{0,8},{4,12},{8,0},{12,4},{1,9},{5,13},{9,1},{13,5},{2,10},{6,14},... | collective-permute-start | bytes 884744 | tf_op jit(solution)/shard_map/ppermute | solution.py:94
  82.5 20.5 %collective-permute-start.22 = (bf16[192,768]{1,0:T(8,128)(2,1)S(1)}, bf16[192,768]{1,0:T(8,128)(2,1)S(1)}, u32[]{:S(2)}, u32[]{:S(2)}) collective-permute-start(bf16[192,768]{1,0:T(8,128)(2,1)S(1)} %get-tuple-element.432.refs_7_.refs_12_), channel_id=1, source_target_pairs={{0,12},{4,8},{8,4},{12,0},{1,13},{5,9},{9,5},{13,1},{2,14},{6,10},... | collective-permute-start | bytes 884744 | tf_op jit(solution)/shard_map/ppermute | solution.py:94
  121.7 18.6 %collective-permute-start.27 = (bf16[256,768]{1,0:T(8,128)(2,1)S(1)}, bf16[256,768]{1,0:T(8,128)(2,1)S(1)}, u32[]{:S(2)}, u32[]{:S(2)}) collective-permute-start(bf16[256,768]{1,0:T(8,128)(2,1)S(1)} %get-tuple-element.423.refs_7_), channel_id=1, source_target_pairs={{0,8},{4,12},{8,0},{12,4},{1,9},{5,13},{9,1},{13,5},{2,10},{6,14},... | collective-permute-start | bytes 1179656 | tf_op jit(solution)/shard_map/ppermute | solution.py:94
  124.4 28.6 %collective-permute-start.29 = (bf16[256,768]{1,0:T(8,128)(2,1)S(1)}, bf16[256,768]{1,0:T(8,128)(2,1)S(1)}, u32[]{:S(2)}, u32[]{:S(2)}) collective-permute-start(bf16[256,768]{1,0:T(8,128)(2,1)S(1)} %dynamic-slice_bitcast_fusion.refs_10_.refs_0_), channel_id=1, source_target_pairs={{0,4},{4,0},{8,12},{12,8},{1,5},{5,1},{9,13},{13,9},{2,6},{6,2},{1... | collective-permute-start | bytes 1179656 | tf_op jit(solution)/shard_map/ppermute | solution.py:94
  125.8 27.2 %collective-permute-start.30 = (bf16[256,768]{1,0:T(8,128)(2,1)S(1)}, bf16[256,768]{1,0:T(8,128)(2,1)S(1)}, u32[]{:S(2)}, u32[]{:S(2)}) collective-permute-start(bf16[256,768]{1,0:T(8,128)(2,1)S(1)} %dynamic-slice_bitcast_fusion.refs_10_.refs_0_), channel_id=1, source_target_pairs={{0,8},{4,12},{8,0},{12,4},{1,9},{5,13},{9,1},{13,5},{2,10},{6,14},... | collective-permute-start | bytes 1179656 | tf_op jit(solution)/shard_map/ppermute | solution.py:94
  180.2 18.3 %collective-permute-start.37 = (bf16[256,768]{1,0:T(8,128)(2,1)S(1)}, bf16[256,768]{1,0:T(8,128)(2,1)S(1)}, u32[]{:S(2)}, u32[]{:S(2)}) collective-permute-start(bf16[256,768]{1,0:T(8,128)(2,1)S(1)} %dynamic-slice_bitcast_fusion.refs_10_.refs_0_), channel_id=1, source_target_pairs={{0,12},{4,8},{8,4},{12,0},{1,13},{5,9},{9,5},{13,1},{2,14},{6,10},... | collective-permute-start | bytes 1179656 | tf_op jit(solution)/shard_map/ppermute | solution.py:94
  198.5 21.3 %collective-permute-start.41 = (bf16[4,2,320,768]{3,2,1,0:T(8,128)(2,1)}, bf16[4,2,320,768]{3,2,1,0:T(8,128)(2,1)S(1)}, u32[]{:S(2)}, u32[]{:S(2)}) collective-permute-start(bf16[4,2,320,768]{3,2,1,0:T(8,128)(2,1)} %get-tuple-element.472.fwd_own), channel_id=1, source_target_pairs={{0,16},{16,0},{1,17},{17,1},{2,18},{18,2},{3,19},{19,3},{4,20},{20... | collective-permute-start | bytes 11796488 | tf_op jit(solution)/shard_map/ppermute | solution.py:94
  198.5 19.7 %collective-permute-start.38 = (bf16[256,768]{1,0:T(8,128)(2,1)S(1)}, bf16[256,768]{1,0:T(8,128)(2,1)S(1)}, u32[]{:S(2)}, u32[]{:S(2)}) collective-permute-start(bf16[256,768]{1,0:T(8,128)(2,1)S(1)} %get-tuple-element.469), channel_id=1, source_target_pairs={{0,4},{4,0},{8,12},{12,8},{1,5},{5,1},{9,13},{13,9},{2,6},{6,2},{1... | collective-permute-start | bytes 1179656 | tf_op jit(solution)/shard_map/ppermute | solution.py:94
  200.5 19.3 %collective-permute-start.40 = (bf16[256,768]{1,0:T(8,128)(2,1)S(1)}, bf16[256,768]{1,0:T(8,128)(2,1)S(1)}, u32[]{:S(2)}, u32[]{:S(2)}) collective-permute-start(bf16[256,768]{1,0:T(8,128)(2,1)S(1)} %get-tuple-element.471), channel_id=1, source_target_pairs={{0,12},{4,8},{8,4},{12,0},{1,13},{5,9},{9,5},{13,1},{2,14},{6,10},... | collective-permute-start | bytes 1179656 | tf_op jit(solution)/shard_map/ppermute | solution.py:94
  220.4 19.6 %collective-permute-start.44 = (bf16[256,768]{1,0:T(8,128)(2,1)S(1)}, bf16[256,768]{1,0:T(8,128)(2,1)S(1)}, u32[]{:S(2)}, u32[]{:S(2)}) collective-permute-start(bf16[256,768]{1,0:T(8,128)(2,1)S(1)} %get-tuple-element.480), channel_id=1, source_target_pairs={{0,8},{4,12},{8,0},{12,4},{1,9},{5,13},{9,1},{13,5},{2,10},{6,14},... | collective-permute-start | bytes 1179656 | tf_op jit(solution)/shard_map/ppermute | solution.py:94
  241.6 220.1 %reduce-scatter.5.cloned.1.call-start = ((), (), s32[]{:S(2)}) async-start(), calls=%async_computation.3 | async-start | bytes 5898240 | tf_op jit(solution)/shard_map/reduce_scatter | solution.py:1071
  241.7 95.4 %collective-permute-start.60 = (bf16[4,2,320,768]{3,2,1,0:T(8,128)(2,1)}, bf16[4,2,320,768]{3,2,1,0:T(8,128)(2,1)S(1)}, u32[]{:S(2)}, u32[]{:S(2)}) collective-permute-start(bf16[4,2,320,768]{3,2,1,0:T(8,128)(2,1)} %get-tuple-element.559.fwd_own), channel_id=1, source_target_pairs={{0,16},{16,0},{1,17},{17,1},{2,18},{18,2},{3,19},{19,3},{4,20},{20... | collective-permute-start | bytes 11796488 | tf_op jit(solution)/shard_map/ppermute | solution.py:94
  255.9 20.2 %collective-permute-start.50 = (bf16[192,768]{1,0:T(8,128)(2,1)S(1)}, bf16[192,768]{1,0:T(8,128)(2,1)S(1)}, u32[]{:S(2)}, u32[]{:S(2)}) collective-permute-start(bf16[192,768]{1,0:T(8,128)(2,1)S(1)} %get-tuple-element.517), channel_id=1, source_target_pairs={{0,4},{4,0},{8,12},{12,8},{1,5},{5,1},{9,13},{13,9},{2,6},{6,2},{1... | collective-permute-start | bytes 884744 | tf_op jit(solution)/shard_map/ppermute | solution.py:94
  256.8 19.3 %collective-permute-start.51 = (bf16[192,768]{1,0:T(8,128)(2,1)S(1)}, bf16[192,768]{1,0:T(8,128)(2,1)S(1)}, u32[]{:S(2)}, u32[]{:S(2)}) collective-permute-start(bf16[192,768]{1,0:T(8,128)(2,1)S(1)} %get-tuple-element.518), channel_id=1, source_target_pairs={{0,8},{4,12},{8,0},{12,4},{1,9},{5,13},{9,1},{13,5},{2,10},{6,14},... | collective-permute-start | bytes 884744 | tf_op jit(solution)/shard_map/ppermute | solution.py:94
  277.0 18.3 %collective-permute-start.54 = (bf16[256,768]{1,0:T(8,128)(2,1)}, bf16[256,768]{1,0:T(8,128)(2,1)S(1)}, u32[]{:S(2)}, u32[]{:S(2)}) collective-permute-start(bf16[256,768]{1,0:T(8,128)(2,1)} %get-tuple-element.522), channel_id=1, source_target_pairs={{0,8},{4,12},{8,0},{12,4},{1,9},{5,13},{9,1},{13,5},{2,10},{6,14},... | collective-permute-start | bytes 1179656 | tf_op jit(solution)/shard_map/ppermute | solution.py:94
  298.2 18.1 %collective-permute-start.57 = (bf16[256,768]{1,0:T(8,128)(2,1)S(1)}, bf16[256,768]{1,0:T(8,128)(2,1)S(1)}, u32[]{:S(2)}, u32[]{:S(2)}) collective-permute-start(bf16[256,768]{1,0:T(8,128)(2,1)S(1)} %get-tuple-element.549.refs_10_.refs_0_), channel_id=1, source_target_pairs={{0,8},{4,12},{8,0},{12,4},{1,9},{5,13},{9,1},{13,5},{2,10},{6,14},... | collective-permute-start | bytes 1179656 | tf_op jit(solution)/shard_map/ppermute | solution.py:94
  299.2 18.7 %collective-permute-start.58 = (bf16[256,768]{1,0:T(8,128)(2,1)S(1)}, bf16[256,768]{1,0:T(8,128)(2,1)S(1)}, u32[]{:S(2)}, u32[]{:S(2)}) collective-permute-start(bf16[256,768]{1,0:T(8,128)(2,1)S(1)} %get-tuple-element.549.refs_10_.refs_0_), channel_id=1, source_target_pairs={{0,12},{4,8},{8,4},{12,0},{1,13},{5,9},{9,5},{13,1},{2,14},{6,10},... | collective-permute-start | bytes 1179656 | tf_op jit(solution)/shard_map/ppermute | solution.py:94
  317.9 19.3 %collective-permute-start.61 = (bf16[192,384]{1,0:T(8,128)(2,1)S(1)}, bf16[192,384]{1,0:T(8,128)(2,1)S(1)}, u32[]{:S(2)}, u32[]{:S(2)}) collective-permute-start(bf16[192,384]{1,0:T(8,128)(2,1)S(1)} %get-tuple-element.561), channel_id=1, source_target_pairs={{0,1},{1,0},{2,3},{3,2},{4,5},{5,4},{6,7},{7,6},{8,9},{9,8},{10,11... | collective-permute-start | bytes 442376 | tf_op jit(solution)/shard_map/ppermute | solution.py:94
  339.3 19.7 %collective-permute-start.65 = (bf16[256,768]{1,0:T(8,128)(2,1)S(1)}, bf16[256,768]{1,0:T(8,128)(2,1)S(1)}, u32[]{:S(2)}, u32[]{:S(2)}) collective-permute-start(bf16[256,768]{1,0:T(8,128)(2,1)S(1)} %get-tuple-element.566), channel_id=1, source_target_pairs={{0,8},{4,12},{8,0},{12,4},{1,9},{5,13},{9,1},{13,5},{2,10},{6,14},... | collective-permute-start | bytes 1179656 | tf_op jit(solution)/shard_map/ppermute | solution.py:94
  340.8 18.2 %collective-permute-start.66 = (bf16[256,768]{1,0:T(8,128)(2,1)S(1)}, bf16[256,768]{1,0:T(8,128)(2,1)S(1)}, u32[]{:S(2)}, u32[]{:S(2)}) collective-permute-start(bf16[256,768]{1,0:T(8,128)(2,1)S(1)} %get-tuple-element.567), channel_id=1, source_target_pairs={{0,12},{4,8},{8,4},{12,0},{1,13},{5,9},{9,5},{13,1},{2,14},{6,10},... | collective-permute-start | bytes 1179656 | tf_op jit(solution)/shard_map/ppermute | solution.py:94
  373.5 19.0 %collective-permute-start.71 = (bf16[192,768]{1,0:T(8,128)(2,1)S(1)}, bf16[192,768]{1,0:T(8,128)(2,1)S(1)}, u32[]{:S(2)}, u32[]{:S(2)}) collective-permute-start(bf16[192,768]{1,0:T(8,128)(2,1)S(1)} %get-tuple-element.605), channel_id=1, source_target_pairs={{0,4},{4,0},{8,12},{12,8},{1,5},{5,1},{9,13},{13,9},{2,6},{6,2},{1... | collective-permute-start | bytes 884744 | tf_op jit(solution)/shard_map/ppermute | solution.py:94
  374.7 18.4 %collective-permute-start.72 = (bf16[192,768]{1,0:T(8,128)(2,1)S(1)}, bf16[192,768]{1,0:T(8,128)(2,1)S(1)}, u32[]{:S(2)}, u32[]{:S(2)}) collective-permute-start(bf16[192,768]{1,0:T(8,128)(2,1)S(1)} %get-tuple-element.606), channel_id=1, source_target_pairs={{0,8},{4,12},{8,0},{12,4},{1,9},{5,13},{9,1},{13,5},{2,10},{6,14},... | collective-permute-start | bytes 884744 | tf_op jit(solution)/shard_map/ppermute | solution.py:94
  398.3 28.0 %collective-permute-start.83 = (bf16[4,192,768]{2,1,0:T(8,128)(2,1)}, bf16[4,192,768]{2,1,0:T(8,128)(2,1)S(1)}, u32[]{:S(2)}, u32[]{:S(2)}) collective-permute-start(bf16[4,192,768]{2,1,0:T(8,128)(2,1)} %reduce-scatter.3.cloned.1.call-done), channel_id=1, source_target_pairs={{0,16},{1,17},{2,18},{3,19},{4,20},{5,21},{6,22},{7,23},{8,24},{9,... | collective-permute-start | bytes 3538952 | tf_op jit(solution)/shard_map/ppermute | solution.py:1319
  432.5 29.1 %collective-permute-start.85 = (bf16[192,384]{1,0:T(8,128)(2,1)S(1)}, bf16[192,384]{1,0:T(8,128)(2,1)S(1)}, u32[]{:S(2)}, u32[]{:S(2)}) collective-permute-start(bf16[192,384]{1,0:T(8,128)(2,1)S(1)} %get-tuple-element.645), channel_id=1, source_target_pairs={{0,2},{1,3},{2,0},{3,1},{4,6},{5,7},{6,4},{7,5},{8,10},{9,11},{10,... | collective-permute-start | bytes 442376 | tf_op jit(solution)/shard_map/ppermute | solution.py:94
  436.9 24.8 %collective-permute-start.84 = (bf16[192,384]{1,0:T(8,128)(2,1)S(1)}, bf16[192,384]{1,0:T(8,128)(2,1)S(1)}, u32[]{:S(2)}, u32[]{:S(2)}) collective-permute-start(bf16[192,384]{1,0:T(8,128)(2,1)S(1)} %get-tuple-element.644), channel_id=1, source_target_pairs={{0,1},{1,0},{2,3},{3,2},{4,5},{5,4},{6,7},{7,6},{8,9},{9,8},{10,11... | collective-permute-start | bytes 442376 | tf_op jit(solution)/shard_map/ppermute | solution.py:94
  (184 other events, 2797.2 us)
Sparse Core Ops, SparseCore 0:
  241.7 91.0 reduce-scatter.2
  360.6 96.0 reduce-scatter.4
